TPU v7x, 128 devices: a whole 4x4x4 slice. The times are simulated.
128 devices in a mesh: seq: 2 (over x_hi), exp: 64 (over y, z, x_lo, core).
Axes of the slice: x: 4 (x_hi: 2, x_lo: 2; x = x_hi * 2 + x_lo), y: 4, z: 4, core: 2. Of those that a mesh axis runs over, the one named last changes fastest.
Arguments:
- tokens: bfloat16 [64, 256, 1280], P('exp', 'seq'), may hold values from -6 to 6
- cotangent: bfloat16 [64, 256, 1280], P('exp', 'seq'), may hold values from -6 to 6
- segments: int32 [64, 256], P('exp'), may hold values from 0 to 4, as said below
- routes: int32 [64, 256, 7], P('exp', 'seq'), may hold values from 0 to 63, all different within a row; in each aligned block of 128 rows (0 to 127, 128 to 255, ..., all dimensions but the last counted through in order) at most 17 rows name the same one
- norm_gain_attn: bfloat16 [1280], P('exp'), may hold values from 0.5 to 1.5
- w_query: bfloat16 [1280, 1280], P('exp'), may hold values from -0.25 to 0.25
- w_key: bfloat16 [1280, 1280], P('exp'), may hold values from -0.25 to 0.25
- w_value: bfloat16 [1280, 1280], P('exp'), may hold values from -0.15625 to 0.15625
- w_out: bfloat16 [1280, 1280], P('exp'), may hold values from -0.5 to 0.5
- norm_gain_ffn: bfloat16 [1280], P('exp'), may hold values from 0.5 to 1.5
- w_router: bfloat16 [1280, 64], P('exp'), may hold values from -0.078125 to 0.078125
- shared_gate: bfloat16 [1280, 896], P('exp'), may hold values from -0.15625 to 0.15625
- shared_up: bfloat16 [1280, 896], P('exp'), may hold values from -0.15625 to 0.15625
- shared_down: bfloat16 [896, 1280], P('exp'), may hold values from -0.1875 to 0.1875
- expert_gate: bfloat16 [64, 1280, 896], P('exp'), may hold values from -0.15625 to 0.15625
- expert_up: bfloat16 [64, 1280, 896], P('exp'), may hold values from -0.15625 to 0.15625
- expert_down: bfloat16 [64, 896, 1280], P('exp'), may hold values from -0.1875 to 0.1875
Outputs:
- layer_out: bfloat16 [64, 256, 1280], P('exp', 'seq')
- grad_tokens: float32 [64, 256, 1280], P('exp', 'seq')
- grad_norm_attn: float32 [1280], P('exp')
- grad_w_query: float32 [1280, 1280], P('exp')
- grad_w_key: float32 [1280, 1280], P('exp')
- grad_w_value: float32 [1280, 1280], P('exp')
- grad_w_out: float32 [1280, 1280], P('exp')
- grad_norm_ffn: float32 [1280], P('exp')
- grad_router: float32 [1280, 64], P('exp')
- grad_shared_gate: float32 [1280, 896], P('exp')
- grad_shared_up: float32 [1280, 896], P('exp')
- grad_shared_down: float32 [896, 1280], P('exp')
- grad_expert_gate: float32 [64, 1280, 896], P('exp')
- grad_expert_up: float32 [64, 1280, 896], P('exp')
- grad_expert_down: float32 [64, 896, 1280], P('exp')
Inputs may be any that keep to these rules, and one draw needn't show every extreme that they name: `routes`: each row names 7 different experts. Within the rows of one device (aligned blocks of 128 rows, in the order of sequences and then positions) no expert is named more than 17 times. `segments`: along each sequence the numbers start at 0 and rise by one at the start of each document, so every sequence holds 5 documents.
All inputs are finite; a program needn't handle non-finite values.
Results may differ from a plain program's by a relative error of at most 0.015.
The roundings to bfloat16 on the way count: a program that leaves them out, or rounds other values in their place, can miss the bound.
Values may be sent and summed in bfloat16 or wider, within the bound.
A program may use at most 192 MiB of HBM per device.

v0:
```python
import jax
import jax.numpy as jnp
from jax import lax
from jax.sharding import PartitionSpec as P

HEADS = 10


EPSILON = 1e-06
NEG_BIG = -1e30


def passed_along(x, axis, by):
    devices = lax.axis_size(axis)
    pairs = [(i, i + by) for i in range(devices) if 0 <= i + by < devices]
    return lax.ppermute(x, axis, pairs)


def rms_forward(values, gain_vec):
    inv_rms = lax.rsqrt(jnp.mean(values * values, axis=-1, keepdims=True) + EPSILON)
    return (values * inv_rms * gain_vec, inv_rms)


def rms_backward(values, inv_rms, gain_vec, upstream):
    weighted = upstream * gain_vec
    inner = jnp.mean(weighted * values, axis=-1, keepdims=True)
    grad_in = inv_rms * weighted - values * (inv_rms * inv_rms * inv_rms) * inner
    grad_gain = jnp.sum(upstream * values * inv_rms, axis=0)
    return (grad_in, grad_gain)


def rotary_tables(positions, head_width):
    half_width = head_width // 2
    freq = jnp.power(10000.0, -2.0 * jnp.arange(half_width, dtype=jnp.float32) / head_width)
    angles = positions.astype(jnp.float32)[:, None] * freq[None, :]
    return (jnp.cos(angles)[:, None, :], jnp.sin(angles)[:, None, :])


def rotate(values, cosine, sine):
    half_width = values.shape[-1] // 2
    first = values[..., :half_width]
    second = values[..., half_width:]
    return jnp.concatenate(
        [first * cosine - second * sine, second * cosine + first * sine], axis=-1
    )


def unrotate(values, cosine, sine):
    half_width = values.shape[-1] // 2
    first = values[..., :half_width]
    second = values[..., half_width:]
    return jnp.concatenate(
        [first * cosine + second * sine, second * cosine - first * sine], axis=-1
    )


def silu_parts(pre_act):
    sigma = jax.nn.sigmoid(pre_act)
    return (pre_act * sigma, sigma * (1.0 + pre_act * (1.0 - sigma)))


def score_block(queries, keys_all, allowed, inv_root):
    scores = (
        jnp.einsum("thd,shd->hts", queries, keys_all, preferred_element_type=jnp.float32) * inv_root
    )
    return jnp.where(allowed[None], scores, NEG_BIG)


def per_device(
    tokens,
    cotangent,
    segments,
    routes,
    norm_gain_attn,
    w_query,
    w_key,
    w_value,
    w_out,
    norm_gain_ffn,
    w_router,
    shared_gate,
    shared_up,
    shared_down,
    expert_gate,
    expert_up,
    expert_down,
):
    gathered = (
        lax.all_gather(norm_gain_attn, "exp", axis=0, tiled=True),
        lax.all_gather(w_query, "exp", axis=0, tiled=True),
        lax.all_gather(w_key, "exp", axis=0, tiled=True),
        lax.all_gather(w_value, "exp", axis=0, tiled=True),
        lax.all_gather(w_out, "exp", axis=0, tiled=True),
        lax.all_gather(norm_gain_ffn, "exp", axis=0, tiled=True),
        lax.all_gather(w_router, "exp", axis=0, tiled=True),
        lax.all_gather(shared_gate, "exp", axis=0, tiled=True),
        lax.all_gather(shared_up, "exp", axis=0, tiled=True),
        lax.all_gather(shared_down, "exp", axis=0, tiled=True),
    )
    gain_attn, query_w, key_w, value_w, out_w, gain_ffn, router_w, sgate_w, sup_w, sdown_w = (
        gathered
    )
    tok_rows = tokens.shape[1]
    model_width = tokens.shape[2]
    head_count = HEADS
    head_width = model_width // head_count
    top_count = routes.shape[2]
    experts = w_router.shape[1]
    slot_count = tok_rows * top_count * 5 // (experts * 4)
    inv_root = head_width ** (-0.5)
    seq_place = lax.axis_index("seq")
    inputs = tokens[0].astype(jnp.float32)
    positions = seq_place * tok_rows + jnp.arange(tok_rows, dtype=jnp.int32)
    cosine, sine = rotary_tables(positions, head_width)
    seg_row = segments[0]
    own_seg = lax.dynamic_slice_in_dim(seg_row, seq_place * tok_rows, tok_rows)
    prior_seg = lax.dynamic_slice_in_dim(
        seg_row, jnp.maximum(seq_place - 1, 0) * tok_rows, tok_rows
    )
    key_places = jnp.concatenate([positions - tok_rows, positions])
    key_segs = jnp.concatenate([prior_seg, own_seg])
    allowed = (
        (key_places[None, :] <= positions[:, None])
        & (key_places[None, :] >= 0)
        & (key_segs[None, :] == own_seg[:, None])
    )
    normed_attn, inv_attn = rms_forward(inputs, gain_attn.astype(jnp.float32))
    act_attn = normed_attn.astype(jnp.bfloat16)
    queries = rotate(
        jnp.dot(act_attn, query_w, preferred_element_type=jnp.float32).reshape(
            tok_rows, head_count, head_width
        ),
        cosine,
        sine,
    ).astype(jnp.bfloat16)
    keys_own = rotate(
        jnp.dot(act_attn, key_w, preferred_element_type=jnp.float32).reshape(
            tok_rows, head_count, head_width
        ),
        cosine,
        sine,
    ).astype(jnp.bfloat16)
    values_own = (
        jnp.dot(act_attn, value_w, preferred_element_type=jnp.float32)
        .astype(jnp.bfloat16)
        .reshape(tok_rows, head_count, head_width)
    )
    keys_prior, values_prior = passed_along((keys_own, values_own), "seq", 1)
    keys_all = jnp.concatenate([keys_prior, keys_own], axis=0)
    values_all = jnp.concatenate([values_prior, values_own], axis=0)
    scores = score_block(queries, keys_all, allowed, inv_root)
    top_score = jnp.max(scores, axis=-1, keepdims=True)
    expo = jnp.exp(scores - top_score)
    total = jnp.sum(expo, axis=-1, keepdims=True)
    probs = expo / total
    log_total = top_score + jnp.log(total)
    mixed = (
        jnp.einsum(
            "hts,shd->thd",
            probs.astype(jnp.bfloat16),
            values_all,
            preferred_element_type=jnp.float32,
        )
        .reshape(tok_rows, model_width)
        .astype(jnp.bfloat16)
    )
    hidden_one = inputs + jnp.dot(mixed, out_w, preferred_element_type=jnp.float32)
    normed_ffn, inv_ffn = rms_forward(hidden_one, gain_ffn.astype(jnp.float32))
    act_ffn = normed_ffn.astype(jnp.bfloat16)
    logits = jnp.dot(act_ffn, router_w, preferred_element_type=jnp.float32)
    route_rows = routes[0]
    picked = route_rows[:, :, None] == jnp.arange(experts, dtype=jnp.int32)[None, None, :]
    chosen = jnp.sum(jnp.where(picked, logits[:, None, :], 0.0), axis=-1)
    gates = jax.nn.softmax(chosen, axis=-1)
    gate_s = jnp.dot(act_ffn, sgate_w, preferred_element_type=jnp.float32)
    up_s = jnp.dot(act_ffn, sup_w, preferred_element_type=jnp.float32)
    hidden_s = (jax.nn.silu(gate_s) * up_s).astype(jnp.bfloat16)
    out_s = jnp.dot(hidden_s, sdown_w, preferred_element_type=jnp.float32)
    flat_route = route_rows.reshape(-1)
    member = (flat_route[:, None] == jnp.arange(experts, dtype=jnp.int32)[None, :]).astype(
        jnp.int32
    )
    rank = jnp.sum((jnp.cumsum(member, axis=0) - member) * member, axis=1)
    slot = flat_route * slot_count + rank
    source_rows = jnp.repeat(act_ffn, top_count, axis=0)
    outgoing = (
        jnp.zeros((experts * slot_count, model_width), jnp.bfloat16)
        .at[slot]
        .set(source_rows)
        .reshape(experts, slot_count, model_width)
    )
    gate_local = expert_gate[0]
    up_local = expert_up[0]
    down_local = expert_down[0]
    arrived = lax.all_to_all(outgoing, "exp", split_axis=0, concat_axis=0, tiled=True)
    gate_e = jnp.einsum("scd,dh->sch", arrived, gate_local, preferred_element_type=jnp.float32)
    up_e = jnp.einsum("scd,dh->sch", arrived, up_local, preferred_element_type=jnp.float32)
    hidden_e = (jax.nn.silu(gate_e) * up_e).astype(jnp.bfloat16)
    result = jnp.einsum(
        "sch,hd->scd", hidden_e, down_local, preferred_element_type=jnp.float32
    ).astype(jnp.bfloat16)
    result, arrived, gate_e, up_e, hidden_e = (result, arrived, gate_e, up_e, hidden_e)
    returned = lax.all_to_all(result, "exp", split_axis=0, concat_axis=0, tiled=True)
    picked_out = (
        returned.reshape(experts * slot_count, model_width)[slot]
        .reshape(tok_rows, top_count, model_width)
        .astype(jnp.float32)
    )
    routed = jnp.sum(gates[:, :, None] * picked_out, axis=1)
    final = hidden_one + out_s + routed
    layer_out = final.astype(jnp.bfloat16)
    gain_attn, query_w, key_w, value_w, out_w, gain_ffn, router_w, sgate_w, sup_w, sdown_w = (
        gathered
    )
    grad_final = cotangent[0].astype(jnp.float32)
    grad_picked = (gates[:, :, None] * grad_final[:, None, :]).astype(jnp.bfloat16)
    grad_gates = jnp.sum(grad_final[:, None, :] * picked_out, axis=-1)
    send_grad = (
        jnp.zeros((experts * slot_count, model_width), jnp.bfloat16)
        .at[slot]
        .set(grad_picked.reshape(-1, model_width))
        .reshape(experts, slot_count, model_width)
    )
    grad_result = lax.all_to_all(send_grad, "exp", split_axis=0, concat_axis=0, tiled=True)
    grad_expert_down = jnp.einsum(
        "sch,scd->hd", hidden_e, grad_result, preferred_element_type=jnp.float32
    )
    grad_hidden_e = jnp.einsum(
        "scd,hd->sch", grad_result, down_local, preferred_element_type=jnp.float32
    )
    silu_e, slope_e = silu_parts(gate_e)
    grad_gate_e = (grad_hidden_e * up_e * slope_e).astype(jnp.bfloat16)
    grad_up_e = (grad_hidden_e * silu_e).astype(jnp.bfloat16)
    grad_expert_gate = jnp.einsum(
        "scd,sch->dh", arrived, grad_gate_e, preferred_element_type=jnp.float32
    )
    grad_expert_up = jnp.einsum(
        "scd,sch->dh", arrived, grad_up_e, preferred_element_type=jnp.float32
    )
    grad_arrived = (
        jnp.einsum("sch,dh->scd", grad_gate_e, gate_local, preferred_element_type=jnp.float32)
        + jnp.einsum("sch,dh->scd", grad_up_e, up_local, preferred_element_type=jnp.float32)
    ).astype(jnp.bfloat16)
    grad_returned = lax.all_to_all(grad_arrived, "exp", split_axis=0, concat_axis=0, tiled=True)
    grad_routed = jnp.sum(
        grad_returned.reshape(experts * slot_count, model_width)[slot]
        .reshape(tok_rows, top_count, model_width)
        .astype(jnp.float32),
        axis=1,
    )
    grad_chosen = gates * (grad_gates - jnp.sum(gates * grad_gates, axis=-1, keepdims=True))
    grad_logits = jnp.sum(jnp.where(picked, grad_chosen[:, :, None], 0.0), axis=1).astype(
        jnp.bfloat16
    )
    grad_router = jnp.einsum("td,te->de", act_ffn, grad_logits, preferred_element_type=jnp.float32)
    grad_low = grad_final.astype(jnp.bfloat16)
    grad_shared_down = jnp.einsum(
        "th,td->hd", hidden_s, grad_low, preferred_element_type=jnp.float32
    )
    grad_hidden_s = jnp.dot(grad_low, sdown_w.T, preferred_element_type=jnp.float32)
    silu_s, slope_s = silu_parts(gate_s)
    grad_gate_s = (grad_hidden_s * up_s * slope_s).astype(jnp.bfloat16)
    grad_up_s = (grad_hidden_s * silu_s).astype(jnp.bfloat16)
    grad_shared_gate = jnp.einsum(
        "td,th->dh", act_ffn, grad_gate_s, preferred_element_type=jnp.float32
    )
    grad_shared_up = jnp.einsum("td,th->dh", act_ffn, grad_up_s, preferred_element_type=jnp.float32)
    grad_act_ffn = (
        grad_routed
        + jnp.dot(grad_logits, router_w.T, preferred_element_type=jnp.float32)
        + jnp.dot(grad_gate_s, sgate_w.T, preferred_element_type=jnp.float32)
        + jnp.dot(grad_up_s, sup_w.T, preferred_element_type=jnp.float32)
    )
    grad_norm_f, grad_gain_ffn = rms_backward(
        hidden_one, inv_ffn, gain_ffn.astype(jnp.float32), grad_act_ffn
    )
    grad_hidden_one = grad_final + grad_norm_f
    grad_attn_low = grad_hidden_one.astype(jnp.bfloat16)
    grad_w_out = jnp.einsum("tk,td->kd", mixed, grad_attn_low, preferred_element_type=jnp.float32)
    grad_mixed = (
        jnp.dot(grad_attn_low, out_w.T, preferred_element_type=jnp.float32)
        .astype(jnp.bfloat16)
        .reshape(tok_rows, head_count, head_width)
    )
    probs_back = jnp.exp(score_block(queries, keys_all, allowed, inv_root) - log_total)
    grad_probs = jnp.einsum(
        "thd,shd->hts", grad_mixed, values_all, preferred_element_type=jnp.float32
    )
    inner = jnp.sum(probs_back * grad_probs, axis=-1, keepdims=True)
    grad_scores = (probs_back * (grad_probs - inner)).astype(jnp.bfloat16)
    grad_values_all = jnp.einsum(
        "hts,thd->shd",
        probs_back.astype(jnp.bfloat16),
        grad_mixed,
        preferred_element_type=jnp.float32,
    )
    grad_query_rot = (
        jnp.einsum("hts,shd->thd", grad_scores, keys_all, preferred_element_type=jnp.float32)
        * inv_root
    )
    grad_keys_all = (
        jnp.einsum("hts,thd->shd", grad_scores, queries, preferred_element_type=jnp.float32)
        * inv_root
    )
    keys_later, values_later = (
        passed_along(grad_keys_all[:tok_rows].astype(jnp.bfloat16), "seq", -1).astype(jnp.float32),
        passed_along(grad_values_all[:tok_rows].astype(jnp.bfloat16), "seq", -1).astype(
            jnp.float32
        ),
    )
    grad_key_rot = grad_keys_all[tok_rows:] + keys_later
    grad_value = (
        (grad_values_all[tok_rows:] + values_later)
        .astype(jnp.bfloat16)
        .reshape(tok_rows, model_width)
    )
    grad_query = (
        unrotate(grad_query_rot, cosine, sine).astype(jnp.bfloat16).reshape(tok_rows, model_width)
    )
    grad_key = (
        unrotate(grad_key_rot, cosine, sine).astype(jnp.bfloat16).reshape(tok_rows, model_width)
    )
    grad_w_query = jnp.einsum("td,tk->dk", act_attn, grad_query, preferred_element_type=jnp.float32)
    grad_w_key = jnp.einsum("td,tk->dk", act_attn, grad_key, preferred_element_type=jnp.float32)
    grad_w_value = jnp.einsum("td,tk->dk", act_attn, grad_value, preferred_element_type=jnp.float32)
    grad_act_attn = (
        jnp.dot(grad_query, query_w.T, preferred_element_type=jnp.float32)
        + jnp.dot(grad_key, key_w.T, preferred_element_type=jnp.float32)
        + jnp.dot(grad_value, value_w.T, preferred_element_type=jnp.float32)
    )
    grad_norm_a, grad_gain_attn = rms_backward(
        inputs, inv_attn, gain_attn.astype(jnp.float32), grad_act_attn
    )
    grad_tokens = grad_hidden_one + grad_norm_a
    (
        part_gain_attn,
        part_query,
        part_key,
        part_value,
        part_out,
        part_gain_ffn,
        part_router,
        part_sgate,
        part_sup,
        part_sdown,
    ) = (
        lax.psum_scatter(grad_gain_attn, "exp", scatter_dimension=0, tiled=True),
        lax.psum_scatter(grad_w_query, "exp", scatter_dimension=0, tiled=True),
        lax.psum_scatter(grad_w_key, "exp", scatter_dimension=0, tiled=True),
        lax.psum_scatter(grad_w_value, "exp", scatter_dimension=0, tiled=True),
        lax.psum_scatter(grad_w_out, "exp", scatter_dimension=0, tiled=True),
        lax.psum_scatter(grad_gain_ffn, "exp", scatter_dimension=0, tiled=True),
        lax.psum_scatter(grad_router, "exp", scatter_dimension=0, tiled=True),
        lax.psum_scatter(grad_shared_gate, "exp", scatter_dimension=0, tiled=True),
        lax.psum_scatter(grad_shared_up, "exp", scatter_dimension=0, tiled=True),
        lax.psum_scatter(grad_shared_down, "exp", scatter_dimension=0, tiled=True),
    )
    summed = (
        lax.psum(part_gain_attn.astype(jnp.bfloat16), "seq").astype(jnp.float32),
        lax.psum(part_query.astype(jnp.bfloat16), "seq").astype(jnp.float32),
        lax.psum(part_key.astype(jnp.bfloat16), "seq").astype(jnp.float32),
        lax.psum(part_value.astype(jnp.bfloat16), "seq").astype(jnp.float32),
        lax.psum(part_out.astype(jnp.bfloat16), "seq").astype(jnp.float32),
        lax.psum(part_gain_ffn.astype(jnp.bfloat16), "seq").astype(jnp.float32),
        lax.psum(part_router.astype(jnp.bfloat16), "seq").astype(jnp.float32),
        lax.psum(part_sgate.astype(jnp.bfloat16), "seq").astype(jnp.float32),
        lax.psum(part_sup.astype(jnp.bfloat16), "seq").astype(jnp.float32),
        lax.psum(part_sdown.astype(jnp.bfloat16), "seq").astype(jnp.float32),
        lax.psum(grad_expert_gate.astype(jnp.bfloat16), "seq").astype(jnp.float32),
        lax.psum(grad_expert_up.astype(jnp.bfloat16), "seq").astype(jnp.float32),
        lax.psum(grad_expert_down.astype(jnp.bfloat16), "seq").astype(jnp.float32),
    )
    return (
        layer_out[None],
        grad_tokens[None],
        summed[0],
        summed[1],
        summed[2],
        summed[3],
        summed[4],
        summed[5],
        summed[6],
        summed[7],
        summed[8],
        summed[9],
        summed[10][None],
        summed[11][None],
        summed[12][None],
    )


def solution(mesh):
    in_specs = (
        P("exp", "seq", None),
        P("exp", "seq", None),
        P("exp", None),
        P("exp", "seq", None),
        P("exp"),
        P("exp", None),
        P("exp", None),
        P("exp", None),
        P("exp", None),
        P("exp"),
        P("exp", None),
        P("exp", None),
        P("exp", None),
        P("exp", None),
        P("exp", None, None),
        P("exp", None, None),
        P("exp", None, None),
    )
    out_specs = (
        P("exp", "seq", None),
        P("exp", "seq", None),
        P("exp"),
        P("exp", None),
        P("exp", None),
        P("exp", None),
        P("exp", None),
        P("exp"),
        P("exp", None),
        P("exp", None),
        P("exp", None),
        P("exp", None),
        P("exp", None, None),
        P("exp", None, None),
        P("exp", None, None),
    )
    return jax.shard_map(
        per_device, mesh=mesh, in_specs=in_specs, out_specs=out_specs, check_vma=False
    )
```

profile of v0, /device:TPU:1, one launch (start us, length us, event | category | flops | bytes accessed | tf_op | source)
XLA Modules:
  0.0 2178.4 jit_solution(13799068319228711951)
XLA Ops:
  20.4 143.6 %all-reduce.18 = (bf16[1280]{0:T(1024)(128)(2,1)S(1)}, bf16[1280]{0:T(1024)(128)(2,1)S(1)}) all-reduce(bf16[1280]{0:T(1024)(128)(2,1)S(1)} %dynamic-update-slice, bf16[1280]{0:T(1024)(128)(2,1)S(1)} %dynamic-update-slice.1), channel_id=1, replica_groups=mesh['seq'=2,'exp'=64] {'exp'}, use_global_device_ids=true, to_apply=%add | all-reduce | flops 2560 | bytes 10240
  167.0 6.1 reshape.562
  173.2 5.7 copy.106
  178.8 47.1 %all-gather.20.cloned.1.call-done = bf16[64,20,1280]{2,1,0:T(8,128)(2,1)} async-done(((bf16[1,20,1280]{2,1,0:T(8,128)(2,1)}), bf16[64,20,1280]{2,1,0:T(8,128)(2,1)}) %all-gather.20.cloned.1.call-update) | async-done | bytes 3276816 | tf_op jit(solution)/shard_map/all_gather | solution.py:91
  226.0 6.1 reshape.564
  232.1 5.7 copy.107
  243.8 5.2 collective-permute-start.1
  249.1 83.8 %all-gather.16.cloned.1.call-done = bf16[64,20,1280]{2,1,0:T(8,128)(2,1)} async-done(((bf16[1,20,1280]{2,1,0:T(8,128)(2,1)}), bf16[64,20,1280]{2,1,0:T(8,128)(2,1)}) %all-gather.16.cloned.1.call-update) | async-done | bytes 3276816 | tf_op jit(solution)/shard_map/all_gather | solution.py:92
  332.9 6.1 reshape.560
  341.8 5.0 collective-permute-start
  346.9 92.2 %all-gather.22.cloned.1.call-done = bf16[64,20,1280]{2,1,0:T(8,128)(2,1)} async-done(((bf16[1,20,1280]{2,1,0:T(8,128)(2,1)}), bf16[64,20,1280]{2,1,0:T(8,128)(2,1)}) %all-gather.22.cloned.1.call-update) | async-done | bytes 3276816 | tf_op jit(solution)/shard_map/all_gather | solution.py:93
  439.1 6.1 reshape.566
  457.0 8.5 scatter_custom_fusion
  470.1 6.4 all-to-all-start
  480.2 5.3 mul.475
  485.4 118.2 %all-gather.7 = bf16[64,20,64]{2,1,0:T(8,128)(2,1)} all-gather(bf16[1,20,64]{2,1,0:T(8,128)(2,1)S(1)} %bitcast.240), channel_id=1, replica_groups=mesh['seq'=2,'exp'=64] {'exp'}, dimensions={0}, use_global_device_ids=true | all-gather | bytes 166400 | tf_op jit(solution)/shard_map/all_gather | solution.py:95
  608.3 12.4 scatter_custom_fusion.1
  625.3 5.7 all-to-all-start.2
  633.5 4.8 reshape.568
  638.3 79.7 %all-gather.26.cloned.1.call-done = bf16[64,20,896]{2,1,0:T(8,128)(2,1)} async-done(((bf16[1,20,896]{2,1,0:T(8,128)(2,1)}), bf16[64,20,896]{2,1,0:T(8,128)(2,1)}) %all-gather.26.cloned.1.call-update) | async-done | bytes 2293776 | tf_op jit(solution)/shard_map/all_gather | solution.py:97
  718.0 4.7 reshape.570
  722.8 100.8 %all-gather.28.cloned.1.call-done = bf16[64,14,1280]{2,1,0:T(8,128)(2,1)} async-done(((bf16[1,14,1280]{2,1,0:T(8,128)(2,1)}), bf16[64,14,1280]{2,1,0:T(8,128)(2,1)}) %all-gather.28.cloned.1.call-update) | async-done | bytes 2293776 | tf_op jit(solution)/shard_map/all_gather | solution.py:98
  832.1 7.2 fusion.21
  839.4 7.1 fusion.17
  846.5 10.6 multiply_convert_fusion.1
  864.0 6.2 all-to-all-start.1
  891.6 28.8 %all-to-all-done.1 = bf16[64,17,1280]{2,1,0:T(8,128)(2,1)} async-done(((bf16[64,17,1280]{2,1,0:T(8,128)(2,1)}), bf16[64,17,1280]{2,1,0:T(8,128)(2,1)}, u32[]{:S(2)}, u32[]{:S(2)}) %all-to-all-start.1) | async-done | bytes 2785312 | tf_op jit(solution)/shard_map/all_to_all | solution.py:203
  920.5 7.8 all-to-all-start.3
  928.9 7.7 fusion.6
  936.7 7.4 fusion.7
  956.5 4.9 multiply_reduce_fusion
  961.5 17.0 all-to-all-done.3
  991.0 5.0 reduce_sum.154
  1015.5 7.1 collective-permute-done.2
  1034.7 393.7 %fusion.101 = (f32[24,1280]{1,0:T(8,128)S(1)}, f32[24,1280]{1,0:T(8,128)S(1)}, f32[24,1280]{1,0:T(8,128)S(1)}, f32[24,1280]{1,0:T(8,128)S(1)}, f32[16,1280]{1,0:T(8,128)S(1)}) fusion(f32[1280,1280]{1,0:T(8,128)} %fusion.65, f32[1280,1280]{1,0:T(8,128)} %fusion.69, f32[1280,1280]{1,0:T(8,128)} %fusion.67, f32[1280,1280]{1,0:T(8,128)} %fusion.77, ...), kind=kCustom, calls=%all-reduce-scatter.5 | all-reduce-scatter fusion | flops 9175042 | bytes 31375872
  1428.4 8.4 collective-permute-start.14
  1442.2 5.3 collective-permute-start.36
  1447.6 4.8 collective-permute-start.47
  1489.1 331.3 %all-reduce.29 = (bf16[1280]{0:T(1024)(128)(2,1)S(1)}, bf16[1280]{0:T(1024)(128)(2,1)S(1)}, bf16[1280,64]{1,0:T(8,128)(2,1)}, bf16[1280,896]{1,0:T(8,128)(2,1)}, bf16[1280,896]{1,0:T(8,128)(2,1)}) all-reduce(f32[1280]{0:T(1024)S(1)} %get-tuple-element.19, f32[1280]{0:T(1024)S(1)} %copy-done.71, ...), channel_id=2, replica_groups=mesh['seq'=2,'exp'=64] {'exp'}, use_global_device_ids=true, to_apply=%region_21.22.clone | all-reduce | flops 2378240 | bytes 14269440
  1841.5 18.2 collective-permute-start.19
  1859.6 5.6 collective-permute-start.18
  1877.2 7.1 concatenate.42
  1897.7 4.9 concatenate.38
  1916.1 7.1 concatenate.39
  1931.8 4.9 concatenate.40
  1953.7 7.3 fusion.8
  1966.4 17.6 all-reduce.26.cloned.1.call-done
  1997.9 164.4 %all-reduce.28.cloned.1.call-done = (bf16[1,1280,896]{2,1,0:T(8,128)(2,1)}, bf16[1,1280,896]{2,1,0:T(8,128)(2,1)}, bf16[1,896,1280]{2,1,0:T(8,128)(2,1)}) async-done(((bf16[1,1280,896]{2,1,0:T(8,128)(2,1)}, bf16[1,1280,896]{2,1,0:T(8,128)(2,1)}, bf16[1,896,1280]{2,1,0:T(8,128)(2,1)}), (bf16[1,1280,896]{2,1,0:T(8,128)(2,1)}, bf16[1,1280,896]{2,1,0:T(8,128)(2,1)}, ...) | async-done | bytes 6881296 | tf_op jit(solution)/shard_map/psum | solution.py:369
  (457 shorter events, 302.8 us)
Async XLA Ops:
  7.2 159.8 %all-gather.18.cloned.1.call-start = ((), (), s32[]{:S(2)}) async-start(), calls=%async_computation.5 | async-start | bytes 3993600 | tf_op jit(solution)/shard_map/all_gather | solution.py:90
  7.9 218.1 %all-gather.20.cloned.1.call-start = ((), (), s32[]{:S(2)}) async-start(), calls=%async_computation.6 | async-start | bytes 3993600 | tf_op jit(solution)/shard_map/all_gather | solution.py:91
  8.7 324.2 %all-gather.16.cloned.1.call-start = ((), (), s32[]{:S(2)}) async-start(), calls=%async_computation.4 | async-start | bytes 3993600 | tf_op jit(solution)/shard_map/all_gather | solution.py:92
  9.4 429.7 %all-gather.22.cloned.1.call-start = ((), (), s32[]{:S(2)}) async-start(), calls=%async_computation.7 | async-start | bytes 3993600 | tf_op jit(solution)/shard_map/all_gather | solution.py:93
  10.0 623.6 %all-gather.24.cloned.1.call-start = ((), (), s32[]{:S(2)}) async-start(), calls=%async_computation.8 | async-start | bytes 2795520 | tf_op jit(solution)/shard_map/all_gather | solution.py:96
  10.6 707.5 %all-gather.26.cloned.1.call-start = ((), (), s32[]{:S(2)}) async-start(), calls=%async_computation.9 | async-start | bytes 2795520 | tf_op jit(solution)/shard_map/all_gather | solution.py:97
  11.2 812.4 %all-gather.28.cloned.1.call-start = ((), (), s32[]{:S(2)}) async-start(), calls=%async_computation.10 | async-start | bytes 2662400 | tf_op jit(solution)/shard_map/all_gather | solution.py:98
  243.8 201.4 %collective-permute-start.1 = (bf16[128,10,128]{0,2,1:T(8,128)(2,1)}, bf16[128,10,128]{0,2,1:T(8,128)(2,1)}, u32[]{:S(2)}, u32[]{:S(2)}) collective-permute-start(bf16[128,10,128]{0,2,1:T(8,128)(2,1)} %pad_maximum_fusion.4), channel_id=1, source_target_pairs={{0,64},{1,65},{2,66},{3,67},{4,68},{5,69},{6,70},{7,71},{8,72},{9,... | collective-permute-start | bytes 983048 | tf_op jit(solution)/shard_map/ppermute | solution.py:16
  341.8 105.4 %collective-permute-start = (bf16[128,10,128]{0,2,1:T(8,128)(2,1)S(1)}, bf16[128,10,128]{0,2,1:T(8,128)(2,1)}, u32[]{:S(2)}, u32[]{:S(2)}) collective-permute-start(bf16[128,10,128]{0,2,1:T(8,128)(2,1)S(1)} %bitcast.227), channel_id=1, source_target_pairs={{0,64},{1,65},{2,66},{3,67},{4,68},{5,69},{6,70},{7,71},{8,72},{9,... | collective-permute-start | bytes 983048 | tf_op jit(solution)/shard_map/ppermute | solution.py:16
  470.1 155.1 %all-to-all-start = ((bf16[64,17,1280]{2,1,0:T(8,128)(2,1)}), bf16[64,17,1280]{2,1,0:T(8,128)(2,1)}, u32[]{:S(2)}, u32[]{:S(2)}) async-start(bf16[64,17,1280]{2,1,0:T(8,128)(2,1)} %reshape.512), calls=%async_computation | async-start | bytes 7864320 | tf_op jit(solution)/shard_map/all_to_all | solution.py:195
  625.3 221.2 %all-to-all-start.2 = ((bf16[64,17,1280]{2,1,0:T(8,128)(2,1)}), bf16[64,17,1280]{2,1,0:T(8,128)(2,1)}, u32[]{:S(2)}, u32[]{:S(2)}) async-start(bf16[64,17,1280]{2,1,0:T(8,128)(2,1)} %reshape.514), calls=%async_computation.2 | async-start | bytes 7864320 | tf_op jit(solution)/shard_map/all_to_all | solution.py:224
  864.0 56.4 %all-to-all-start.1 = ((bf16[64,17,1280]{2,1,0:T(8,128)(2,1)}), bf16[64,17,1280]{2,1,0:T(8,128)(2,1)}, u32[]{:S(2)}, u32[]{:S(2)}) async-start(bf16[64,17,1280]{2,1,0:T(8,128)(2,1)} %copy.117), calls=%async_computation.1 | async-start | bytes 7864320 | tf_op jit(solution)/shard_map/all_to_all | solution.py:203
  920.5 58.0 %all-to-all-start.3 = ((bf16[64,17,1280]{2,1,0:T(8,128)(2,1)}), bf16[64,17,1280]{2,1,0:T(8,128)(2,1)}, u32[]{:S(2)}, u32[]{:S(2)}) async-start(bf16[64,17,1280]{2,1,0:T(8,128)(2,1)} %copy.120), calls=%async_computation.3 | async-start | bytes 7864320 | tf_op jit(solution)/shard_map/all_to_all | solution.py:244
  928.2 1055.8 %all-reduce.26.cloned.1.call-start = ((), (), s32[]{:S(2)}) async-start(), calls=%async_computation.11 | async-start | bytes 759808 | tf_op jit(solution)/shard_map/psum | solution.py:359
  1012.9 17.8 collective-permute-start.3
  1428.4 19.2 collective-permute-start.14
  1438.9 29.5 %collective-permute-start.54 = (bf16[16,1280]{1,0:T(8,128)(2,1)S(1)}, bf16[16,1280]{1,0:T(8,128)(2,1)S(1)}, u32[]{:S(2)}, u32[]{:S(2)}) collective-permute-start(bf16[16,1280]{1,0:T(8,128)(2,1)S(1)} %convert.136), channel_id=1, source_target_pairs={{0,7},{1,8},{2,9},{3,10},{4,11},{5,12},{6,13},{7,14},{8,15},{9,16}... | collective-permute-start | bytes 122888
  1440.2 30.8 %collective-permute-start.53 = (bf16[16,1280]{1,0:T(8,128)(2,1)S(1)}, bf16[16,1280]{1,0:T(8,128)(2,1)S(1)}, u32[]{:S(2)}, u32[]{:S(2)}) collective-permute-start(bf16[16,1280]{1,0:T(8,128)(2,1)S(1)} %convert.136), channel_id=1, source_target_pairs={{0,6},{1,7},{2,8},{3,9},{4,10},{5,11},{6,12},{7,13},{8,14},{9,15},... | collective-permute-start | bytes 122888
  1457.9 18.1 collective-permute-start.52
  1460.9 17.9 collective-permute-start.51
  1464.1 16.0 collective-permute-start.50
  1475.9 345.7 %collective-permute-start.13 = (bf16[24,1280]{1,0:T(8,128)(2,1)S(1)}, bf16[24,1280]{1,0:T(8,128)(2,1)S(1)}, u32[]{:S(2)}, u32[]{:S(2)}) collective-permute-start(bf16[24,1280]{1,0:T(8,128)(2,1)S(1)} %convert.135), channel_id=1, source_target_pairs={{0,10},{1,11},{2,12},{3,13},{4,14},{5,15},{6,16},{7,17},{8,18},{9,... | collective-permute-start | bytes 184328
  1478.8 344.1 %collective-permute-start.12 = (bf16[24,1280]{1,0:T(8,128)(2,1)S(1)}, bf16[24,1280]{1,0:T(8,128)(2,1)S(1)}, u32[]{:S(2)}, u32[]{:S(2)}) collective-permute-start(bf16[24,1280]{1,0:T(8,128)(2,1)S(1)} %convert.135), channel_id=1, source_target_pairs={{0,9},{1,10},{2,11},{3,12},{4,13},{5,14},{6,15},{7,16},{8,17},{9,1... | collective-permute-start | bytes 184328
  1480.1 344.1 %collective-permute-start.11 = (bf16[24,1280]{1,0:T(8,128)(2,1)S(1)}, bf16[24,1280]{1,0:T(8,128)(2,1)S(1)}, u32[]{:S(2)}, u32[]{:S(2)}) collective-permute-start(bf16[24,1280]{1,0:T(8,128)(2,1)S(1)} %convert.135), channel_id=1, source_target_pairs={{0,8},{1,9},{2,10},{3,11},{4,12},{5,13},{6,14},{7,15},{8,16},{9,17... | collective-permute-start | bytes 184328
  1482.7 343.5 %collective-permute-start.10 = (bf16[24,1280]{1,0:T(8,128)(2,1)S(1)}, bf16[24,1280]{1,0:T(8,128)(2,1)S(1)}, u32[]{:S(2)}, u32[]{:S(2)}) collective-permute-start(bf16[24,1280]{1,0:T(8,128)(2,1)S(1)} %convert.135), channel_id=1, source_target_pairs={{0,7},{1,8},{2,9},{3,10},{4,11},{5,12},{6,13},{7,14},{8,15},{9,16}... | collective-permute-start | bytes 184328
  1485.3 342.8 %collective-permute-start.9 = (bf16[24,1280]{1,0:T(8,128)(2,1)S(1)}, bf16[24,1280]{1,0:T(8,128)(2,1)S(1)}, u32[]{:S(2)}, u32[]{:S(2)}) collective-permute-start(bf16[24,1280]{1,0:T(8,128)(2,1)S(1)} %convert.135), channel_id=1, source_target_pairs={{0,6},{1,7},{2,8},{3,9},{4,10},{5,11},{6,12},{7,13},{8,14},{9,15},... | collective-permute-start | bytes 184328
  1832.7 26.9 %collective-permute-start.23 = (bf16[24,1280]{1,0:T(8,128)(2,1)S(1)}, bf16[24,1280]{1,0:T(8,128)(2,1)S(1)}, u32[]{:S(2)}, u32[]{:S(2)}) collective-permute-start(bf16[24,1280]{1,0:T(8,128)(2,1)S(1)} %convert.134), channel_id=1, source_target_pairs={{0,9},{1,10},{2,11},{3,12},{4,13},{5,14},{6,15},{7,16},{8,17},{9,1... | collective-permute-start | bytes 184328
  1834.1 31.2 %collective-permute-start.22 = (bf16[24,1280]{1,0:T(8,128)(2,1)S(1)}, bf16[24,1280]{1,0:T(8,128)(2,1)S(1)}, u32[]{:S(2)}, u32[]{:S(2)}) collective-permute-start(bf16[24,1280]{1,0:T(8,128)(2,1)S(1)} %convert.134), channel_id=1, source_target_pairs={{0,8},{1,9},{2,10},{3,11},{4,12},{5,13},{6,14},{7,15},{8,16},{9,17... | collective-permute-start | bytes 184328
  1835.4 33.6 %collective-permute-start.21 = (bf16[24,1280]{1,0:T(8,128)(2,1)S(1)}, bf16[24,1280]{1,0:T(8,128)(2,1)S(1)}, u32[]{:S(2)}, u32[]{:S(2)}) collective-permute-start(bf16[24,1280]{1,0:T(8,128)(2,1)S(1)} %convert.134), channel_id=1, source_target_pairs={{0,7},{1,8},{2,9},{3,10},{4,11},{5,12},{6,13},{7,14},{8,15},{9,16}... | collective-permute-start | bytes 184328
  1836.7 35.6 %collective-permute-start.20 = (bf16[24,1280]{1,0:T(8,128)(2,1)S(1)}, bf16[24,1280]{1,0:T(8,128)(2,1)S(1)}, u32[]{:S(2)}, u32[]{:S(2)}) collective-permute-start(bf16[24,1280]{1,0:T(8,128)(2,1)S(1)} %convert.134), channel_id=1, source_target_pairs={{0,6},{1,7},{2,8},{3,9},{4,10},{5,11},{6,12},{7,13},{8,14},{9,15},... | collective-permute-start | bytes 184328
  1841.5 42.9 %collective-permute-start.19 = (bf16[24,1280]{1,0:T(8,128)(2,1)S(1)}, bf16[24,1280]{1,0:T(8,128)(2,1)S(1)}, u32[]{:S(2)}, u32[]{:S(2)}) collective-permute-start(bf16[24,1280]{1,0:T(8,128)(2,1)S(1)} %convert.134), channel_id=1, source_target_pairs={{0,5},{1,6},{2,7},{3,8},{4,9},{5,10},{6,11},{7,12},{8,13},{9,14},{... | collective-permute-start | bytes 184328
  1859.6 27.9 %collective-permute-start.18 = (bf16[24,1280]{1,0:T(8,128)(2,1)S(1)}, bf16[24,1280]{1,0:T(8,128)(2,1)S(1)}, u32[]{:S(2)}, u32[]{:S(2)}) collective-permute-start(bf16[24,1280]{1,0:T(8,128)(2,1)S(1)} %convert.134), channel_id=1, source_target_pairs={{0,4},{1,5},{2,6},{3,7},{4,8},{5,9},{6,10},{7,11},{8,12},{9,13},{1... | collective-permute-start | bytes 184328
  1865.2 25.2 %collective-permute-start.17 = (bf16[24,1280]{1,0:T(8,128)(2,1)S(1)}, bf16[24,1280]{1,0:T(8,128)(2,1)S(1)}, u32[]{:S(2)}, u32[]{:S(2)}) collective-permute-start(bf16[24,1280]{1,0:T(8,128)(2,1)S(1)} %convert.134), channel_id=1, source_target_pairs={{0,3},{1,4},{2,5},{3,6},{4,7},{5,8},{6,9},{7,10},{8,11},{9,12},{10... | collective-permute-start | bytes 184328
  1868.9 23.4 %collective-permute-start.16 = (bf16[24,1280]{1,0:T(8,128)(2,1)S(1)}, bf16[24,1280]{1,0:T(8,128)(2,1)S(1)}, u32[]{:S(2)}, u32[]{:S(2)}) collective-permute-start(bf16[24,1280]{1,0:T(8,128)(2,1)S(1)} %convert.134), channel_id=1, source_target_pairs={{0,2},{1,3},{2,4},{3,5},{4,6},{5,7},{6,8},{7,9},{8,10},{9,11},{10,... | collective-permute-start | bytes 184328
  1872.3 22.8 %collective-permute-start.15 = (bf16[24,1280]{1,0:T(8,128)(2,1)S(1)}, bf16[24,1280]{1,0:T(8,128)(2,1)S(1)}, u32[]{:S(2)}, u32[]{:S(2)}) collective-permute-start(bf16[24,1280]{1,0:T(8,128)(2,1)S(1)} %convert.134), channel_id=1, source_target_pairs={{0,1},{1,2},{2,3},{3,4},{4,5},{5,6},{6,7},{7,8},{8,9},{9,10},{10,1... | collective-permute-start | bytes 184328
  1884.3 18.2 collective-permute-start.35
  1887.6 17.3 collective-permute-start.34
  1890.4 15.8 collective-permute-start.33
  1892.3 16.0 collective-permute-start.32
  1895.1 16.7 collective-permute-start.31
  1902.6 20.6 collective-permute-start.30
  1904.8 19.8 collective-permute-start.29
  1906.2 19.8 collective-permute-start.28
  1908.4 19.2 collective-permute-start.27
  1911.8 17.1 collective-permute-start.26
  1927.6 16.1 collective-permute-start.43
  1928.9 17.2 collective-permute-start.42
  1953.7 208.6 %all-reduce.28.cloned.1.call-start = ((), (), s32[]{:S(2)}) async-start(), calls=%async_computation.12 | async-start | bytes 13762560 | tf_op jit(solution)/shard_map/psum | solution.py:369
  (114 other events, 3456.1 us)
Sparse Core Ops, SparseCore 0:
  9.7 109.3 all-gather.17
  120.9 105.0 all-gather.19
  227.7 105.1 all-gather.15
  334.5 104.5 all-gather.21
  440.6 137.6 all-gather.23
  579.9 138.1 all-gather.25
  719.7 103.7 all-gather.27
  1953.8 30.2 all-reduce.25
  1987.7 174.5 all-reduce.27
where the time goes:
time: 2190 us; the launch traced here: 2180 us
  blocking collectives  987 us (45%)
  waiting for transfers between devices  644 us (29%)
  starting transfers between devices  190 us (9%)
  local copies, waits for them, and re-layouts  163 us (7%)
  matrix products  120 us (5%)
  other arithmetic  56.8 us (3%)
    unnamed x3, blocking collectives  869 us
    psum x1, waiting for transfers between devices, per_device(): lax.psum(grad_expert_gate.astype(jnp.bfloat16), 'seq').astype(jnp.float32)  164 us
    unnamed x52, starting transfers between devices  150 us
    all_gather x1, blocking collectives, per_device(): lax.all_gather(w_router, 'exp', axis=0, tiled=True)  118 us
    all_gather x1, waiting for transfers between devices, per_device(): lax.all_gather(shared_down, 'exp', axis=0, tiled=True)  101 us
    all_gather x1, waiting for transfers between devices, per_device(): lax.all_gather(w_out, 'exp', axis=0, tiled=True)  92.2 us
    all_gather x1, waiting for transfers between devices, per_device(): lax.all_gather(w_value, 'exp', axis=0, tiled=True)  83.8 us
    all_gather x1, waiting for transfers between devices, per_device(): lax.all_gather(shared_up, 'exp', axis=0, tiled=True)  79.7 us
  transfers between devices with their start and end apart: 69, of which 11 were waited for; matrix products, arithmetic and copies ran while one was open for 12% of the time, Pallas kernels for 0%

commit v1 on v0

v1 whole, which is shorter than its diff:
```python
import functools
import jax
import jax.numpy as jnp
from jax import lax
from jax.experimental import pallas as pl
from jax.experimental.pallas import tpu as pltpu
from jax.sharding import PartitionSpec as P

HEADS = 10
EPSILON = 1e-06
NEG_BIG = -1e30
F32 = jnp.float32
BF16 = jnp.bfloat16
MESH = pl.DeviceIdType.MESH

WIDE = 58
HALF = 29 * 128
UNITS = ((0, 15, 8, 0, 3, 2), (15, 14, 7, 3, 2, 1))


def place():
    hi = lax.axis_index("seq")
    e = lax.axis_index("exp")
    return hi, e // 16, lax.rem(e // 4, 4), lax.rem(e // 2, 2), lax.rem(e, 2)


def device(hi, y, z, lo, c):
    return (hi, ((y * 4 + z) * 2 + lo) * 2 + c)


def up(v):
    return lax.rem(v + 1, 4)


def dn(v):
    return lax.rem(v + 3, 4)


def opp(v):
    return lax.rem(v + 2, 4)


def greet(devices):
    bar = pltpu.get_barrier_semaphore()
    for to in devices:
        pl.semaphore_signal(bar, inc=1, device_id=to, device_id_type=MESH)
    pl.semaphore_wait(bar, len(devices))


class Sender:
    def __init__(self, send_sem, recv_sem, local_sem):
        self.sems = (send_sem, recv_sem, local_sem)
        self.sent = []
        self.kept = 0

    def remote(self, src, dst, to):
        k = len(self.sent)
        copy = pltpu.make_async_remote_copy(
            src_ref=src,
            dst_ref=dst,
            send_sem=self.sems[0].at[k],
            recv_sem=self.sems[1].at[k],
            device_id=to,
            device_id_type=MESH,
        )
        copy.start()
        self.sent.append(copy)
        return copy

    def local(self, src, dst):
        copy = pltpu.make_async_copy(src, dst, self.sems[2].at[self.kept])
        self.kept += 1
        copy.start()
        return copy

    def finish(self):
        for copy in self.sent:
            copy.wait_send()


def arrived(copies):
    for copy in copies:
        copy.wait_recv()


def ring_neighbours(hi, y, z, lo, c):
    return {
        ("y", 1): device(hi, up(y), z, lo, c),
        ("y", -1): device(hi, dn(y), z, lo, c),
        ("z", 1): device(hi, y, up(z), lo, c),
        ("z", -1): device(hi, y, dn(z), lo, c),
    }


def columns(u, half, core):
    s, w, w0, s2, v, v0 = UNITS[u]
    if half == 0:
        w, v = w0, v0
    elif half == 1:
        s, w, s2, v = s + w0, w - w0, s2 + v0, v - v0
    return (
        pl.ds(pl.multiple_of(core * HALF + s * 128, 128), w * 128),
        pl.ds(pl.multiple_of(core * 640 + s2 * 128, 128), v * 128),
    )


def gather_kernel(win, sdw, out, osd, wsib, pw, pwx, blk, bsd, ssem, rsem, lsem):
    hi, y, z, lo, c = place()
    sib = device(hi, y, z, lo, 1 - c)
    xn = device(hi, y, z, 1 - lo, c)
    nb = ring_neighbours(hi, y, z, lo, c)
    greet([sib, xn] + list(nb.values()))
    wires = Sender(ssem, rsem, lsem)
    mul = pl.multiple_of
    j = lo * 2 + c
    other = pl.ds(mul((1 - c) * HALF, 128), HALF)
    mine = pl.ds(mul(c * HALF, 128), HALF)
    other2 = pl.ds(mul((1 - c) * 640, 128), 640)
    mine2 = pl.ds(mul(c * 640, 128), 640)
    r16 = pl.ds(mul(j * 16, 16), 16)
    a = wires.remote(win.at[:, other], wsib, sib)
    b = wires.remote(sdw.at[:, other2], bsd.at[r16], sib)
    bsd[r16, :] = sdw[:, mine2]
    own = win[:, mine]
    a.wait_recv()
    got = wsib[...]
    first = jnp.where(c == 0, own, got)
    second = jnp.where(c == 0, got, own)
    pw[0:16] = first[0:16]
    pw[16:32] = first[16:32] + second[0:16]
    pw[32:48] = second[16:32]
    b.wait_recv()
    a = wires.remote(pw, pwx, xn)
    r32 = pl.ds(mul(lo * 32, 16), 32)
    b = wires.remote(bsd.at[r32], bsd.at[r32], xn)
    a.wait_recv()
    own = pw[...]
    got = pwx[...]
    first = jnp.where(lo == 0, own, got)
    second = jnp.where(lo == 0, got, own)
    blk[0:32] = first[0:32]
    blk[32:48] = first[32:48] + second[0:16]
    blk[48:80] = second[16:48]
    b.wait_recv()
    keep = [wires.local(blk, out.at[y, z, :, mine]), wires.local(bsd, osd.at[y, z, :, mine2])]

    def region(u, half, by, bz):
        c1, c2 = columns(u, half, c)
        return out.at[by, bz, :, c1], osd.at[by, bz, :, c2]

    def send(u, half, by, bz, to, src=None):
        r = region(u, half, by, bz)
        s = src or r
        return [wires.remote(s[0], r[0], to), wires.remote(s[1], r[1], to)]

    def spot(u, q1, q2):
        return (q1, q2) if u == 0 else (q2, q1)

    units = []
    for u in (0, 1):
        a1, a2 = ("y", "z") if u == 0 else ("z", "y")
        p1, p2 = (y, z) if u == 0 else (z, y)
        s, w, w0, s2, v, v0 = UNITS[u]
        src = (blk.at[:, pl.ds(s * 128, w * 128)], bsd.at[:, pl.ds(s2 * 128, v * 128)])
        at = spot(u, p1, p2)
        unit = dict(a1=a1, a2=a2, p1=p1, p2=p2)
        unit["up1"] = send(u, None, *at, nb[a1, 1], src)
        unit["dn1"] = send(u, None, *at, nb[a1, -1], src)
        unit["up2"] = [send(u, None, *at, nb[a2, 1], src)]
        unit["dn2"] = [send(u, None, *at, nb[a2, -1], src)]
        unit["sib"] = [send(u, None, *at, sib, src)]
        units.append(unit)

    def second_axis(u, q1):
        unit = units[u]
        at = spot(u, q1, unit["p2"])
        unit["up2"].append(send(u, None, *at, nb[unit["a2"], 1]))
        unit["dn2"].append(send(u, None, *at, nb[unit["a2"], -1]))
        unit["sib"].append(send(u, None, *at, sib))

    for u, unit in enumerate(units):
        arrived(unit["up1"])
        unit["f1"] = send(u, 0, *spot(u, dn(unit["p1"]), unit["p2"]), nb[unit["a1"], 1])
    for u, unit in enumerate(units):
        arrived(unit["dn1"])
        unit["f2"] = send(u, 1, *spot(u, up(unit["p1"]), unit["p2"]), nb[unit["a1"], -1])
    for u, unit in enumerate(units):
        second_axis(u, dn(unit["p1"]))
        second_axis(u, up(unit["p1"]))
    for u, unit in enumerate(units):
        arrived(unit["f1"])
        arrived(unit["f2"])
        second_axis(u, opp(unit["p1"]))
    turn = [lambda p: p, dn, up, opp]
    for k in range(4):
        for u, unit in enumerate(units):
            q1 = turn[k](unit["p1"])
            arrived(unit["up2"][k])
            at = spot(u, q1, dn(unit["p2"]))
            unit["g1", k] = send(u, 0, *at, nb[unit["a2"], 1])
            unit["sib"].append(send(u, None, *at, sib))
            arrived(unit["dn2"][k])
            at = spot(u, q1, up(unit["p2"]))
            unit["g2", k] = send(u, 1, *at, nb[unit["a2"], -1])
            unit["sib"].append(send(u, None, *at, sib))
    for k in range(4):
        for u, unit in enumerate(units):
            arrived(unit["g1", k])
            arrived(unit["g2", k])
            at = spot(u, turn[k](unit["p1"]), opp(unit["p2"]))
            unit["sib"].append(send(u, None, *at, sib))
    for unit in units:
        for copies in unit["sib"]:
            arrived(copies)
    wires.finish()
    for copy in keep:
        copy.wait()


def gather_weights(shard, down):
    offset = 4 * lax.rem(lax.axis_index("exp"), 4)
    window = lax.dynamic_update_slice(jnp.zeros((32, WIDE * 128), BF16), shard, (offset, 0))
    down = jnp.pad(down, ((0, 2), (0, 0)))
    sems = 4 + 2 * 2 * 36
    out, osd = pl.pallas_call(
        gather_kernel,
        out_shape=(
            jax.ShapeDtypeStruct((4, 4, 80, WIDE * 128), BF16),
            jax.ShapeDtypeStruct((4, 4, 64, 1280), BF16),
        ),
        in_specs=[pl.BlockSpec(memory_space=pltpu.VMEM)] * 2,
        out_specs=(pl.BlockSpec(memory_space=pl.ANY),) * 2,
        scratch_shapes=[
            pltpu.VMEM((32, HALF), BF16),
            pltpu.VMEM((48, HALF), BF16),
            pltpu.VMEM((48, HALF), BF16),
            pltpu.VMEM((80, HALF), BF16),
            pltpu.VMEM((64, 640), BF16),
            pltpu.SemaphoreType.DMA((sems,)),
            pltpu.SemaphoreType.DMA((sems,)),
            pltpu.SemaphoreType.DMA((2,)),
        ],
        compiler_params=pltpu.CompilerParams(
            collective_id=1, has_side_effects=True, vmem_limit_bytes=40 << 20
        ),
        name="gather_weights",
    )(window, down)
    return out.reshape(1280, WIDE * 128), osd.reshape(1024, 1280)


def scatter_kernel(gw, gsd, out, osd, *scratch):
    hold = [scratch[0:2], scratch[2:4]]
    from_sib = [scratch[4:6], scratch[6:8]]
    bufs = [[scratch[8 + 8 * u + 4 * a : 12 + 8 * u + 4 * a] for a in (0, 1)] for u in (0, 1)]
    fin, fsd, wx, wxd, wh, whd, snd, sndd, acc, accd, ssem, rsem, lsem = scratch[24:]
    hi, y, z, lo, c = place()
    sib = device(hi, y, z, lo, 1 - c)
    xn = device(hi, y, z, 1 - lo, c)
    hn = device(1 - hi, y, z, lo, c)
    nb = ring_neighbours(hi, y, z, lo, c)
    greet([sib, xn, hn] + list(nb.values()))
    wires = Sender(ssem, rsem, lsem)
    mul = pl.multiple_of
    first_pos, second_pos = (y, z), (z, y)
    first_axis, second_axis = ("y", "z"), ("z", "y")

    def pair(src, dst, to):
        return [wires.remote(src[0], dst[0], to), wires.remote(src[1], dst[1], to)]

    def region(u, core, q1, q2):
        by, bz = (q1, q2) if u == 0 else (q2, q1)
        c1, c2 = columns(u, None, core)
        return gw.at[by, bz, :, c1], gsd.at[by, bz, :, c2]

    def at(refs, *index):
        return [refs[0].at[index], refs[1].at[index]]

    def order(u):
        p1, p2 = first_pos[u], second_pos[u]
        ones = [opp(p1), up(p1), dn(p1), p1]
        return [(q1, q2) for q2 in (opp(p2), up(p2), dn(p2), p2) for q1 in ones]

    orders = [order(0), order(1)]
    coming = {}
    for k in range(16):
        for u in (0, 1):
            q = orders[u][k]
            coming[u, k] = pair(region(u, 1 - c, *q), at(from_sib[u], *q), sib)
            coming[u, k, "own"] = [wires.local(a, b) for a, b in zip(region(u, c, *q), at(hold[u], *q))]

    def add_in(dst, *more):
        @pl.loop(0, dst.shape[-2] // 16)
        def _(i):
            r = pl.ds(mul(i * 16, 16), 16)
            value = dst[r, :].astype(F32)
            for ref in more:
                value = value + ref[r, :].astype(F32)
            dst[r, :] = value.astype(BF16)

    def ready(u, k):
        arrived(coming[u, k])
        for copy in coming[u, k, "own"]:
            copy.wait()
        for a in (0, 1):
            add_in(hold[u][a].at[orders[u][k]], from_sib[u][a].at[orders[u][k]])
        return at(hold[u], *orders[u][k])

    def half(refs, u, h):
        s, w, w0, s2, v, v0 = UNITS[u]
        lanes = [(0, w0), (w0, w - w0)][h], [(0, v0), (v0, v - v0)][h]
        return [refs[i].at[:, pl.ds(lanes[i][0] * 128, lanes[i][1] * 128)] for i in (0, 1)]

    def buffer(u, i, slot):
        return [bufs[u][0][i].at[slot], bufs[u][1][i].at[slot]]

    ring = {}

    def far_block(u, slot, blk, axis):
        ring[u, slot, 0] = pair(half(blk, u, 0), buffer(u, 0, slot), nb[axis, 1])
        ring[u, slot, 1] = pair(half(blk, u, 1), buffer(u, 1, slot), nb[axis, -1])

    def near_block(u, slot, blk, axis, way):
        h = 0 if way == 1 else 1
        arrived(ring[u, slot, h])
        for dst, more in zip(half(blk, u, h), buffer(u, h, slot)):
            add_in(dst, more)
        ring[u, slot, 2 + h] = pair(blk, buffer(u, 2 + h, slot), nb[axis, way])

    def own_block(u, slot, blk):
        arrived(ring[u, slot, 2])
        arrived(ring[u, slot, 3])
        for dst, one, two in zip(blk, buffer(u, 2, slot), buffer(u, 3, slot)):
            add_in(dst, one, two)

    for i in range(4):
        for u in (0, 1):
            far_block(u, i, ready(u, i), second_axis[u])
    for i in range(4):
        for u in (0, 1):
            near_block(u, i, ready(u, 4 + i), second_axis[u], 1)
        for u in (0, 1):
            near_block(u, i, ready(u, 8 + i), second_axis[u], -1)
    for i in range(4):
        for u in (0, 1):
            blk = ready(u, 12 + i)
            own_block(u, i, blk)
            if i == 0:
                far_block(u, 4, blk, first_axis[u])
            if i == 1:
                near_block(u, 4, blk, first_axis[u], 1)
            if i == 2:
                near_block(u, 4, blk, first_axis[u], -1)
    for u in (0, 1):
        blk = at(hold[u], *orders[u][15])
        own_block(u, 4, blk)
        s, w, w0, s2, v, v0 = UNITS[u]
        fin[:, s * 128 : (s + w) * 128] = blk[0][...]
        fsd[:, s2 * 128 : (s2 + v) * 128] = blk[1][...]
    r = mul((1 - lo) * 32, 16)
    arrived(pair((fin.at[pl.ds(r, 48)], fsd.at[pl.ds(r, 32)]), (wx, wxd), xn))
    r = mul(lo * 32, 16)
    snd[...] = (fin[pl.ds(r, 48), :].astype(F32) + wx[...].astype(F32)).astype(BF16)
    sndd[...] = (fsd[pl.ds(r, 32), :].astype(F32) + wxd[...].astype(F32)).astype(BF16)
    arrived(pair((snd, sndd), (wh, whd), hn))
    acc[...] = snd[...].astype(F32) + wh[...].astype(F32)
    accd[...] = sndd[...].astype(F32) + whd[...].astype(F32)
    mine = pl.ds(mul(c * HALF, 128), HALF)
    mine2 = pl.ds(mul(c * 640, 128), 640)
    r = mul((1 - c) * 16, 16)
    last = pair((acc.at[pl.ds(r, 32)], accd.at[pl.ds(r, 16)]), (out.at[:, mine], osd.at[:, mine2]), sib)
    r = mul(c * 16, 16)
    out[:, mine] = acc[pl.ds(r, 32), :]
    osd[:, mine2] = accd[pl.ds(r, 16), :]
    arrived(last)
    wires.finish()


def scatter_sums(gw, gsd):
    scratch = []
    for _ in (0, 1):
        for s, w, w0, s2, v, v0 in UNITS:
            scratch += [pltpu.VMEM((4, 4, 80, w * 128), BF16), pltpu.VMEM((4, 4, 64, v * 128), BF16)]
    for s, w, w0, s2, v, v0 in UNITS:
        for rows, n, n0 in ((80, w, w0), (64, v, v0)):
            for tiles in (n0, n - n0, n, n):
                scratch.append(pltpu.VMEM((5, rows, tiles * 128), BF16))
    for rows, rows2 in ((80, 64), (48, 32), (48, 32), (48, 32)):
        scratch += [pltpu.VMEM((rows, HALF), BF16), pltpu.VMEM((rows2, 640), BF16)]
    scratch += [pltpu.VMEM((48, HALF), F32), pltpu.VMEM((32, 640), F32)]
    sems = 64 + 2 * 2 * 4 * 5 + 6
    scratch += [
        pltpu.SemaphoreType.DMA((sems,)),
        pltpu.SemaphoreType.DMA((sems,)),
        pltpu.SemaphoreType.DMA((64,)),
    ]
    out, osd = pl.pallas_call(
        scatter_kernel,
        out_shape=(jax.ShapeDtypeStruct((32, WIDE * 128), F32), jax.ShapeDtypeStruct((16, 1280), F32)),
        in_specs=[pl.BlockSpec(memory_space=pl.ANY)] * 2,
        out_specs=(pl.BlockSpec(memory_space=pltpu.VMEM),) * 2,
        scratch_shapes=scratch,
        compiler_params=pltpu.CompilerParams(
            collective_id=2, has_side_effects=True, vmem_limit_bytes=56 << 20
        ),
        name="scatter_sums",
    )(gw.reshape(4, 4, 80, WIDE * 128), gsd.reshape(4, 4, 64, 1280))
    offset = 4 * lax.rem(lax.axis_index("exp"), 4)
    return lax.dynamic_slice(out, (offset, 0), (20, WIDE * 128)), osd[:14]


PART_AXES = (("y", "z", "g"), ("z", "g", "y"), ("g", "y", "z"))


def exchange_kernel(cuts, *refs):
    n = len(cuts)
    stages = [refs[0:n], refs[2 * n : 3 * n], refs[3 * n : 4 * n], refs[n : 2 * n]]
    hi, y, z, lo, c = place()
    me = {"y": y, "z": z, "g": lo * 2 + c}
    wires = Sender(*refs[4 * n :])

    def peer(axis, k):
        q = dict(me)
        q[axis] = lax.rem(me[axis] + k, 4)
        return q[axis], device(hi, q["y"], q["z"], q["g"] // 2, lax.rem(q["g"], 2))

    greet([peer(axis, k)[1] for axis in "yzg" for k in (1, 2, 3)])
    every = slice(None)

    def view(ref, axis, v, lanes):
        index = {"y": (v, every, every), "z": (every, v, every), "g": (every, every, v)}[axis]
        return ref.at[index + (every, pl.ds(lanes[0] * 128, lanes[1] * 128))]

    pending = {}

    def go(part, phase):
        axis = PART_AXES[part][phase]
        waits = []
        for a in range(n):
            src, dst = stages[phase][a], stages[phase + 1][a]
            lanes = cuts[a][part]
            own = view(dst, axis, me[axis], lanes)
            for k in (2, 1, 3):
                v, to = peer(axis, k)
                waits.append(wires.remote(view(src, axis, v, lanes), own, to).wait_recv)
            waits.append(wires.local(view(src, axis, me[axis], lanes), own).wait)
        pending[part, phase] = waits

    for part in range(3):
        go(part, 0)
    for phase in (1, 2):
        for part in range(3):
            for wait in pending[part, phase - 1]:
                wait()
            go(part, phase)
    for part in range(3):
        for wait in pending[part, 2]:
            wait()
    wires.finish()


def exchange(collective_id, arrays, cuts):
    n = len(arrays)
    split = [a.reshape((4, 4, 4) + a.shape[1:]) for a in arrays]
    shapes = [jax.ShapeDtypeStruct(a.shape, a.dtype) for a in split]
    out = pl.pallas_call(
        functools.partial(exchange_kernel, cuts),
        out_shape=tuple(shapes),
        in_specs=[pl.BlockSpec(memory_space=pl.ANY)] * n,
        out_specs=(pl.BlockSpec(memory_space=pl.ANY),) * n,
        scratch_shapes=[pltpu.VMEM(s.shape, s.dtype) for s in shapes] * 2
        + [
            pltpu.SemaphoreType.DMA((27 * n,)),
            pltpu.SemaphoreType.DMA((27 * n,)),
            pltpu.SemaphoreType.DMA((9 * n,)),
        ],
        compiler_params=pltpu.CompilerParams(
            collective_id=collective_id, has_side_effects=True, vmem_limit_bytes=40 << 20
        ),
        name="exchange_rows",
    )(*split)
    return [o.reshape(a.shape) for o, a in zip(out, arrays)]


def weight_grad_kernel(left, right, out):
    out[...] = lax.dot_general(
        left[0], right[...], (((0,), (0,)), ((), ())), preferred_element_type=F32
    ).astype(BF16)


def weight_grads(left, right):
    rows = left.shape[1]
    wide = 256
    return pl.pallas_call(
        weight_grad_kernel,
        grid=(WIDE * 128 // wide,),
        out_shape=jax.ShapeDtypeStruct((left.shape[2], WIDE * 128), BF16),
        in_specs=[
            pl.BlockSpec(
                (1, rows, left.shape[2]),
                lambda i: (jnp.where(i < 15, 0, jnp.where(i < 20, 1, 2)), 0, 0),
            ),
            pl.BlockSpec((rows, wide), lambda i: (0, i)),
        ],
        out_specs=pl.BlockSpec((left.shape[2], wide), lambda i: (0, i)),
        compiler_params=pltpu.CompilerParams(vmem_limit_bytes=32 << 20),
        name="weight_grads",
    )(left, right)


def rms_forward(values, gain_vec):
    inv_rms = lax.rsqrt(jnp.mean(values * values, axis=-1, keepdims=True) + EPSILON)
    return (values * inv_rms * gain_vec, inv_rms)


def rms_backward(values, inv_rms, gain_vec, upstream):
    weighted = upstream * gain_vec
    inner = jnp.mean(weighted * values, axis=-1, keepdims=True)
    grad_in = inv_rms * weighted - values * (inv_rms * inv_rms * inv_rms) * inner
    grad_gain = jnp.sum(upstream * values * inv_rms, axis=0)
    return (grad_in, grad_gain)


def rotary_tables(positions, head_width):
    half_width = head_width // 2
    freq = jnp.power(10000.0, -2.0 * jnp.arange(half_width, dtype=F32) / head_width)
    angles = positions.astype(F32)[:, None] * freq[None, :]
    return (jnp.cos(angles)[:, None, :], jnp.sin(angles)[:, None, :])


def rotate(values, cosine, sine):
    half_width = values.shape[-1] // 2
    first = values[..., :half_width]
    second = values[..., half_width:]
    return jnp.concatenate([first * cosine - second * sine, second * cosine + first * sine], axis=-1)


def unrotate(values, cosine, sine):
    return rotate(values, cosine, -sine)


def silu_parts(pre_act):
    sigma = jax.nn.sigmoid(pre_act)
    return (pre_act * sigma, sigma * (1.0 + pre_act * (1.0 - sigma)))


def dot(a, b):
    return jnp.dot(a, b, preferred_element_type=F32)


def dot_t(a, b):
    return lax.dot_general(a, b, (((1,), (1,)), ((), ())), preferred_element_type=F32)


def t_dot(a, b):
    return lax.dot_general(a, b, (((0,), (0,)), ((), ())), preferred_element_type=F32)


def score_block(queries, keys_all, allowed, inv_root):
    scores = jnp.einsum("thd,shd->hts", queries, keys_all, preferred_element_type=F32) * inv_root
    return jnp.where(allowed[None], scores, NEG_BIG)


def per_device(
    tokens,
    cotangent,
    segments,
    routes,
    norm_gain_attn,
    w_query,
    w_key,
    w_value,
    w_out,
    norm_gain_ffn,
    w_router,
    shared_gate,
    shared_up,
    shared_down,
    expert_gate,
    expert_up,
    expert_down,
):
    tok_rows = tokens.shape[1]
    width = tokens.shape[2]
    head_width = width // HEADS
    experts = w_router.shape[1]
    top_count = routes.shape[2]
    slots = tok_rows * top_count * 5 // (experts * 4)
    even = slots - 1

    def spread(w):
        w = w.reshape(w.shape[0], experts, w.shape[1] // experts)
        return jnp.pad(w, ((0, 0), (0, 0), (0, 2))).reshape(w.shape[0], experts * 16)

    shard = jnp.concatenate(
        [
            w_query,
            w_key,
            w_value,
            w_out,
            spread(shared_gate),
            spread(shared_up),
            w_router,
            norm_gain_attn[:, None],
            norm_gain_ffn[:, None],
            jnp.zeros((w_query.shape[0], 190), BF16),
        ],
        axis=1,
    )
    weights, sdown_w = gather_weights(shard, shared_down)
    qkv_w = weights[:, :3840]
    out_w = weights[:, 3840:5120]
    sgu_w = weights[:, 5120:7168]
    router_w = weights[:, 7168 : 7168 + experts]
    gain_attn = weights[:, 7168 + experts].astype(F32)
    gain_ffn = weights[:, 7169 + experts].astype(F32)

    route_rows = routes[0]
    picked = route_rows[:, :, None] == jnp.arange(experts, dtype=jnp.int32)[None, None, :]
    member = jnp.any(picked, axis=1)
    before = jnp.arange(tok_rows)[None, :] < jnp.arange(tok_rows)[:, None]
    rank = dot(before.astype(BF16), member.astype(BF16)).astype(jnp.int32)
    slot_of = jnp.where(member, rank, -1).T
    place_even = slot_of[:, None, :] == jnp.arange(even, dtype=jnp.int32)[None, :, None]
    place_last = slot_of == even
    even_hot = place_even.astype(BF16).reshape(experts * even, tok_rows)
    last_hot = place_last.astype(BF16)

    inv_root = head_width ** (-0.5)
    seq_place = lax.axis_index("seq")
    inputs = tokens[0].astype(F32)
    positions = seq_place * tok_rows + jnp.arange(tok_rows, dtype=jnp.int32)
    cosine, sine = rotary_tables(positions, head_width)
    seg_row = segments[0]
    own_seg = lax.dynamic_slice_in_dim(seg_row, seq_place * tok_rows, tok_rows)
    prior_seg = lax.dynamic_slice_in_dim(seg_row, jnp.maximum(seq_place - 1, 0) * tok_rows, tok_rows)
    key_places = jnp.concatenate([positions - tok_rows, positions])
    key_segs = jnp.concatenate([prior_seg, own_seg])
    allowed = (
        (key_places[None, :] <= positions[:, None])
        & (key_places[None, :] >= 0)
        & (key_segs[None, :] == own_seg[:, None])
    )
    normed_attn, inv_attn = rms_forward(inputs, gain_attn)
    act_attn = normed_attn.astype(BF16)
    qkv = dot(act_attn, qkv_w)
    heads = lambda v: v.reshape(tok_rows, HEADS, head_width)
    queries = rotate(heads(qkv[:, :width]), cosine, sine).astype(BF16)
    keys_own = rotate(heads(qkv[:, width : 2 * width]), cosine, sine).astype(BF16)
    values_own = heads(qkv[:, 2 * width :].astype(BF16))
    prior = lax.ppermute(jnp.stack([keys_own, values_own]), "seq", [(0, 1)])
    keys_all = jnp.concatenate([prior[0], keys_own], axis=0)
    values_all = jnp.concatenate([prior[1], values_own], axis=0)
    scores = score_block(queries, keys_all, allowed, inv_root)
    top_score = jnp.max(scores, axis=-1, keepdims=True)
    expo = jnp.exp(scores - top_score)
    probs = expo / jnp.sum(expo, axis=-1, keepdims=True)
    probs_low = probs.astype(BF16)
    mixed = (
        jnp.einsum("hts,shd->thd", probs_low, values_all, preferred_element_type=F32)
        .reshape(tok_rows, width)
        .astype(BF16)
    )
    hidden_one = inputs + dot(mixed, out_w)
    normed_ffn, inv_ffn = rms_forward(hidden_one, gain_ffn)
    act_ffn = normed_ffn.astype(BF16)
    logits = jnp.where(member, dot(act_ffn, router_w), NEG_BIG)
    gate_expo = jnp.where(member, jnp.exp(logits - jnp.max(logits, axis=-1, keepdims=True)), 0.0)
    gates = gate_expo / jnp.sum(gate_expo, axis=-1, keepdims=True)

    grad_low = cotangent[0]
    gates_t = gates.T
    slot_gates = jnp.concatenate(
        [
            jnp.sum(jnp.where(place_even, gates_t[:, None, :], 0.0), axis=-1),
            jnp.sum(jnp.where(place_last, gates_t, 0.0), axis=-1, keepdims=True),
        ],
        axis=1,
    )
    both = jnp.concatenate([act_ffn, grad_low], axis=1)
    even_rows = dot(even_hot, both).astype(BF16).reshape(experts, even, 2 * width)
    last_rows = jnp.concatenate(
        [dot(last_hot, both), jnp.pad(slot_gates, ((0, 0), (0, 128 - slots)))], axis=1
    )
    rows_x, rows_g, rows_l = exchange(
        3,
        (even_rows[:, :, :width], even_rows[:, :, width:], last_rows[:, None, :]),
        (((0, 4), (4, 3), (7, 3)), ((0, 3), (3, 4), (7, 3)), ((0, 6), (6, 6), (12, 9))),
    )
    rows_l = rows_l[:, 0]
    arrived_x = jnp.concatenate([rows_x.reshape(-1, width), rows_l[:, :width].astype(BF16)])
    arrived_g = jnp.concatenate([rows_g.reshape(-1, width), rows_l[:, width : 2 * width].astype(BF16)])
    row_gates = jnp.concatenate(
        [rows_l[:, 2 * width : 2 * width + even].reshape(-1), rows_l[:, 2 * width + even]]
    )

    gate_local, up_local, down_local = expert_gate[0], expert_up[0], expert_down[0]
    gate_e = dot(arrived_x, gate_local)
    up_e = dot(arrived_x, up_local)
    silu_e, slope_e = silu_parts(gate_e)
    hidden_e = (silu_e * up_e).astype(BF16)
    result = dot(hidden_e, down_local).astype(BF16)
    grad_result = (row_gates[:, None] * arrived_g.astype(F32)).astype(BF16)
    grad_hidden_e = dot_t(grad_result, down_local)
    grad_gate_e = (grad_hidden_e * up_e * slope_e).astype(BF16)
    grad_up_e = (grad_hidden_e * silu_e).astype(BF16)
    part_expert = (
        t_dot(arrived_x, grad_gate_e).astype(BF16),
        t_dot(arrived_x, grad_up_e).astype(BF16),
        t_dot(hidden_e, grad_result).astype(BF16),
    )
    grad_arrived = (dot_t(grad_gate_e, gate_local) + dot_t(grad_up_e, up_local)).astype(BF16)
    swapped = [lax.ppermute(g, "seq", [(0, 1), (1, 0)]) for g in part_expert]
    rows_out = experts * even
    back = exchange(
        4,
        (
            result[:rows_out].reshape(experts, even, width),
            grad_arrived[:rows_out].reshape(experts, even, width),
            jnp.concatenate([result[rows_out:], grad_arrived[rows_out:]], axis=1).astype(F32)[:, None, :],
        ),
        (((0, 4), (4, 3), (7, 3)), ((0, 3), (3, 4), (7, 3)), ((0, 6), (6, 6), (12, 8))),
    )
    back_out, back_grad = back[0].reshape(-1, width), back[1].reshape(-1, width)
    back_last = back[2][:, 0].astype(BF16)

    gate_s = dot(act_ffn, sgu_w[:, :1024])
    up_s = dot(act_ffn, sgu_w[:, 1024:])
    silu_s, slope_s = silu_parts(gate_s)
    hidden_s = (silu_s * up_s).astype(BF16)
    out_s = dot(hidden_s, sdown_w)
    grad_hidden_s = dot_t(grad_low, sdown_w)
    grad_gate_s = (grad_hidden_s * up_s * slope_s).astype(BF16)
    grad_up_s = (grad_hidden_s * silu_s).astype(BF16)
    grad_shared_down = t_dot(hidden_s, grad_low).astype(BF16)

    weight_even = jnp.where(place_even, gates_t[:, None, :], 0.0).reshape(rows_out, tok_rows)
    weight_last = jnp.where(place_last, gates_t, 0.0)

    def weighted(w, rows):
        top = lax.reduce_precision(w, 8, 7)
        mid = lax.reduce_precision(w - top, 8, 7)
        low = (w - top) - mid
        three = jnp.concatenate([top, mid, low], axis=1).astype(BF16)
        s = t_dot(three, rows)
        return s[:tok_rows] + s[tok_rows : 2 * tok_rows] + s[2 * tok_rows :]

    routed = weighted(weight_even, back_out) + weighted(weight_last, back_last[:, :width])
    layer_out = (hidden_one + out_s + routed).astype(BF16)

    grad_final = grad_low.astype(F32)
    dots_even = dot_t(back_out, grad_low).reshape(experts, even, tok_rows)
    dots_last = dot_t(back_last[:, :width], grad_low)
    grad_gates = (
        jnp.sum(jnp.where(place_even, dots_even, 0.0), axis=1) + jnp.where(place_last, dots_last, 0.0)
    ).T
    grad_logits = (gates * (grad_gates - jnp.sum(gates * grad_gates, axis=-1, keepdims=True))).astype(BF16)
    grad_routed = t_dot(even_hot, back_grad) + t_dot(last_hot, back_last[:, width:])
    grad_gu_s = jnp.concatenate([grad_gate_s, grad_up_s], axis=1)
    grad_act_ffn = grad_routed + dot_t(grad_logits, router_w) + dot_t(grad_gu_s, sgu_w)
    grad_norm_f, grad_gain_ffn = rms_backward(hidden_one, inv_ffn, gain_ffn, grad_act_ffn)
    grad_hidden_one = grad_final + grad_norm_f
    grad_attn_low = grad_hidden_one.astype(BF16)
    grad_mixed = heads(dot_t(grad_attn_low, out_w).astype(BF16))

    grad_probs = jnp.einsum("thd,shd->hts", grad_mixed, values_all, preferred_element_type=F32)
    inner = jnp.sum(probs * grad_probs, axis=-1, keepdims=True)
    grad_scores = (probs * (grad_probs - inner)).astype(BF16)
    grad_values_all = jnp.einsum("hts,thd->shd", probs_low, grad_mixed, preferred_element_type=F32)
    grad_query_rot = jnp.einsum("hts,shd->thd", grad_scores, keys_all, preferred_element_type=F32) * inv_root
    grad_keys_all = jnp.einsum("hts,thd->shd", grad_scores, queries, preferred_element_type=F32) * inv_root
    later = lax.ppermute(
        jnp.stack([grad_keys_all[:tok_rows], grad_values_all[:tok_rows]]).astype(BF16), "seq", [(1, 0)]
    ).astype(F32)
    grad_key_rot = grad_keys_all[tok_rows:] + later[0]
    grad_value = (grad_values_all[tok_rows:] + later[1]).astype(BF16).reshape(tok_rows, width)
    grad_query = unrotate(grad_query_rot, cosine, sine).astype(BF16).reshape(tok_rows, width)
    grad_key = unrotate(grad_key_rot, cosine, sine).astype(BF16).reshape(tok_rows, width)
    grad_qkv = jnp.concatenate([grad_query, grad_key, grad_value], axis=1)
    grad_act_attn = dot_t(grad_qkv, qkv_w)
    grad_norm_a, grad_gain_attn = rms_backward(inputs, inv_attn, gain_attn, grad_act_attn)
    grad_tokens = grad_hidden_one + grad_norm_a

    right = jnp.concatenate(
        [grad_qkv, grad_attn_low, grad_gu_s, grad_logits, jnp.zeros((tok_rows, 256 - experts), BF16)], axis=1
    )
    grads = weight_grads(jnp.stack([act_attn, mixed, act_ffn]), right)
    gains = jnp.stack([grad_gain_attn, grad_gain_ffn], axis=1).astype(BF16)
    grads = lax.dynamic_update_slice(grads, gains, (0, 7168 + experts))
    own, own_down = scatter_sums(grads, grad_shared_down)

    def gathered_hidden(w):
        return w.reshape(w.shape[0], experts, 16)[:, :, :14].reshape(w.shape[0], experts * 14)

    expert_grads = [
        (a.astype(F32) + b.astype(F32))[None] for a, b in zip(part_expert, swapped)
    ]
    return (
        layer_out[None],
        grad_tokens[None],
        own[:, 7168 + experts],
        own[:, :1280],
        own[:, 1280:2560],
        own[:, 2560:3840],
        own[:, 3840:5120],
        own[:, 7169 + experts],
        own[:, 7168 : 7168 + experts],
        gathered_hidden(own[:, 5120:6144]),
        gathered_hidden(own[:, 6144:7168]),
        own_down,
        *expert_grads,
    )


def solution(mesh):
    rows = P("exp", None)
    deep = P("exp", None, None)
    split = P("exp", "seq", None)
    gain = P("exp")
    in_specs = (split, split, rows, split, gain, rows, rows, rows, rows, gain) + (rows,) * 4 + (deep,) * 3
    out_specs = (split, split, gain, rows, rows, rows, rows, gain) + (rows,) * 4 + (deep,) * 3
    return jax.shard_map(per_device, mesh=mesh, in_specs=in_specs, out_specs=out_specs, check_vma=False)
```

time: 2190 us -> 651 us (0.30)
  blocking collectives: 987 us -> 0 us
  waiting for transfers between devices: 644 us -> 7.75 us
  Pallas kernels: 0 us -> 377 us
  starting transfers between devices: 190 us -> 15.1 us
  local copies, waits for them, and re-layouts: 163 us -> 91.1 us
    unnamed x3 -> x0, blocking collectives: 869 us -> none
    all_gather x7 -> x0, waiting for transfers between devices: 404 us -> none  [the longest x1 101 us: per_device(): lax.all_gather(shared_down, 'exp', axis=0, tiled=True)]
    pallas_call x0 -> x5, Pallas kernels: none -> 377 us  [the longest x2 151 us: exchange(): pl.pallas_call(functools.partial(exchange_kernel, cuts), out_shape=tuple(...]
    psum x2 -> x0, waiting for transfers between devices: 182 us -> none  [the longest x1 164 us: per_device(): lax.psum(grad_expert_gate.astype(jnp.bfloat16), 'seq').astype(jnp.float32)]
    unnamed x52 -> x0, starting transfers between devices: 150 us -> none
    all_gather x1 -> x0, blocking collectives: 118 us -> none  [per_device(): lax.all_gather(w_router, 'exp', axis=0, tiled=True)]
    all_to_all x4 -> x0, waiting for transfers between devices: 45.8 us -> none  [the longest x1 28.8 us: per_device(): lax.all_to_all(result, 'exp', split_axis=0, concat_axis=0, tiled=True)]
    unnamed x213 -> x197, local copies, waits for them, and re-layouts: 76.5 us -> 31.9 us
  transfers between devices with their start and end apart: 69 -> 5, of which waited for: 11 -> 2; matrix products, arithmetic and copies ran while one was open for 12% -> 9% of each run, Pallas kernels for 0% -> 22%
where the time goes in v1:
time: 651 us; the launch traced here: 642 us
  Pallas kernels  377 us (58%)
  matrix products  107 us (16%)
  local copies, waits for them, and re-layouts  91.1 us (14%)
  other arithmetic  42.2 us (6%)
  starting transfers between devices  15.1 us (2%)
  waiting for transfers between devices  7.75 us (1%)
    pallas_call x2, Pallas kernels, exchange(): pl.pallas_call(functools.partial(exchange_kernel, cuts), out_shape=tuple(...  151 us
    pallas_call x1, Pallas kernels, scatter_sums(): pl.pallas_call(scatter_kernel, out_shape=(jax.ShapeDtypeStruct((32, WIDE...  129 us
    pallas_call x1, Pallas kernels, gather_weights(): pl.pallas_call(gather_kernel, out_shape=(jax.ShapeDtypeStruct((4, 4, 80,...  84.9 us
    dot_general x10, matrix products, dot_t(): lax.dot_general(a, b, (((1,), (1,)), ((), ())), preferred_element_type=F32)  38.1 us
    dot_general x12, matrix products, dot(): return jnp.dot(a, b, preferred_element_type=F32)  36.4 us
    unnamed x197, local copies, waits for them, and re-layouts  31.9 us
    dot_general x8, matrix products, t_dot(): lax.dot_general(a, b, (((0,), (0,)), ((), ())), preferred_element_type=F32)  21.3 us
    broadcast_in_dim x3, other arithmetic, per_device(): (a.astype(F32) + b.astype(F32))[None]  13.1 us
  transfers between devices with their start and end apart: 5, of which 2 were waited for; matrix products, arithmetic and copies ran while one was open for 9% of the time, Pallas kernels for 22%

profile of v1, /device:TPU:1, one launch (start us, length us, event | category | flops | bytes accessed | tf_op | source)
XLA Modules:
  0.0 642.4 jit_solution(2801034127522128257)
XLA Ops:
  6.9 2.1 dynamic_update_slice.6.win
  9.0 84.9 %gather_weights.1 = (bf16[4,4,80,7424]{3,2,1,0:T(8,128)(2,1)}, bf16[4,4,64,1280]{3,2,1,0:T(8,128)(2,1)S(1)}) custom-call(bf16[32,7424]{1,0:T(8,128)(2,1)S(1)} %dynamic_update_slice.6.win, bf16[16,1280]{1,0:T(8,128)(2,1)S(1)} %pad.17.sdw), custom_call_target="tpu_custom_call" | custom-call | tf_op jit(solution)/shard_map/gather_weights/pallas_call | solution.py:225
  95.4 2.0 fusion.140
  98.3 5.3 fusion.3
  107.4 2.2 copy.283
  111.5 2.0 copy.350
  113.6 2.0 copy.349
  120.9 3.0 subtract_convert_fusion.2
  125.0 5.7 collective-permute-start
  132.1 3.5 convolution_bitcast_fusion.1
  136.7 7.1 %collective-permute-done = bf16[2,128,10,128]{3,1,2,0:T(8,128)(2,1)} collective-permute-done((bf16[2,128,10,128]{3,1,2,0:T(8,128)(2,1)}, bf16[2,128,10,128]{3,1,2,0:T(8,128)(2,1)}, u32[]{:S(2)}, u32[]{:S(2)}) %collective-permute-start) | collective-permute-done | bytes 655392 | tf_op jit(solution)/shard_map/ppermute | solution.py:650
  143.9 2.0 slice_bitcast_fusion.2
  145.9 3.1 fusion.148
  149.0 2.6 convolution_convert_fusion.6
  151.6 2.8 multiply_reduce_fusion.3
  155.1 3.2 fusion.13
  164.4 2.8 fusion.141
  175.1 76.1 %exchange_rows.2 = (bf16[4,4,4,16,1280]{4,3,2,1,0:T(8,128)(2,1)S(1)}, bf16[4,4,4,16,1280]{4,3,2,1,0:T(8,128)(2,1)S(1)}, f32[4,4,4,1,2688]{4,3,2,1,0:T(1,128)S(1)}) custom-call(bf16[4,4,4,16,1280]{4,3,2,1,0:T(8,128)(2,1)S(1)} %bitcast.225, bf16[4,4,4,16,1280]{4,3,2,1,0:T(8,128)(2,1)S(1)} %bitcast.224, f32[4,4,4,1,2688]{4,3,2,1,0:T(1,128)S(1)} %reshape_broadcast_in_dim.4.refs_2_), custom_call_target="tpu_custom_call" | custom-call | tf_op jit(solution)/shard_map/exchange_rows/pallas_call | solution.py:465
  255.1 3.7 reduce.2
  261.6 7.6 %fusion.35 = f32[1088,896]{1,0:T(8,128)} fusion(bf16[1,1280,896]{2,1,0:T(8,128)(2,1)} %param.31, bf16[64,1280]{1,0:T(8,128)(2,1)S(1)} %get-tuple-element.82, bf16[1024,1280]{1,0:T(8,128)(2,1)} %bitcast.233), kind=kOutput, calls=%fused_computation.50 | convolution fusion | flops 2501181440 | bytes 8978432 | tf_op jit(solution)/shard_map/dot_general | solution.py:547
  269.2 5.0 fusion.31
  274.4 7.7 %multiply_convert_fusion.1 = (bf16[1088,896]{1,0:T(8,128)(2,1)S(1)}, bf16[1088,896]{1,0:T(8,128)(2,1)S(1)}, bf16[1088,896]{1,0:T(8,128)(2,1)S(1)}) fusion(f32[1088,896]{1,0:T(8,128)} %fusion.35, f32[1088,896]{1,0:T(8,128)} %fusion.31, bf16[1,896,1280]{2,1,0:T(8,128)(2,1)S(1)} %copy-done, bf16[64,1280]{1,0:T(8,128)(2,1)S(1)} %get-tuple-element.81, ...), kind=kOutput, calls=%fused_computation.15 | convolution fusion | flops 2518589440 | bytes 18731264 | tf_op jit(solution)/shard_map/dot_general | solution.py:551
  282.1 3.1 fusion.33
  285.2 3.6 fusion.5
  291.2 3.2 convolution_convert_fusion
  300.0 4.8 convolution_convert_fusion.5
  304.8 4.9 convolution_convert_fusion.4
  309.6 4.7 convolution_convert_fusion.3
  318.7 74.6 %exchange_rows.3 = (bf16[4,4,4,16,1280]{4,3,2,1,0:T(8,128)(2,1)S(1)}, bf16[4,4,4,16,1280]{4,3,2,1,0:T(8,128)(2,1)S(1)}, f32[4,4,4,1,2560]{4,3,2,1,0:T(1,128)S(1)}) custom-call(bf16[4,4,4,16,1280]{4,3,2,1,0:T(8,128)(2,1)S(1)} %bitcast.227, bf16[4,4,4,16,1280]{4,3,2,1,0:T(8,128)(2,1)S(1)} %bitcast.226, f32[4,4,4,1,2560]{4,3,2,1,0:T(1,128)S(1)} %maximum_convert_fusion.refs_2_), custom_call_target="tpu_custom_call" | custom-call | tf_op jit(solution)/shard_map/exchange_rows/pallas_call | solution.py:465
  398.2 2.6 fusion.42
  401.0 3.2 multiply_convert_fusion.7
  404.2 4.6 fusion.6
  412.7 3.3 fusion.23
  416.9 3.3 convolution_bitcast_fusion
  427.7 5.1 collective-permute-start.2
  432.8 3.1 collective-permute-start.4
  437.6 3.3 fusion.55
  441.6 2.4 convolution_convert_fusion.2
  451.4 8.0 %fusion.70 = (bf16[1280]{0:T(1024)(128)(2,1)S(1)}, f32[128]{0:T(128)S(1)}, f32[128,1280]{1,0:T(8,128)}) fusion(bf16[1,128,1280]{2,1,0:T(8,128)(2,1)S(1)} %copy-done.24, f32[128]{0:T(128)S(1)} %copy-done.81, f32[1280]{0:T(1024)S(1)} %convert_reduce_fusion.2, bf16[1280,7424]{1,0:T(8,128)(2,1)} %bitcast.266, bf16[128,1280]{0,1:T(8,128)(2,1)S(1)} %bitcast.249, ...), kind=kOutput, calls=%fused_computation.104 | convolution fusion | flops 1262385792 | bytes 11805184 | tf_op jit(solution)/shard_map/dot_general | solution.py:551
  463.1 2.6 concatenate.124.right
  465.7 11.9 %weight_grads.1 = bf16[1280,7424]{1,0:T(8,128)(2,1)S(1)} custom-call(bf16[3,128,1280]{2,1,0:T(8,128)(2,1)S(1)} %pad_maximum_fusion.1.left, bf16[128,7424]{1,0:T(8,128)(2,1)S(1)} %concatenate.124.right), custom_call_target="tpu_custom_call" | custom-call | tf_op jit(solution)/shard_map/weight_grads/pallas_call | solution.py:493
  477.7 6.4 %copy-done.2 = bf16[1280,7424]{1,0:T(8,128)(2,1)} copy-done((bf16[1280,7424]{1,0:T(8,128)(2,1)}, bf16[1280,7424]{1,0:T(8,128)(2,1)S(1)}, u32[]{:S(2)}) %copy-start.2) | copy-done | bytes 19005464
  484.1 5.3 dynamic_update_slice.7
  489.3 129.2 %scatter_sums.1 = (f32[32,7424]{1,0:T(8,128)}, f32[16,1280]{1,0:T(8,128)}) custom-call(bf16[4,4,80,7424]{3,2,1,0:T(8,128)(2,1)} %bitcast.221, bf16[4,4,64,1280]{3,2,1,0:T(8,128)(2,1)} %bitcast.238), custom_call_target="tpu_custom_call" | custom-call | tf_op jit(solution)/shard_map/scatter_sums/pallas_call | solution.py:396
  625.2 2.0 fusion.144
  628.4 4.4 add_bitcast_fusion.2
  632.8 4.4 add_bitcast_fusion.1
  637.2 4.3 add_bitcast_fusion
  (321 shorter events, 95.4 us)
Async XLA Ops:
  0.6 273.7 %copy-start = (bf16[1,896,1280]{2,1,0:T(8,128)(2,1)S(1)}, bf16[1,896,1280]{2,1,0:T(8,128)(2,1)}, u32[]{:S(2)}) copy-start(bf16[1,896,1280]{2,1,0:T(8,128)(2,1)} %param.33) | copy-start | bytes 6881284
  0.7 5.1 copy-start.67
  4.3 93.4 %copy-start.22 = (bf16[1,128,1280]{2,1,0:T(8,128)(2,1)S(1)}, bf16[1,128,1280]{2,1,0:T(8,128)(2,1)}, u32[]{:S(2)}) copy-start(bf16[1,128,1280]{2,1,0:T(8,128)(2,1)} %param.17) | copy-start | bytes 983044
  98.3 37.5 %copy-start.80 = (f32[128]{0:T(128)}, f32[128]{0:T(128)S(1)}, u32[]{:S(2)}) copy-start(f32[128]{0:T(128)S(1)} %get-tuple-element.99) | copy-start | bytes 1540
  120.9 10.7 %copy-start.42 = (bf16[1280,1]{1,0:T(8,128)(2,1)S(1)}, bf16[1280,1]{1,0:T(8,128)(2,1)}, u32[]{:S(2)}) copy-start(bf16[1280,1]{1,0:T(8,128)(2,1)} %get-tuple-element.47) | copy-start | bytes 7684
  120.9 11.0 %copy-start.79 = (s32[1,128,7]{1,0,2:T(1,128)S(1)}, s32[1,128,7]{1,0,2:T(1,128)}, u32[]{:S(2)}) copy-start(s32[1,128,7]{1,0,2:T(1,128)} %param.20) | copy-start | bytes 10756
  120.9 11.2 %copy-start.84 = (s32[1,256]{1,0:T(1,128)S(1)}, s32[1,256]{1,0:T(1,128)}, u32[]{:S(2)}) copy-start(s32[1,256]{1,0:T(1,128)} %param.19) | copy-start | bytes 3076
  120.9 11.2 %copy-start.20 = (bf16[1,128,1280]{2,1,0:T(8,128)(2,1)S(1)}, bf16[1,128,1280]{2,1,0:T(8,128)(2,1)}, u32[]{:S(2)}) copy-start(bf16[1,128,1280]{2,1,0:T(8,128)(2,1)} %param.18) | copy-start | bytes 983044
  125.0 18.9 %collective-permute-start = (bf16[2,128,10,128]{3,1,2,0:T(8,128)(2,1)}, bf16[2,128,10,128]{3,1,2,0:T(8,128)(2,1)}, u32[]{:S(2)}, u32[]{:S(2)}) collective-permute-start(bf16[2,128,10,128]{3,1,2,0:T(8,128)(2,1)} %pad_maximum_fusion.3), channel_id=1, source_target_pairs={{0,64},{1,65},{2,66},{3,67},{4,68},{5,69},{6,70},{7,71},{8,72},{9,... | collective-permute-start | bytes 1966088 | tf_op jit(solution)/shard_map/ppermute | solution.py:650
  131.9 30.7 %copy-start.68 = (s32[1024]{0:T(1024)}, s32[1024]{0:T(1024)S(1)}, u32[]{:S(2)}) copy-start(s32[1024]{0:T(1024)S(1)} %eq.87) | copy-start | bytes 12292
  132.1 13.7 %copy-start.44 = (bf16[128,10,64]{2,0,1:T(8,128)(2,1)S(1)}, bf16[128,10,64]{2,0,1:T(8,128)(2,1)}, u32[]{:S(2)}) copy-start(bf16[128,10,64]{2,0,1:T(8,128)(2,1)} %get-tuple-element.56) | copy-start | bytes 491524
  135.9 13.1 %copy-start.71 = (pred[128,256]{0,1:T(8,128)(4,1)}, pred[128,256]{0,1:T(8,128)(4,1)S(1)}, u32[]{:S(2)}) copy-start(pred[128,256]{0,1:T(8,128)(4,1)S(1)} %compare_and_fusion) | copy-start | bytes 98308
  154.4 5.2 copy-start.18
  155.0 4.6 copy-start.74
  155.1 7.7 %copy-start.25 = (bf16[128,1280]{1,0:T(8,128)(2,1)}, bf16[128,1280]{1,0:T(8,128)(2,1)S(1)}, u32[]{:S(2)}) copy-start(bf16[128,1280]{1,0:T(8,128)(2,1)S(1)} %multiply_convert_fusion.5) | copy-start | bytes 983044
  159.6 4.7 copy-start.77
  164.3 4.6 copy-start.34
  261.6 7.6 %copy-start.16 = (bf16[4,4,4,16,1280]{4,3,2,1,0:T(8,128)(2,1)S(1)}, bf16[4,4,4,16,1280]{4,3,2,1,0:T(8,128)(2,1)}, u32[]{:S(2)}) copy-start(bf16[4,4,4,16,1280]{4,3,2,1,0:T(8,128)(2,1)} %copy-done.15) | copy-start | bytes 7864324
  261.6 7.6 %copy-start.90 = (bf16[1,1280,896]{2,1,0:T(8,128)(2,1)S(1)}, bf16[1,1280,896]{2,1,0:T(8,128)(2,1)}, u32[]{:S(2)}) copy-start(bf16[1,1280,896]{2,1,0:T(8,128)(2,1)} %param.32) | copy-start | bytes 6881284
  269.2 5.0 copy-start.65
  269.2 5.1 copy-start.64
  274.4 7.8 %copy-start.89 = (bf16[1,1280,896]{2,1,0:T(8,128)(2,1)S(1)}, bf16[1,1280,896]{2,1,0:T(8,128)(2,1)}, u32[]{:S(2)}) copy-start(bf16[1,1280,896]{2,1,0:T(8,128)(2,1)} %param.31) | copy-start | bytes 6881284
  294.5 4.6 copy-start.19
  294.5 4.6 copy-start.75
  294.5 5.4 copy-start.17
  304.8 4.9 copy-start.14
  309.6 4.7 slice-start
  309.6 4.8 slice-start.1
  396.3 4.7 copy-start.26
  396.3 4.7 copy-start.53
  404.1 4.6 copy-start.60
  404.1 4.6 copy-start.61
  404.1 4.6 copy-start.10
  404.1 4.7 copy-start.57
  423.9 12.0 %copy-start.62 = (bf16[64,128]{0,1:T(8,128)(2,1)S(1)}, bf16[64,128]{0,1:T(8,128)(2,1)}, u32[]{:S(2)}) copy-start(bf16[64,128]{0,1:T(8,128)(2,1)} %get-tuple-element.87) | copy-start | bytes 49156
  423.9 12.0 %copy-start.63 = (bf16[64,128]{0,1:T(8,128)(2,1)S(1)}, bf16[64,128]{0,1:T(8,128)(2,1)}, u32[]{:S(2)}) copy-start(bf16[64,128]{0,1:T(8,128)(2,1)} %get-tuple-element.88) | copy-start | bytes 49156
  423.9 12.0 %copy-start.70 = (bf16[64,128]{0,1:T(8,128)(2,1)S(1)}, bf16[64,128]{0,1:T(8,128)(2,1)}, u32[]{:S(2)}) copy-start(bf16[64,128]{0,1:T(8,128)(2,1)} %get-tuple-element.43) | copy-start | bytes 49156
  424.3 13.3 %copy-start.27 = (f32[256,10,128]{2,0,1:T(8,128)}, f32[256,10,128]{2,0,1:T(8,128)S(1)}, u32[]{:S(2)}) copy-start(f32[256,10,128]{2,0,1:T(8,128)S(1)} %fusion.39) | copy-start | bytes 3932164
  425.5 20.5 %collective-permute-start.1 = (bf16[2,128,10,128]{3,1,2,0:T(8,128)(2,1)}, bf16[2,128,10,128]{3,1,2,0:T(8,128)(2,1)}, u32[]{:S(2)}, u32[]{:S(2)}) collective-permute-start(bf16[2,128,10,128]{3,1,2,0:T(8,128)(2,1)} %pad_maximum_fusion.6), channel_id=1, source_target_pairs={{64,0},{65,1},{66,2},{67,3},{68,4},{69,5},{70,6},{71,7},{72,8},{73... | collective-permute-start | bytes 1966088 | tf_op jit(solution)/shard_map/ppermute | solution.py:771
  427.7 200.7 %collective-permute-start.2 = (bf16[1280,896]{1,0:T(8,128)(2,1)}, bf16[1280,896]{1,0:T(8,128)(2,1)}, u32[]{:S(2)}, u32[]{:S(2)}) collective-permute-start(bf16[1280,896]{1,0:T(8,128)(2,1)} %convolution_convert_fusion.5), channel_id=1, source_target_pairs={{0,64},{64,0},{1,65},{65,1},{2,66},{66,2},{3,67},{67,3},{4,68},{68... | collective-permute-start | bytes 6881288 | tf_op jit(solution)/shard_map/ppermute | solution.py:712
  432.8 200.0 %collective-permute-start.3 = (bf16[1280,896]{1,0:T(8,128)(2,1)}, bf16[1280,896]{1,0:T(8,128)(2,1)}, u32[]{:S(2)}, u32[]{:S(2)}) collective-permute-start(bf16[1280,896]{1,0:T(8,128)(2,1)} %convolution_convert_fusion.4), channel_id=1, source_target_pairs={{0,64},{64,0},{1,65},{65,1},{2,66},{66,2},{3,67},{67,3},{4,68},{68... | collective-permute-start | bytes 6881288 | tf_op jit(solution)/shard_map/ppermute | solution.py:712
  432.8 204.4 %collective-permute-start.4 = (bf16[896,1280]{1,0:T(8,128)(2,1)}, bf16[896,1280]{1,0:T(8,128)(2,1)}, u32[]{:S(2)}, u32[]{:S(2)}) collective-permute-start(bf16[896,1280]{1,0:T(8,128)(2,1)} %convolution_convert_fusion.3), channel_id=1, source_target_pairs={{0,64},{64,0},{1,65},{65,1},{2,66},{66,2},{3,67},{67,3},{4,68},{68... | collective-permute-start | bytes 6881288 | tf_op jit(solution)/shard_map/ppermute | solution.py:712
  477.6 6.5 %copy-start.2 = (bf16[1280,7424]{1,0:T(8,128)(2,1)}, bf16[1280,7424]{1,0:T(8,128)(2,1)S(1)}, u32[]{:S(2)}) copy-start(bf16[1280,7424]{1,0:T(8,128)(2,1)S(1)} %weight_grads.1) | copy-start | bytes 57016324
  618.5 8.7 %copy-start.31 = (f32[128,1280]{1,0:T(8,128)S(1)}, f32[128,1280]{1,0:T(8,128)}, u32[]{:S(2)}) copy-start(f32[128,1280]{1,0:T(8,128)} %get-tuple-element.42) | copy-start | bytes 1966084
  618.6 8.7 %copy-start.56 = (f32[128,1280]{1,0:T(8,128)S(1)}, f32[128,1280]{1,0:T(8,128)}, u32[]{:S(2)}) copy-start(f32[128,1280]{1,0:T(8,128)} %get-tuple-element.114) | copy-start | bytes 1966084
  618.6 8.7 %copy-start.85 = (f32[128]{0:T(128)S(1)}, f32[128]{0:T(128)}, u32[]{:S(2)}) copy-start(f32[128]{0:T(128)} %get-tuple-element.98) | copy-start | bytes 1540
  623.6 4.8 copy-start.37
  632.8 9.4 %copy-start.1 = (bf16[1,896,1280]{2,1,0:T(8,128)(2,1)S(1)}, bf16[1,896,1280]{2,1,0:T(8,128)(2,1)}, u32[]{:S(2)}) copy-start(bf16[1,896,1280]{2,1,0:T(8,128)(2,1)} %param.33) | copy-start | bytes 6881284
  (53 other events, 145.9 us)

commit v2 on v1

--- a/solution.py
+++ b/solution.py
@@ -1,6 +1,7 @@
 import functools
 import jax
 import jax.numpy as jnp
+import numpy as np
 from jax import lax
 from jax.experimental import pallas as pl
 from jax.experimental.pallas import tpu as pltpu
@@ -411,12 +412,16 @@
 PART_AXES = (("y", "z", "g"), ("z", "g", "y"), ("g", "y", "z"))
 
 
-def exchange_kernel(cuts, *refs):
+def exchange_kernel(cuts, work, counts, *refs):
     n = len(cuts)
+    n_in, n_out, n_scratch = counts
+    work_in, refs = refs[n : n + n_in], refs[:n] + refs[n + n_in :]
+    work_out, refs = refs[2 * n : 2 * n + n_out], refs[: 2 * n] + refs[2 * n + n_out :]
+    work_scratch = refs[4 * n + 3 :]
     stages = [refs[0:n], refs[2 * n : 3 * n], refs[3 * n : 4 * n], refs[n : 2 * n]]
     hi, y, z, lo, c = place()
     me = {"y": y, "z": z, "g": lo * 2 + c}
-    wires = Sender(*refs[4 * n :])
+    wires = Sender(*refs[4 * n : 4 * n + 3])
 
     def peer(axis, k):
         q = dict(me)
@@ -445,97 +450,99 @@
             waits.append(wires.local(view(src, axis, me[axis], lanes), own).wait)
         pending[part, phase] = waits
 
-    for part in range(3):
-        go(part, 0)
-    for phase in (1, 2):
+    for phase in (0, 1, 2):
         for part in range(3):
-            for wait in pending[part, phase - 1]:
-                wait()
+            if phase > 0:
+                for wait in pending[part, phase - 1]:
+                    wait()
             go(part, phase)
+        work(phase, work_in, work_out, work_scratch)
     for part in range(3):
         for wait in pending[part, 2]:
             wait()
     wires.finish()
 
 
-def exchange(collective_id, arrays, cuts):
+def exchange(collective_id, arrays, cuts, work, work_in, work_out, work_scratch=()):
     n = len(arrays)
     split = [a.reshape((4, 4, 4) + a.shape[1:]) for a in arrays]
     shapes = [jax.ShapeDtypeStruct(a.shape, a.dtype) for a in split]
+    vmem = pl.BlockSpec(memory_space=pltpu.VMEM)
     out = pl.pallas_call(
-        functools.partial(exchange_kernel, cuts),
-        out_shape=tuple(shapes),
-        in_specs=[pl.BlockSpec(memory_space=pl.ANY)] * n,
-        out_specs=(pl.BlockSpec(memory_space=pl.ANY),) * n,
+        functools.partial(exchange_kernel, cuts, work, (len(work_in), len(work_out), len(work_scratch))),
+        out_shape=tuple(shapes) + tuple(work_out),
+        in_specs=[pl.BlockSpec(memory_space=pl.ANY)] * n + [vmem] * len(work_in),
+        out_specs=(pl.BlockSpec(memory_space=pl.ANY),) * n + (vmem,) * len(work_out),
         scratch_shapes=[pltpu.VMEM(s.shape, s.dtype) for s in shapes] * 2
         + [
             pltpu.SemaphoreType.DMA((27 * n,)),
             pltpu.SemaphoreType.DMA((27 * n,)),
             pltpu.SemaphoreType.DMA((9 * n,)),
-        ],
+        ]
+        + list(work_scratch),
         compiler_params=pltpu.CompilerParams(
-            collective_id=collective_id, has_side_effects=True, vmem_limit_bytes=40 << 20
+            collective_id=collective_id, has_side_effects=True, vmem_limit_bytes=56 << 20
         ),
         name="exchange_rows",
-    )(*split)
-    return [o.reshape(a.shape) for o, a in zip(out, arrays)]
-
-
-def weight_grad_kernel(left, right, out):
-    out[...] = lax.dot_general(
-        left[0], right[...], (((0,), (0,)), ((), ())), preferred_element_type=F32
-    ).astype(BF16)
-
-
-def weight_grads(left, right):
-    rows = left.shape[1]
-    wide = 256
+    )(*split, *work_in)
+    return [o.reshape(a.shape) for o, a in zip(out, arrays)] + list(out[n:])
+
+
+def dot(a, b):
+    return jnp.dot(a, b, preferred_element_type=F32)
+
+
+def dot_t(a, b):
+    return lax.dot_general(a, b, (((1,), (1,)), ((), ())), preferred_element_type=F32)
+
+
+def t_dot(a, b):
+    return lax.dot_general(a, b, (((0,), (0,)), ((), ())), preferred_element_type=F32)
+
+
+def iota(shape, dim):
+    return lax.broadcasted_iota(jnp.int32, shape, dim)
+
+
+def shape(dtype, *dims):
+    return jax.ShapeDtypeStruct(dims, dtype)
+
+
+def local_call(kernel, name, outs, *operands):
     return pl.pallas_call(
-        weight_grad_kernel,
-        grid=(WIDE * 128 // wide,),
-        out_shape=jax.ShapeDtypeStruct((left.shape[2], WIDE * 128), BF16),
-        in_specs=[
-            pl.BlockSpec(
-                (1, rows, left.shape[2]),
-                lambda i: (jnp.where(i < 15, 0, jnp.where(i < 20, 1, 2)), 0, 0),
-            ),
-            pl.BlockSpec((rows, wide), lambda i: (0, i)),
-        ],
-        out_specs=pl.BlockSpec((left.shape[2], wide), lambda i: (0, i)),
-        compiler_params=pltpu.CompilerParams(vmem_limit_bytes=32 << 20),
-        name="weight_grads",
-    )(left, right)
-
-
-def rms_forward(values, gain_vec):
+        kernel,
+        out_shape=tuple(outs),
+        compiler_params=pltpu.CompilerParams(vmem_limit_bytes=56 << 20),
+        name=name,
+    )(*operands)
+
+
+def gain_rows(block):
+    pick = (iota((8, 128), 1) == iota((8, 128), 0) + 64).astype(BF16)
+    return dot_t(pick, block)
+
+
+def rms_forward(values, gain):
     inv_rms = lax.rsqrt(jnp.mean(values * values, axis=-1, keepdims=True) + EPSILON)
-    return (values * inv_rms * gain_vec, inv_rms)
-
-
-def rms_backward(values, inv_rms, gain_vec, upstream):
-    weighted = upstream * gain_vec
+    return values * inv_rms * gain, inv_rms
+
+
+def rms_backward(values, inv_rms, gain, upstream):
+    weighted = upstream * gain
     inner = jnp.mean(weighted * values, axis=-1, keepdims=True)
     grad_in = inv_rms * weighted - values * (inv_rms * inv_rms * inv_rms) * inner
-    grad_gain = jnp.sum(upstream * values * inv_rms, axis=0)
-    return (grad_in, grad_gain)
-
-
-def rotary_tables(positions, head_width):
-    half_width = head_width // 2
-    freq = jnp.power(10000.0, -2.0 * jnp.arange(half_width, dtype=F32) / head_width)
-    angles = positions.astype(F32)[:, None] * freq[None, :]
-    return (jnp.cos(angles)[:, None, :], jnp.sin(angles)[:, None, :])
-
-
-def rotate(values, cosine, sine):
-    half_width = values.shape[-1] // 2
-    first = values[..., :half_width]
-    second = values[..., half_width:]
-    return jnp.concatenate([first * cosine - second * sine, second * cosine + first * sine], axis=-1)
-
-
-def unrotate(values, cosine, sine):
-    return rotate(values, cosine, -sine)
+    grad_gain = jnp.sum(upstream * values * inv_rms, axis=0, keepdims=True)
+    return grad_in, grad_gain
+
+
+def rotary_tables(rows):
+    freq = np.power(10000.0, -2.0 * np.arange(64) / 128)
+    angles = np.arange(rows)[:, None] * freq[None, :]
+    cos, sin = np.cos(angles), np.sin(angles)
+    return (
+        jnp.asarray(np.concatenate([cos, cos], axis=1), F32),
+        jnp.asarray(np.concatenate([-sin, sin], axis=1), F32),
+    )
 
 
 def silu_parts(pre_act):
@@ -543,21 +550,497 @@
     return (pre_act * sigma, sigma * (1.0 + pre_act * (1.0 - sigma)))
 
 
-def dot(a, b):
-    return jnp.dot(a, b, preferred_element_type=F32)
-
-
-def dot_t(a, b):
-    return lax.dot_general(a, b, (((1,), (1,)), ((), ())), preferred_element_type=F32)
-
-
-def t_dot(a, b):
-    return lax.dot_general(a, b, (((0,), (0,)), ((), ())), preferred_element_type=F32)
-
-
-def score_block(queries, keys_all, allowed, inv_root):
-    scores = jnp.einsum("thd,shd->hts", queries, keys_all, preferred_element_type=F32) * inv_root
-    return jnp.where(allowed[None], scores, NEG_BIG)
+def seq_rows():
+    return pl.ds(pl.multiple_of(lax.axis_index("seq") * 128, 128), 128)
+
+
+def qkv_kernel(tok, gains, cos, sin, w, act, q, kv):
+    i = pl.program_id(0)
+
+    @pl.when(i == 0)
+    def _():
+        normed, _inv = rms_forward(tok[...].astype(F32), gain_rows(gains[...])[0:1])
+        act[...] = normed.astype(BF16)
+
+    x = dot(act[...], w[...])
+    here = seq_rows()
+    cosine, sine = cos[here, :], sin[here, :]
+    heads = [x[:, h * 128 : (h + 1) * 128] for h in range(5)]
+    turned = jnp.concatenate([h * cosine + pltpu.roll(h, 64, 1) * sine for h in heads], axis=1)
+
+    @pl.when(i < 2)
+    def _():
+        q[...] = turned.astype(BF16)
+
+    @pl.when(i >= 2)
+    def _():
+        kv[...] = jnp.where(i < 4, turned, x).astype(BF16)
+
+
+def project(tokens, weights, cos, sin):
+    rows, width = tokens.shape
+    whole = lambda a: pl.BlockSpec(a.shape, lambda i: (0, 0))
+    return pl.pallas_call(
+        qkv_kernel,
+        grid=(6,),
+        out_shape=(shape(BF16, rows, width), shape(BF16, rows, width), shape(BF16, rows, 2 * width)),
+        in_specs=[
+            whole(tokens),
+            pl.BlockSpec((width, 128), lambda i: (0, 56)),
+            whole(cos),
+            whole(sin),
+            pl.BlockSpec((width, 640), lambda i: (0, i)),
+        ],
+        out_specs=(
+            pl.BlockSpec((rows, width), lambda i: (0, 0)),
+            pl.BlockSpec((rows, 640), lambda i: (0, jnp.minimum(i, 1))),
+            pl.BlockSpec((rows, 640), lambda i: (0, jnp.maximum(i - 2, 0))),
+        ),
+        compiler_params=pltpu.CompilerParams(vmem_limit_bytes=56 << 20),
+        name="queries_keys_values",
+    )(tokens, weights, cos, sin, weights)
+
+
+def allowed_keys(seg_row, seg_col):
+    hi = lax.axis_index("seq")
+    here = seq_rows()
+    mine = seg_col[here, :]
+    rows = mine.shape[0]
+    own = (seg_row[:, here] == mine) & (iota((rows, rows), 1) <= iota((rows, rows), 0))
+    prior = (seg_row[:, 0:rows] == mine) & (hi == 1)
+    return own, prior
+
+
+def head_probs(h, q, kv, prior, own_ok, prior_ok, width):
+    lanes = slice(h * 128, (h + 1) * 128)
+    behind = slice(width + h * 128, width + (h + 1) * 128)
+    query = q[:, lanes]
+    keys = jnp.concatenate([prior[:, lanes], kv[:, lanes]], axis=0)
+    values = jnp.concatenate([prior[:, behind], kv[:, behind]], axis=0)
+    scores = dot_t(query, keys) * (128.0**-0.5)
+    rows = query.shape[0]
+    scores = jnp.concatenate(
+        [jnp.where(prior_ok, scores[:, :rows], NEG_BIG), jnp.where(own_ok, scores[:, rows:], NEG_BIG)], axis=1
+    )
+    expo = jnp.exp(scores - jnp.max(scores, axis=-1, keepdims=True))
+    return query, keys, values, expo / jnp.sum(expo, axis=-1, keepdims=True)
+
+
+def attend_kernel(tok, q, kv, prior, seg_row, seg_col, routes, out_w, router_w, mixed, hidden_one, act, gates_t, slot_t):
+    rows, width = tok.shape
+    own_ok, prior_ok = allowed_keys(seg_row, seg_col)
+    for h in range(HEADS):
+        _query, _keys, values, probs = head_probs(h, q, kv, prior, own_ok, prior_ok, width)
+        mixed[:, h * 128 : (h + 1) * 128] = dot(probs.astype(BF16), values).astype(BF16)
+    hidden = tok[...].astype(F32) + dot(mixed[...], out_w[...])
+    hidden_one[...] = hidden
+    router = router_w[...]
+    normed, _inv = rms_forward(hidden, gain_rows(router)[1:2])
+    low = normed.astype(BF16)
+    act[...] = low
+    expert = iota((rows, 128), 1)
+    named = routes[...]
+    member = named[:, 0:1] == expert
+    for k in range(1, named.shape[1]):
+        member = member | (named[:, k : k + 1] == expert)
+    logits = jnp.where(member, dot(low, router), NEG_BIG)
+    expo = jnp.where(member, jnp.exp(logits - jnp.max(logits, axis=-1, keepdims=True)), 0.0)
+    gates_t[...] = (expo / jnp.sum(expo, axis=-1, keepdims=True)).T
+    before = (iota((rows, rows), 1) < iota((rows, rows), 0)).astype(BF16)
+    rank = dot(before, member.astype(BF16))
+    slot_t[...] = jnp.where(member, rank, -1.0).T
+
+
+def attend(tokens, q, kv, prior, seg_row, seg_col, routes, weights):
+    rows, width = tokens.shape
+    whole = lambda a: pl.BlockSpec(a.shape, lambda i: (0, 0))
+    operands = (tokens, q, kv, prior, seg_row, seg_col, routes)
+    outs = (
+        shape(BF16, rows, width),
+        shape(F32, rows, width),
+        shape(BF16, rows, width),
+        shape(F32, 128, rows),
+        shape(F32, 128, rows),
+    )
+    return pl.pallas_call(
+        attend_kernel,
+        grid=(1,),
+        out_shape=outs,
+        in_specs=[whole(a) for a in operands]
+        + [pl.BlockSpec((width, 1280), lambda i: (0, 3)), pl.BlockSpec((width, 128), lambda i: (0, 56))],
+        out_specs=tuple(whole(a) for a in outs),
+        compiler_params=pltpu.CompilerParams(vmem_limit_bytes=56 << 20),
+        name="attend",
+    )(*operands, weights, weights)
+
+
+EVEN = 16
+
+
+def even_places(slot_t):
+    experts, rows = slot_t.shape
+    wide = jnp.broadcast_to(slot_t[:, None, :], (experts, EVEN, rows))
+    place_of = iota((experts, EVEN, rows), 1).astype(F32)
+    return wide == place_of
+
+
+def dispatch_kernel(act, grad, gates, slot_t, out_x, out_g, out_l):
+    block, even, width = out_x.shape
+    rows = act.shape[0]
+    here = pl.ds(pl.multiple_of(pl.program_id(0) * block, block), block)
+    slots = slot_t[here, :]
+    places = even_places(slots)
+    last = slots == float(EVEN)
+    hot = places.astype(F32).reshape(block * even, rows).astype(BF16)
+    last_hot = last.astype(BF16)
+    x, g = act[...], grad[...]
+    out_x[...] = dot(hot, x).astype(BF16).reshape(block, even, width)
+    out_g[...] = dot(hot, g).astype(BF16).reshape(block, even, width)
+    gt = gates[here, :]
+    at_slot = jnp.sum(
+        jnp.where(places, jnp.broadcast_to(gt[:, None, :], places.shape), 0.0).reshape(block * even, rows),
+        axis=-1,
+        keepdims=True,
+    )
+    spread = jnp.broadcast_to(at_slot, (block * even, 128)).reshape(block, even, 128)
+    lane_of = iota((block, even, 128), 1) == iota((block, even, 128), 2)
+    even_gates = jnp.sum(jnp.where(lane_of, spread, 0.0), axis=1)
+    last_gates = jnp.sum(jnp.where(last, gt, 0.0), axis=-1, keepdims=True)
+    slot_gates = jnp.where(iota((block, 128), 1) == EVEN, last_gates, even_gates)
+    out_l[...] = jnp.concatenate([dot(last_hot, x), dot(last_hot, g), slot_gates], axis=1).reshape(
+        block, 1, 2 * width + 128
+    )
+
+
+def dispatch(act, grad, gates_t, slot_t, experts):
+    width = act.shape[1]
+    block = 8
+    whole = lambda a: pl.BlockSpec(a.shape, lambda i: (0, 0))
+    cut = lambda n, lanes: pl.BlockSpec((block, n, lanes), lambda i: (i, 0, 0))
+    return pl.pallas_call(
+        dispatch_kernel,
+        grid=(experts // block,),
+        out_shape=(
+            shape(BF16, experts, EVEN, width),
+            shape(BF16, experts, EVEN, width),
+            shape(F32, experts, 1, 2 * width + 128),
+        ),
+        in_specs=[whole(act), whole(grad), whole(gates_t), whole(slot_t)],
+        out_specs=(cut(EVEN, width), cut(EVEN, width), cut(1, 2 * width + 128)),
+        compiler_params=pltpu.CompilerParams(vmem_limit_bytes=32 << 20),
+        name="dispatch",
+    )(act, grad, gates_t, slot_t)
+
+
+def expert_kernel(rows_x, rows_g, rows_l, w_gate, w_up, w_down, out_r, out_d, out_l, all_x, all_g, hidden, d_gate, d_up):
+    sources, _one, _lanes = rows_l.shape
+    width = rows_x.shape[-1]
+    last = rows_l[...].reshape(sources, rows_l.shape[-1])
+    even = sources * EVEN
+    x = jnp.concatenate([rows_x[...].reshape(even, width), last[:, :width].astype(BF16)], axis=0)
+    g = jnp.concatenate(
+        [rows_g[...].reshape(even, width).astype(F32), last[:, width : 2 * width]], axis=0
+    )
+    sent = last[:, 2 * width :]
+    spread = jnp.broadcast_to(sent[:, None, :], (sources, EVEN, 128))
+    own = iota((sources, EVEN, 128), 1) == iota((sources, EVEN, 128), 2)
+    even_gates = jnp.sum(jnp.where(own, spread, 0.0).reshape(even, 128), axis=-1, keepdims=True)
+    last_gates = jnp.sum(jnp.where(iota((sources, 128), 1) == EVEN, sent, 0.0), axis=-1, keepdims=True)
+    grad_result = (jnp.concatenate([even_gates, last_gates], axis=0) * g).astype(BF16)
+    all_x[...] = x
+    all_g[...] = grad_result
+    gate = dot(x, w_gate[...])
+    up_ = dot(x, w_up[...])
+    silu, slope = silu_parts(gate)
+    low = (silu * up_).astype(BF16)
+    hidden[...] = low
+    grad_hidden = dot_t(grad_result, w_down[...])
+    grad_gate = (grad_hidden * up_ * slope).astype(BF16)
+    grad_up = (grad_hidden * silu).astype(BF16)
+    d_gate[...] = grad_gate
+    d_up[...] = grad_up
+    result = dot(low, w_down[...]).astype(BF16)
+    grad_in = (dot_t(grad_gate, w_gate[...]) + dot_t(grad_up, w_up[...])).astype(BF16)
+    out_r[...] = result[:even].reshape(sources, EVEN, width)
+    out_d[...] = grad_in[:even].reshape(sources, EVEN, width)
+    out_l[...] = jnp.concatenate([result[even:], grad_in[even:]], axis=1).astype(F32).reshape(sources, 1, 2 * width)
+
+
+def expert(rows_x, rows_g, rows_l, w_gate, w_up, w_down):
+    devices, _even, width = rows_x.shape
+    inner = w_gate.shape[1]
+    steps = 4
+    src = devices // steps
+    rows = src * (EVEN + 1)
+    total = rows * steps
+    whole = lambda a: pl.BlockSpec(a.shape, lambda i: (0, 0))
+    cut = lambda n, lanes: pl.BlockSpec((src, n, lanes), lambda i: (i, 0, 0))
+    flat = lambda lanes: pl.BlockSpec((rows, lanes), lambda i: (i, 0))
+    return pl.pallas_call(
+        expert_kernel,
+        grid=(steps,),
+        out_shape=(
+            shape(BF16, devices, EVEN, width),
+            shape(BF16, devices, EVEN, width),
+            shape(F32, devices, 1, 2 * width),
+            shape(BF16, total, width),
+            shape(BF16, total, width),
+            shape(BF16, total, inner),
+            shape(BF16, total, inner),
+            shape(BF16, total, inner),
+        ),
+        in_specs=[cut(EVEN, width), cut(EVEN, width), cut(1, rows_l.shape[-1]), whole(w_gate), whole(w_up), whole(w_down)],
+        out_specs=(
+            cut(EVEN, width),
+            cut(EVEN, width),
+            cut(1, 2 * width),
+            flat(width),
+            flat(width),
+            flat(inner),
+            flat(inner),
+            flat(inner),
+        ),
+        compiler_params=pltpu.CompilerParams(vmem_limit_bytes=60 << 20),
+        name="expert",
+    )(rows_x, rows_g, rows_l, w_gate, w_up, w_down)
+
+
+def shared_work(phase, ins, outs, scratch):
+    act, grad, sgu, sdown = ins
+    out_s, grad_in, grad_gu, grad_down = outs
+    (hidden,) = scratch
+    inner = sdown.shape[0]
+    if phase == 0:
+        gate = dot(act[...], sgu[:, :inner])
+        up_ = dot(act[...], sgu[:, inner:])
+        silu, slope = silu_parts(gate)
+        hidden[...] = (silu * up_).astype(BF16)
+        grad_hidden = dot_t(grad[...], sdown[...])
+        grad_gu[:, :inner] = (grad_hidden * up_ * slope).astype(BF16)
+        grad_gu[:, inner:] = (grad_hidden * silu).astype(BF16)
+    elif phase == 1:
+        out_s[...] = dot(hidden[...], sdown[...])
+        grad_in[...] = dot_t(grad_gu[...], sgu[...])
+    else:
+
+        @pl.loop(0, inner // 256)
+        def _(i):
+            r = pl.ds(pl.multiple_of(i * 256, 256), 256)
+            grad_down[r, :] = t_dot(hidden[:, r], grad[...]).astype(BF16)
+
+
+def expert_work(phase, ins, outs, scratch):
+    all_x, all_g, hidden, d_gate, d_up = ins
+    g_gate, g_up, g_down = outs
+    if phase < 2:
+        grad, out = (d_gate, g_gate) if phase == 0 else (d_up, g_up)
+
+        @pl.loop(0, out.shape[0] // 256)
+        def _(i):
+            r = pl.ds(pl.multiple_of(i * 256, 256), 256)
+            out[r, :] = t_dot(all_x[:, r], grad[...]).astype(BF16)
+
+    else:
+
+        @pl.loop(0, g_down.shape[0] // 128)
+        def _(i):
+            r = pl.ds(pl.multiple_of(i * 128, 128), 128)
+            g_down[r, :] = t_dot(hidden[:, r], all_g[...]).astype(BF16)
+
+
+def split_terms(w):
+    top = w.astype(BF16)
+    rest = w - top.astype(F32)
+    mid = rest.astype(BF16)
+    return top, mid, (rest - mid.astype(F32)).astype(BF16)
+
+
+def combine_kernel(
+    back_r, back_d, back_l, slot_t, gates_t, grad, hidden_one, out_s, grad_in_s, router_w, out_w,
+    layer_out, grad_hidden, grad_low, grad_mixed, grad_logits, grad_gain,
+):
+    experts = back_r.shape[0]
+    rows, width = hidden_one.shape
+    slots = slot_t[0:experts, :]
+    places = even_places(slots)
+    last = slots == float(EVEN)
+    out_rows = back_r[...].reshape(experts * EVEN, width)
+    last_l = back_l[...].reshape(experts, 2 * width).astype(BF16)
+    gt = gates_t[0:experts, :]
+    even_w = jnp.where(places, jnp.broadcast_to(gt[:, None, :], places.shape), 0.0).reshape(experts * EVEN, rows)
+    last_w = jnp.where(last, gt, 0.0)
+    routed = jnp.zeros((rows, width), F32)
+    for e_term, l_term in zip(split_terms(even_w), split_terms(last_w)):
+        routed = routed + t_dot(e_term, out_rows) + t_dot(l_term, last_l[:, :width])
+    hidden = hidden_one[...]
+    layer_out[...] = (hidden + out_s[...] + routed).astype(BF16)
+    g = grad[...]
+    dots = dot_t(out_rows, g).reshape(experts, EVEN, rows)
+    dots_last = dot_t(last_l[:, :width], g)
+    grad_gates = jnp.sum(jnp.where(places, dots, 0.0), axis=1) + jnp.where(last, dots_last, 0.0)
+    logits_t = gt * (grad_gates - jnp.sum(gt * grad_gates, axis=0, keepdims=True))
+    low_logits = jnp.concatenate([logits_t, jnp.zeros((128 - experts, rows), F32)], axis=0).T.astype(BF16)
+    grad_logits[...] = low_logits
+    hot = places.astype(F32).reshape(experts * EVEN, rows).astype(BF16)
+    grad_routed = t_dot(hot, back_d[...].reshape(experts * EVEN, width)) + t_dot(last.astype(BF16), last_l[:, width:])
+    router = router_w[...]
+    grad_act = grad_routed + dot_t(low_logits, router) + grad_in_s[...]
+    gain = gain_rows(router)[1:2]
+    _normed, inv = rms_forward(hidden, gain)
+    grad_norm, gain_sum = rms_backward(hidden, inv, gain, grad_act)
+    grad_gain[...] = gain_sum
+    total = g.astype(F32) + grad_norm
+    grad_hidden[...] = total
+    low = total.astype(BF16)
+    grad_low[...] = low
+    grad_mixed[...] = dot_t(low, out_w[...]).astype(BF16)
+
+
+def combine(back_r, back_d, back_l, slot_t, gates_t, grad, hidden_one, out_s, grad_in_s, weights):
+    rows, width = hidden_one.shape
+    operands = (back_r, back_d, back_l, slot_t, gates_t, grad, hidden_one, out_s, grad_in_s)
+    whole = lambda a: pl.BlockSpec(a.shape, lambda i: (0,) * len(a.shape))
+    outs = (
+        shape(BF16, rows, width),
+        shape(F32, rows, width),
+        shape(BF16, rows, width),
+        shape(BF16, rows, width),
+        shape(BF16, rows, 128),
+        shape(F32, 1, width),
+    )
+    return pl.pallas_call(
+        combine_kernel,
+        grid=(1,),
+        out_shape=outs,
+        in_specs=[whole(a) for a in operands]
+        + [pl.BlockSpec((width, 128), lambda i: (0, 56)), pl.BlockSpec((width, 1280), lambda i: (0, 3))],
+        out_specs=tuple(whole(a) for a in outs),
+        compiler_params=pltpu.CompilerParams(vmem_limit_bytes=56 << 20),
+        name="combine",
+    )(*operands, weights, weights)
+
+
+def attend_back_kernel(q, kv, prior, seg_row, seg_col, grad_mixed, cos, sin, grad_q, grad_own, grad_prior):
+    rows, width = q.shape
+    own_ok, prior_ok = allowed_keys(seg_row, seg_col)
+    here = seq_rows()
+    cosine, sine = cos[here, :], sin[here, :]
+    inv_root = 128.0**-0.5
+    for h in range(HEADS):
+        query, keys, values, probs = head_probs(h, q, kv, prior, own_ok, prior_ok, width)
+        lanes = slice(h * 128, (h + 1) * 128)
+        behind = slice(width + h * 128, width + (h + 1) * 128)
+        gm = grad_mixed[:, lanes]
+        grad_probs = dot_t(gm, values)
+        inner = jnp.sum(probs * grad_probs, axis=-1, keepdims=True)
+        grad_scores = (probs * (grad_probs - inner)).astype(BF16)
+        grad_values = t_dot(probs.astype(BF16), gm)
+        gq = dot(grad_scores, keys) * inv_root
+        grad_keys = t_dot(grad_scores, query) * inv_root
+        grad_q[:, lanes] = (gq * cosine - pltpu.roll(gq, 64, 1) * sine).astype(BF16)
+        grad_own[:, lanes] = grad_keys[rows:]
+        grad_own[:, behind] = grad_values[rows:]
+        grad_prior[:, lanes] = grad_keys[:rows].astype(BF16)
+        grad_prior[:, behind] = grad_values[:rows].astype(BF16)
+
+
+def input_grad_kernel(tok, gains, cos, sin, grad_q, grad_own, later, grad_hidden, w, grad_qkv, grad_tokens, grad_gain, total):
+    i = pl.program_id(0)
+    rows, width = tok.shape
+
+    @pl.when(i == 0)
+    def _():
+        here = seq_rows()
+        cosine, sine = cos[here, :], sin[here, :]
+        grad_qkv[:, :width] = grad_q[...]
+        for h in range(HEADS):
+            lanes = slice(h * 128, (h + 1) * 128)
+            gk = grad_own[:, lanes] + later[:, lanes].astype(F32)
+            grad_qkv[:, width + h * 128 : width + (h + 1) * 128] = (
+                gk * cosine - pltpu.roll(gk, 64, 1) * sine
+            ).astype(BF16)
+        grad_qkv[:, 2 * width :] = (grad_own[:, width:] + later[:, width:].astype(F32)).astype(BF16)
+        total[...] = jnp.zeros_like(total)
+
+    lanes = pl.ds(pl.multiple_of(i * 640, 128), 640)
+    total[...] += dot_t(grad_qkv[:, lanes], w[...])
+
+    @pl.when(i == pl.num_programs(0) - 1)
+    def _():
+        values = tok[...].astype(F32)
+        gain = gain_rows(gains[...])[0:1]
+        _normed, inv = rms_forward(values, gain)
+        grad_norm, gain_sum = rms_backward(values, inv, gain, total[...])
+        grad_gain[...] = gain_sum
+        grad_tokens[...] = grad_hidden[...] + grad_norm
+
+
+def input_grads(tokens, cos, sin, grad_q, grad_own, later, grad_hidden, weights):
+    rows, width = tokens.shape
+    whole = lambda a: pl.BlockSpec(a.shape, lambda i: (0, 0))
+    outs = (shape(BF16, rows, 3 * width), shape(F32, rows, width), shape(F32, 1, width))
+    return pl.pallas_call(
+        input_grad_kernel,
+        grid=(6,),
+        out_shape=outs,
+        in_specs=[
+            whole(tokens),
+            pl.BlockSpec((width, 128), lambda i: (0, 56)),
+            whole(cos),
+            whole(sin),
+            whole(grad_q),
+            whole(grad_own),
+            whole(later),
+            whole(grad_hidden),
+            pl.BlockSpec((width, 640), lambda i: (0, i)),
+        ],
+        out_specs=tuple(whole(a) for a in outs),
+        scratch_shapes=[pltpu.VMEM((rows, width), F32)],
+        compiler_params=pltpu.CompilerParams(vmem_limit_bytes=56 << 20),
+        name="input_grads",
+    )(tokens, weights, cos, sin, grad_q, grad_own, later, grad_hidden, weights)
+
+
+def weight_grad_kernel(act_attn, mixed, act_ffn, grad_qkv, grad_out, grad_gu, grad_logits, gain_a, gain_f, out):
+    i = pl.program_id(0)
+
+    def product(left, right, start):
+        lanes = pl.ds(pl.multiple_of((i - start) * 256, 256), 256)
+        out[...] = t_dot(left[...], right[:, lanes]).astype(BF16)
+
+    @pl.when(i < 15)
+    def _():
+        product(act_attn, grad_qkv, 0)
+
+    @pl.when((i >= 15) & (i < 20))
+    def _():
+        product(mixed, grad_out, 15)
+
+    @pl.when((i >= 20) & (i < 28))
+    def _():
+        product(act_ffn, grad_gu, 20)
+
+    @pl.when(i == 28)
+    def _():
+        row = iota((8, 1280), 0)
+        gains = jnp.where(row == 0, gain_a[...], jnp.where(row == 1, gain_f[...], 0.0)).astype(BF16)
+        pick = (iota((8, 128), 1) == iota((8, 128), 0) + 64).astype(BF16)
+        out[:, :128] = (t_dot(act_ffn[...], grad_logits[...]) + t_dot(gains, pick)).astype(BF16)
+        out[:, 128:] = jnp.zeros((1280, 128), BF16)
+
+
+def weight_grads(*operands):
+    width = operands[0].shape[1]
+    whole = lambda a: pl.BlockSpec(a.shape, lambda i: (0, 0))
+    return pl.pallas_call(
+        weight_grad_kernel,
+        grid=(WIDE // 2,),
+        out_shape=shape(BF16, width, WIDE * 128),
+        in_specs=[whole(a) for a in operands],
+        out_specs=pl.BlockSpec((width, 256), lambda i: (0, i)),
+        compiler_params=pltpu.CompilerParams(vmem_limit_bytes=56 << 20),
+        name="weight_grads",
+    )(*operands)
 
 
 def per_device(
@@ -579,13 +1062,12 @@
     expert_up,
     expert_down,
 ):
-    tok_rows = tokens.shape[1]
+    rows = tokens.shape[1]
     width = tokens.shape[2]
-    head_width = width // HEADS
     experts = w_router.shape[1]
-    top_count = routes.shape[2]
-    slots = tok_rows * top_count * 5 // (experts * 4)
-    even = slots - 1
+    tokens, grad, routes = tokens[0], cotangent[0], routes[0]
+    seg_row = segments
+    seg_col = segments.reshape(-1, 1)
 
     def spread(w):
         w = w.reshape(w.shape[0], experts, w.shape[1] // experts)
@@ -607,193 +1089,50 @@
         axis=1,
     )
     weights, sdown_w = gather_weights(shard, shared_down)
-    qkv_w = weights[:, :3840]
-    out_w = weights[:, 3840:5120]
-    sgu_w = weights[:, 5120:7168]
-    router_w = weights[:, 7168 : 7168 + experts]
-    gain_attn = weights[:, 7168 + experts].astype(F32)
-    gain_ffn = weights[:, 7169 + experts].astype(F32)
-
-    route_rows = routes[0]
-    picked = route_rows[:, :, None] == jnp.arange(experts, dtype=jnp.int32)[None, None, :]
-    member = jnp.any(picked, axis=1)
-    before = jnp.arange(tok_rows)[None, :] < jnp.arange(tok_rows)[:, None]
-    rank = dot(before.astype(BF16), member.astype(BF16)).astype(jnp.int32)
-    slot_of = jnp.where(member, rank, -1).T
-    place_even = slot_of[:, None, :] == jnp.arange(even, dtype=jnp.int32)[None, :, None]
-    place_last = slot_of == even
-    even_hot = place_even.astype(BF16).reshape(experts * even, tok_rows)
-    last_hot = place_last.astype(BF16)
-
-    inv_root = head_width ** (-0.5)
-    seq_place = lax.axis_index("seq")
-    inputs = tokens[0].astype(F32)
-    positions = seq_place * tok_rows + jnp.arange(tok_rows, dtype=jnp.int32)
-    cosine, sine = rotary_tables(positions, head_width)
-    seg_row = segments[0]
-    own_seg = lax.dynamic_slice_in_dim(seg_row, seq_place * tok_rows, tok_rows)
-    prior_seg = lax.dynamic_slice_in_dim(seg_row, jnp.maximum(seq_place - 1, 0) * tok_rows, tok_rows)
-    key_places = jnp.concatenate([positions - tok_rows, positions])
-    key_segs = jnp.concatenate([prior_seg, own_seg])
-    allowed = (
-        (key_places[None, :] <= positions[:, None])
-        & (key_places[None, :] >= 0)
-        & (key_segs[None, :] == own_seg[:, None])
-    )
-    normed_attn, inv_attn = rms_forward(inputs, gain_attn)
-    act_attn = normed_attn.astype(BF16)
-    qkv = dot(act_attn, qkv_w)
-    heads = lambda v: v.reshape(tok_rows, HEADS, head_width)
-    queries = rotate(heads(qkv[:, :width]), cosine, sine).astype(BF16)
-    keys_own = rotate(heads(qkv[:, width : 2 * width]), cosine, sine).astype(BF16)
-    values_own = heads(qkv[:, 2 * width :].astype(BF16))
-    prior = lax.ppermute(jnp.stack([keys_own, values_own]), "seq", [(0, 1)])
-    keys_all = jnp.concatenate([prior[0], keys_own], axis=0)
-    values_all = jnp.concatenate([prior[1], values_own], axis=0)
-    scores = score_block(queries, keys_all, allowed, inv_root)
-    top_score = jnp.max(scores, axis=-1, keepdims=True)
-    expo = jnp.exp(scores - top_score)
-    probs = expo / jnp.sum(expo, axis=-1, keepdims=True)
-    probs_low = probs.astype(BF16)
-    mixed = (
-        jnp.einsum("hts,shd->thd", probs_low, values_all, preferred_element_type=F32)
-        .reshape(tok_rows, width)
-        .astype(BF16)
-    )
-    hidden_one = inputs + dot(mixed, out_w)
-    normed_ffn, inv_ffn = rms_forward(hidden_one, gain_ffn)
-    act_ffn = normed_ffn.astype(BF16)
-    logits = jnp.where(member, dot(act_ffn, router_w), NEG_BIG)
-    gate_expo = jnp.where(member, jnp.exp(logits - jnp.max(logits, axis=-1, keepdims=True)), 0.0)
-    gates = gate_expo / jnp.sum(gate_expo, axis=-1, keepdims=True)
-
-    grad_low = cotangent[0]
-    gates_t = gates.T
-    slot_gates = jnp.concatenate(
-        [
-            jnp.sum(jnp.where(place_even, gates_t[:, None, :], 0.0), axis=-1),
-            jnp.sum(jnp.where(place_last, gates_t, 0.0), axis=-1, keepdims=True),
-        ],
-        axis=1,
-    )
-    both = jnp.concatenate([act_ffn, grad_low], axis=1)
-    even_rows = dot(even_hot, both).astype(BF16).reshape(experts, even, 2 * width)
-    last_rows = jnp.concatenate(
-        [dot(last_hot, both), jnp.pad(slot_gates, ((0, 0), (0, 128 - slots)))], axis=1
-    )
-    rows_x, rows_g, rows_l = exchange(
+    cos, sin = rotary_tables(2 * rows)
+    act_attn, q, kv = project(tokens, weights, cos, sin)
+    prior = lax.ppermute(kv, "seq", [(0, 1)])
+    mixed, hidden_one, act_ffn, gates_t, slot_t = attend(tokens, q, kv, prior, seg_row, seg_col, routes, weights)
+
+    rows_x, rows_g, rows_l = dispatch(act_ffn, grad, gates_t, slot_t, experts)
+    rows_x, rows_g, rows_l, out_s, grad_in_s, grad_gu, grad_sdown = exchange(
         3,
-        (even_rows[:, :, :width], even_rows[:, :, width:], last_rows[:, None, :]),
+        (rows_x, rows_g, rows_l),
         (((0, 4), (4, 3), (7, 3)), ((0, 3), (3, 4), (7, 3)), ((0, 6), (6, 6), (12, 9))),
-    )
-    rows_l = rows_l[:, 0]
-    arrived_x = jnp.concatenate([rows_x.reshape(-1, width), rows_l[:, :width].astype(BF16)])
-    arrived_g = jnp.concatenate([rows_g.reshape(-1, width), rows_l[:, width : 2 * width].astype(BF16)])
-    row_gates = jnp.concatenate(
-        [rows_l[:, 2 * width : 2 * width + even].reshape(-1), rows_l[:, 2 * width + even]]
-    )
-
-    gate_local, up_local, down_local = expert_gate[0], expert_up[0], expert_down[0]
-    gate_e = dot(arrived_x, gate_local)
-    up_e = dot(arrived_x, up_local)
-    silu_e, slope_e = silu_parts(gate_e)
-    hidden_e = (silu_e * up_e).astype(BF16)
-    result = dot(hidden_e, down_local).astype(BF16)
-    grad_result = (row_gates[:, None] * arrived_g.astype(F32)).astype(BF16)
-    grad_hidden_e = dot_t(grad_result, down_local)
-    grad_gate_e = (grad_hidden_e * up_e * slope_e).astype(BF16)
-    grad_up_e = (grad_hidden_e * silu_e).astype(BF16)
-    part_expert = (
-        t_dot(arrived_x, grad_gate_e).astype(BF16),
-        t_dot(arrived_x, grad_up_e).astype(BF16),
-        t_dot(hidden_e, grad_result).astype(BF16),
-    )
-    grad_arrived = (dot_t(grad_gate_e, gate_local) + dot_t(grad_up_e, up_local)).astype(BF16)
+        shared_work,
+        (act_ffn, grad, weights[:, 5120:7168], sdown_w),
+        (shape(F32, rows, width), shape(F32, rows, width), shape(BF16, rows, 2048), shape(BF16, 1024, width)),
+        (pltpu.VMEM((rows, 1024), BF16),),
+    )
+    out_r, out_d, out_l, *kept = expert(rows_x, rows_g, rows_l, expert_gate[0], expert_up[0], expert_down[0])
+    back_r, back_d, back_l, *part_expert = exchange(
+        4,
+        (out_r, out_d, out_l),
+        (((0, 4), (4, 3), (7, 3)), ((0, 3), (3, 4), (7, 3)), ((0, 6), (6, 6), (12, 8))),
+        expert_work,
+        tuple(kept),
+        tuple(shape(BF16, *w.shape[1:]) for w in (expert_gate, expert_up, expert_down)),
+    )
+    layer_out, grad_hidden, grad_low, grad_mixed, grad_logits, gain_ffn = combine(
+        back_r, back_d, back_l, slot_t, gates_t, grad, hidden_one, out_s, grad_in_s, weights
+    )
+    grad_q, grad_own, grad_prior = local_call(
+        attend_back_kernel,
+        "attend_back",
+        (shape(BF16, rows, width), shape(F32, rows, 2 * width), shape(BF16, rows, 2 * width)),
+        q, kv, prior, seg_row, seg_col, grad_mixed, cos, sin,
+    )
+    later = lax.ppermute(grad_prior, "seq", [(1, 0)])
+    *part_expert, later = lax.optimization_barrier((*part_expert, later))
     swapped = [lax.ppermute(g, "seq", [(0, 1), (1, 0)]) for g in part_expert]
-    rows_out = experts * even
-    back = exchange(
-        4,
-        (
-            result[:rows_out].reshape(experts, even, width),
-            grad_arrived[:rows_out].reshape(experts, even, width),
-            jnp.concatenate([result[rows_out:], grad_arrived[rows_out:]], axis=1).astype(F32)[:, None, :],
-        ),
-        (((0, 4), (4, 3), (7, 3)), ((0, 3), (3, 4), (7, 3)), ((0, 6), (6, 6), (12, 8))),
-    )
-    back_out, back_grad = back[0].reshape(-1, width), back[1].reshape(-1, width)
-    back_last = back[2][:, 0].astype(BF16)
-
-    gate_s = dot(act_ffn, sgu_w[:, :1024])
-    up_s = dot(act_ffn, sgu_w[:, 1024:])
-    silu_s, slope_s = silu_parts(gate_s)
-    hidden_s = (silu_s * up_s).astype(BF16)
-    out_s = dot(hidden_s, sdown_w)
-    grad_hidden_s = dot_t(grad_low, sdown_w)
-    grad_gate_s = (grad_hidden_s * up_s * slope_s).astype(BF16)
-    grad_up_s = (grad_hidden_s * silu_s).astype(BF16)
-    grad_shared_down = t_dot(hidden_s, grad_low).astype(BF16)
-
-    weight_even = jnp.where(place_even, gates_t[:, None, :], 0.0).reshape(rows_out, tok_rows)
-    weight_last = jnp.where(place_last, gates_t, 0.0)
-
-    def weighted(w, rows):
-        top = lax.reduce_precision(w, 8, 7)
-        mid = lax.reduce_precision(w - top, 8, 7)
-        low = (w - top) - mid
-        three = jnp.concatenate([top, mid, low], axis=1).astype(BF16)
-        s = t_dot(three, rows)
-        return s[:tok_rows] + s[tok_rows : 2 * tok_rows] + s[2 * tok_rows :]
-
-    routed = weighted(weight_even, back_out) + weighted(weight_last, back_last[:, :width])
-    layer_out = (hidden_one + out_s + routed).astype(BF16)
-
-    grad_final = grad_low.astype(F32)
-    dots_even = dot_t(back_out, grad_low).reshape(experts, even, tok_rows)
-    dots_last = dot_t(back_last[:, :width], grad_low)
-    grad_gates = (
-        jnp.sum(jnp.where(place_even, dots_even, 0.0), axis=1) + jnp.where(place_last, dots_last, 0.0)
-    ).T
-    grad_logits = (gates * (grad_gates - jnp.sum(gates * grad_gates, axis=-1, keepdims=True))).astype(BF16)
-    grad_routed = t_dot(even_hot, back_grad) + t_dot(last_hot, back_last[:, width:])
-    grad_gu_s = jnp.concatenate([grad_gate_s, grad_up_s], axis=1)
-    grad_act_ffn = grad_routed + dot_t(grad_logits, router_w) + dot_t(grad_gu_s, sgu_w)
-    grad_norm_f, grad_gain_ffn = rms_backward(hidden_one, inv_ffn, gain_ffn, grad_act_ffn)
-    grad_hidden_one = grad_final + grad_norm_f
-    grad_attn_low = grad_hidden_one.astype(BF16)
-    grad_mixed = heads(dot_t(grad_attn_low, out_w).astype(BF16))
-
-    grad_probs = jnp.einsum("thd,shd->hts", grad_mixed, values_all, preferred_element_type=F32)
-    inner = jnp.sum(probs * grad_probs, axis=-1, keepdims=True)
-    grad_scores = (probs * (grad_probs - inner)).astype(BF16)
-    grad_values_all = jnp.einsum("hts,thd->shd", probs_low, grad_mixed, preferred_element_type=F32)
-    grad_query_rot = jnp.einsum("hts,shd->thd", grad_scores, keys_all, preferred_element_type=F32) * inv_root
-    grad_keys_all = jnp.einsum("hts,thd->shd", grad_scores, queries, preferred_element_type=F32) * inv_root
-    later = lax.ppermute(
-        jnp.stack([grad_keys_all[:tok_rows], grad_values_all[:tok_rows]]).astype(BF16), "seq", [(1, 0)]
-    ).astype(F32)
-    grad_key_rot = grad_keys_all[tok_rows:] + later[0]
-    grad_value = (grad_values_all[tok_rows:] + later[1]).astype(BF16).reshape(tok_rows, width)
-    grad_query = unrotate(grad_query_rot, cosine, sine).astype(BF16).reshape(tok_rows, width)
-    grad_key = unrotate(grad_key_rot, cosine, sine).astype(BF16).reshape(tok_rows, width)
-    grad_qkv = jnp.concatenate([grad_query, grad_key, grad_value], axis=1)
-    grad_act_attn = dot_t(grad_qkv, qkv_w)
-    grad_norm_a, grad_gain_attn = rms_backward(inputs, inv_attn, gain_attn, grad_act_attn)
-    grad_tokens = grad_hidden_one + grad_norm_a
-
-    right = jnp.concatenate(
-        [grad_qkv, grad_attn_low, grad_gu_s, grad_logits, jnp.zeros((tok_rows, 256 - experts), BF16)], axis=1
-    )
-    grads = weight_grads(jnp.stack([act_attn, mixed, act_ffn]), right)
-    gains = jnp.stack([grad_gain_attn, grad_gain_ffn], axis=1).astype(BF16)
-    grads = lax.dynamic_update_slice(grads, gains, (0, 7168 + experts))
-    own, own_down = scatter_sums(grads, grad_shared_down)
+    grad_qkv, grad_tokens, gain_attn = input_grads(tokens, cos, sin, grad_q, grad_own, later, grad_hidden, weights)
+    grads = weight_grads(act_attn, mixed, act_ffn, grad_qkv, grad_low, grad_gu, grad_logits, gain_attn, gain_ffn)
+    own, own_down = scatter_sums(grads, grad_sdown)
 
     def gathered_hidden(w):
         return w.reshape(w.shape[0], experts, 16)[:, :, :14].reshape(w.shape[0], experts * 14)
 
-    expert_grads = [
-        (a.astype(F32) + b.astype(F32))[None] for a, b in zip(part_expert, swapped)
-    ]
+    expert_grads = [(a.astype(F32) + b.astype(F32))[None] for a, b in zip(part_expert, swapped)]
     return (
         layer_out[None],
         grad_tokens[None],

time: 651 us -> 568 us (0.87)
  matrix products: 107 us -> 0 us
  Pallas kernels: 377 us -> 479 us
  local copies, waits for them, and re-layouts: 91.1 us -> 31.6 us
  other arithmetic: 42.2 us -> 14.2 us
  waiting for transfers between devices: 7.75 us -> 26.8 us
    dot_general x35 -> x0, matrix products: 104 us -> none  [the longest x10 38.1 us: dot_t(): lax.dot_general(a, b, (((1,), (1,)), ((), ())), preferred_element_type=F32)]
    pallas_call x3 -> x10, Pallas kernels: 163 us -> 253 us  [the longest x2 164 us: exchange(): pl.pallas_call(functools.partial(exchange_kernel, cuts, work, (len(work_i...]
    unnamed x197 -> x46, local copies, waits for them, and re-layouts: 31.9 us -> 10.3 us
    ppermute x2, waiting for transfers between devices: 7.74 us -> 26.8 us  [the longest x1 19.4 us: per_device(): later = lax.ppermute(grad_prior, 'seq', [(1, 0)])]
    slice x18 -> x1, local copies, waits for them, and re-layouts: 18.9 us -> 5.61 us  [per_device(): weights[:, 5120:7168]]
    pallas_call x1, Pallas kernels: 129 us -> 141 us  [scatter_sums(): pl.pallas_call(scatter_kernel, out_shape=(jax.ShapeDtypeStruct((32, WIDE...]
    another operation x10 -> x0, other arithmetic: 10.3 us -> none
  transfers between devices with their start and end apart: 5 -> 5, of which waited for: 2 -> 2; matrix products, arithmetic and copies ran while one was open for 9% -> 5% of each run, Pallas kernels for 22% -> 31%
where the time goes in v2:
time: 568 us; the launch traced here: 561 us
  Pallas kernels  479 us (84%)
  local copies, waits for them, and re-layouts  31.6 us (6%)
  waiting for transfers between devices  26.8 us (5%)
  other arithmetic  14.2 us (2%)
  starting transfers between devices  8.83 us (2%)
    pallas_call x2, Pallas kernels, exchange(): pl.pallas_call(functools.partial(exchange_kernel, cuts, work, (len(work_i...  164 us
    pallas_call x1, Pallas kernels, scatter_sums(): pl.pallas_call(scatter_kernel, out_shape=(jax.ShapeDtypeStruct((32, WIDE...  141 us
    pallas_call x1, Pallas kernels, gather_weights(): pl.pallas_call(gather_kernel, out_shape=(jax.ShapeDtypeStruct((4, 4, 80,...  84.9 us
    pallas_call x1, Pallas kernels, expert(): pl.pallas_call(expert_kernel, grid=(steps,), out_shape=(shape(BF16, devic...  23.2 us
    pallas_call x1, Pallas kernels, weight_grads(): pl.pallas_call(weight_grad_kernel, grid=(WIDE // 2,), out_shape=shape(BF1...  21 us
    ppermute x1, waiting for transfers between devices, per_device(): later = lax.ppermute(grad_prior, 'seq', [(1, 0)])  19.4 us
    broadcast_in_dim x3, other arithmetic, per_device(): (a.astype(F32) + b.astype(F32))[None]  14.2 us
  transfers between devices with their start and end apart: 5, of which 2 were waited for; matrix products, arithmetic and copies ran while one was open for 5% of the time, Pallas kernels for 31%

profile of v2, /device:TPU:1, one launch (start us, length us, event | category | flops | bytes accessed | tf_op | source)
XLA Modules:
  0.0 561.5 jit_solution(9347547837708590570)
XLA Ops:
  0.7 1.5 reshape.105
  2.4 0.4 reshape.106
  2.8 1.4 reshape.107
  4.3 0.4 reshape.108
  4.8 0.1 copy.37
  4.9 0.1 copy.38
  5.1 0.1 concatenate.3
  5.2 2.1 dynamic_update_slice.3.win
  7.4 84.9 %gather_weights.1 = (bf16[4,4,80,7424]{3,2,1,0:T(8,128)(2,1)}, bf16[4,4,64,1280]{3,2,1,0:T(8,128)(2,1)S(1)}) custom-call(bf16[32,7424]{1,0:T(8,128)(2,1)S(1)} %dynamic_update_slice.3.win, bf16[16,1280]{1,0:T(8,128)(2,1)S(1)} %pad.13.sdw), custom_call_target="tpu_custom_call" | custom-call | tf_op jit(solution)/shard_map/gather_weights/pallas_call | solution.py:226
  92.2 1.5 copy-done.2
  93.7 8.2 %queries_keys_values.1 = (bf16[128,1280]{1,0:T(8,128)(2,1)}, bf16[128,1280]{1,0:T(8,128)(2,1)}, bf16[128,2560]{1,0:T(8,128)(2,1)}) custom-call(bf16[128,1280]{1,0:T(8,128)(2,1)} %bitcast.53, bf16[1280,7424]{1,0:T(8,128)(2,1)} %bitcast.43, f32[256,128]{1,0:T(8,128)} %constant.21.clone.cos, f32[256,128]{1,0:T(8,128)} %constant.22.clone.sin, ...), custom_call_target="tpu_custom_call" | custom-call | tf_op jit(solution)/shard_map/queries_keys_values/pallas_call | solution.py:583
  101.9 4.5 collective-permute-start
  106.4 5.6 slice.52.refs_5_
  112.1 0.8 copy.40.seg_col
  112.9 0.7 copy.39
  113.6 7.4 %collective-permute-done.prior = bf16[128,2560]{1,0:T(8,128)(2,1)S(1)} collective-permute-done((bf16[128,2560]{1,0:T(8,128)(2,1)}, bf16[128,2560]{1,0:T(8,128)(2,1)S(1)}, u32[]{:S(2)}, u32[]{:S(2)}) %collective-permute-start) | collective-permute-done | bytes 655392 | tf_op jit(solution)/shard_map/ppermute | solution.py:1094
  121.0 0.9 copy-done.8
  121.9 5.6 %attend.1 = (bf16[128,1280]{1,0:T(8,128)(2,1)}, f32[128,1280]{1,0:T(8,128)}, bf16[128,1280]{1,0:T(8,128)(2,1)}, f32[128,128]{1,0:T(8,128)}, f32[128,128]{1,0:T(8,128)}) custom-call(bf16[128,1280]{1,0:T(8,128)(2,1)} %bitcast.54, bf16[128,1280]{1,0:T(8,128)(2,1)} %get-tuple-element.68.q, bf16[128,2560]{1,0:T(8,128)(2,1)} %get-tuple-element.69.kv, ...), custom_call_target="tpu_custom_call" | custom-call | tf_op jit(solution)/shard_map/attend/pallas_call | solution.py:665
  127.5 1.0 copy-done.1
  128.5 0.8 copy-done.6
  129.3 0.8 copy-done.7
  130.2 3.3 dispatch.1
  133.5 1.5 copy-done.3
  135.0 1.5 copy-done.4
  136.5 0.9 copy-done.5
  137.3 81.6 %exchange_rows.2 = (bf16[4,4,4,16,1280]{4,3,2,1,0:T(8,128)(2,1)}, bf16[4,4,4,16,1280]{4,3,2,1,0:T(8,128)(2,1)}, f32[4,4,4,1,2688]{4,3,2,1,0:T(1,128)}, f32[128,1...) custom-call(bf16[4,4,4,16,1280]{4,3,2,1,0:T(8,128)(2,1)} %bitcast.40, ...), custom_call_target="tpu_custom_call" | custom-call | tf_op jit(solution)/shard_map/exchange_rows/pallas_call | solution.py:471
  218.9 23.2 %expert.1 = (bf16[64,16,1280]{2,1,0:T(8,128)(2,1)}, bf16[64,16,1280]{2,1,0:T(8,128)(2,1)}, f32[64,1,2560]{2,1,0:T(1,128)}, bf16[1088,1280]{1,0:T(8,128)(2,1)}, b...) custom-call(bf16[64,16,1280]{2,1,0:T(8,128)(2,1)} %bitcast.62, ...), custom_call_target="tpu_custom_call" | custom-call | tf_op jit(solution)/shard_map/expert/pallas_call | solution.py:779
  242.1 82.1 %exchange_rows.3 = (bf16[4,4,4,16,1280]{4,3,2,1,0:T(8,128)(2,1)}, bf16[4,4,4,16,1280]{4,3,2,1,0:T(8,128)(2,1)}, f32[4,4,4,1,2560]{4,3,2,1,0:T(1,128)}, bf16[1280...) custom-call(bf16[4,4,4,16,1280]{4,3,2,1,0:T(8,128)(2,1)} %bitcast.58, ...), custom_call_target="tpu_custom_call" | custom-call | tf_op jit(solution)/shard_map/exchange_rows/pallas_call | solution.py:471
  324.2 10.2 %combine.1 = (bf16[128,1280]{1,0:T(8,128)(2,1)}, f32[128,1280]{1,0:T(8,128)}, bf16[128,1280]{1,0:T(8,128)(2,1)}, bf16[128,1280]{1,0:T(8,128)(2,1)}, bf16[128,128]{1,0:T(8,128)(2,1)}, /*index=5*/f32[1,1280]{1,0:T(1,128)}) custom-call(bf16[64,16,1280]{2,1,0:T(8,128)(2,1)} %bitcast.56, bf16[64,16,1280]{2,1,0:T(8,128)(2,1)} %bitcast.57, ...), custom_call_target="tpu_custom_call" | custom-call | tf_op jit(solution)/shard_map/combine/pallas_call | solution.py:911
  334.4 7.3 %attend_back.1 = (bf16[128,1280]{1,0:T(8,128)(2,1)}, f32[128,2560]{1,0:T(8,128)}, bf16[128,2560]{1,0:T(8,128)(2,1)}) custom-call(bf16[128,1280]{1,0:T(8,128)(2,1)} %get-tuple-element.68.q, bf16[128,2560]{1,0:T(8,128)(2,1)} %get-tuple-element.69.kv, bf16[128,2560]{1,0:T(8,128)(2,1)} %copy-done.8, s32[1,256]{1,0:T(1,128)} %seg_row.3, s32[256,1]{1,0:T(8,128)} %copy.40.seg_col, ...), custom_call_target="tpu_custom_call" | custom-call | tf_op jit(solution)/shard_map/attend_back/pallas_call | solution.py:512
  341.8 1.3 collective-permute-start.1
  343.1 19.4 %collective-permute-done.1.later = bf16[128,2560]{1,0:T(8,128)(2,1)S(1)} collective-permute-done((bf16[128,2560]{1,0:T(8,128)(2,1)}, bf16[128,2560]{1,0:T(8,128)(2,1)S(1)}, u32[]{:S(2)}, u32[]{:S(2)}) %collective-permute-start.1) | collective-permute-done | bytes 655392 | tf_op jit(solution)/shard_map/ppermute | solution.py:1125
  362.5 3.0 collective-permute-start.3
  365.5 10.4 %input_grads.1 = (bf16[128,3840]{1,0:T(8,128)(2,1)}, f32[128,1280]{1,0:T(8,128)}, f32[1,1280]{1,0:T(1,128)}) custom-call(bf16[128,1280]{1,0:T(8,128)(2,1)} %bitcast.55, bf16[1280,7424]{1,0:T(8,128)(2,1)} %bitcast.50, f32[256,128]{1,0:T(8,128)} %constant.21.clone.cos, f32[256,128]{1,0:T(8,128)} %constant.22.clone.sin, ...), custom_call_target="tpu_custom_call" | custom-call | tf_op jit(solution)/shard_map/input_grads/pallas_call | solution.py:982
  375.9 21.0 %weight_grads.1 = bf16[1280,7424]{1,0:T(8,128)(2,1)} custom-call(bf16[128,1280]{1,0:T(8,128)(2,1)} %get-tuple-element.105.act_attn, bf16[128,1280]{1,0:T(8,128)(2,1)} %get-tuple-element.106.mixed, bf16[128,1280]{1,0:T(8,128)(2,1)} %get-tuple-element.70.act.refs_3_.act_ffn, bf16[128,3840]{1,0:T(8,128)(2,1)} %get-tuple-element.107.grad_qkv, ...), custom_call_target="tpu_custom_call" | custom-call | tf_op jit(solution)/shard_map/weight_grads/pallas_call | solution.py:1035
  397.0 140.8 %scatter_sums.1 = (f32[32,7424]{1,0:T(8,128)}, f32[16,1280]{1,0:T(8,128)}) custom-call(bf16[4,4,80,7424]{3,2,1,0:T(8,128)(2,1)} %bitcast.52, bf16[4,4,64,1280]{3,2,1,0:T(8,128)(2,1)} %bitcast.64), custom_call_target="tpu_custom_call" | custom-call | tf_op jit(solution)/shard_map/scatter_sums/pallas_call | solution.py:397
  537.8 1.1 fusion
  538.9 0.2 reshape.126
  539.1 1.0 reshape.127
  540.1 0.2 reshape.128
  540.3 1.0 reshape.129
  541.3 1.4 dynamic-slice.6
  542.7 1.5 dynamic-slice_reduce_fusion
  544.2 2.0 fusion.1
  546.3 5.0 add_bitcast_fusion
  551.2 4.9 add_bitcast_fusion.1
  556.2 4.3 add_bitcast_fusion.2
  560.4 0.6 copy.44
  (46 shorter events, 0.3 us)
Async XLA Ops:
  0.7 4.1 copy-start.20
  0.7 4.2 copy-start.21
  0.7 4.3 copy-start.16
  0.7 4.4 copy-start.12
  0.7 4.4 copy-start.13
  0.7 4.4 copy-start.14
  0.7 4.4 copy-start.15
  0.7 4.4 copy-start.18
  92.2 1.5 copy-start.2
  101.9 10.2 %copy-start.17 = (s32[1,256]{1,0:T(1,128)S(1)}, s32[1,256]{1,0:T(1,128)}, u32[]{:S(2)}) copy-start(s32[1,256]{1,0:T(1,128)} %seg_row.3) | copy-start | bytes 3076
  101.9 11.0 %copy-start.19 = (s32[1,128,7]{1,0,2:T(1,128)S(1)}, s32[1,128,7]{1,0,2:T(1,128)}, u32[]{:S(2)}) copy-start(s32[1,128,7]{1,0,2:T(1,128)} %param.22) | copy-start | bytes 10756
  101.9 19.1 %collective-permute-start = (bf16[128,2560]{1,0:T(8,128)(2,1)}, bf16[128,2560]{1,0:T(8,128)(2,1)S(1)}, u32[]{:S(2)}, u32[]{:S(2)}) collective-permute-start(bf16[128,2560]{1,0:T(8,128)(2,1)} %get-tuple-element.69.kv), channel_id=1, source_target_pairs={{0,64},{1,65},{2,66},{3,67},{4,68},{5,69},{6,70},{7,71},{8,72},{9,... | collective-permute-start | bytes 1966088 | tf_op jit(solution)/shard_map/ppermute | solution.py:1094
  121.0 0.9 copy-start.8
  121.8 5.7 %copy-start = (bf16[1,128,1280]{2,1,0:T(8,128)(2,1)S(1)}, bf16[1,128,1280]{2,1,0:T(8,128)(2,1)}, u32[]{:S(2)}) copy-start(bf16[1,128,1280]{2,1,0:T(8,128)(2,1)} %param.20) | copy-start | bytes 983044
  127.5 1.0 copy-start.1
  128.5 0.8 copy-start.6
  129.3 0.8 copy-start.7
  133.5 1.5 copy-start.3
  135.0 1.5 copy-start.4
  136.5 0.9 copy-start.5
  324.2 41.3 %copy-start.9 = (bf16[1280,896]{1,0:T(8,128)(2,1)S(1)}, bf16[1280,896]{1,0:T(8,128)(2,1)}, u32[]{:S(2)}) copy-start(bf16[1280,896]{1,0:T(8,128)(2,1)} %get-tuple-element.116) | copy-start | bytes 6881284
  341.8 20.7 %collective-permute-start.1 = (bf16[128,2560]{1,0:T(8,128)(2,1)}, bf16[128,2560]{1,0:T(8,128)(2,1)S(1)}, u32[]{:S(2)}, u32[]{:S(2)}) collective-permute-start(bf16[128,2560]{1,0:T(8,128)(2,1)} %get-tuple-element.101), channel_id=1, source_target_pairs={{64,0},{65,1},{66,2},{67,3},{68,4},{69,5},{70,6},{71,7},{72,8},{73... | collective-permute-start | bytes 1966088 | tf_op jit(solution)/shard_map/ppermute | solution.py:1125
  362.5 3.0 copy-start.10
  362.5 183.7 %collective-permute-start.4 = (bf16[896,1280]{1,0:T(8,128)(2,1)}, bf16[896,1280]{1,0:T(8,128)(2,1)}, u32[]{:S(2)}, u32[]{:S(2)}) collective-permute-start(bf16[896,1280]{1,0:T(8,128)(2,1)} %get-tuple-element.118), channel_id=1, source_target_pairs={{0,64},{64,0},{1,65},{65,1},{2,66},{66,2},{3,67},{67,3},{4,68},{68... | collective-permute-start | bytes 6881288 | tf_op jit(solution)/shard_map/ppermute | solution.py:1127
  362.5 188.7 %collective-permute-start.3 = (bf16[1280,896]{1,0:T(8,128)(2,1)}, bf16[1280,896]{1,0:T(8,128)(2,1)}, u32[]{:S(2)}, u32[]{:S(2)}) collective-permute-start(bf16[1280,896]{1,0:T(8,128)(2,1)} %get-tuple-element.117), channel_id=1, source_target_pairs={{0,64},{64,0},{1,65},{65,1},{2,66},{66,2},{3,67},{67,3},{4,68},{68... | collective-permute-start | bytes 6881288 | tf_op jit(solution)/shard_map/ppermute | solution.py:1127
  365.5 190.7 %collective-permute-start.2 = (bf16[1280,896]{1,0:T(8,128)(2,1)S(1)}, bf16[1280,896]{1,0:T(8,128)(2,1)}, u32[]{:S(2)}, u32[]{:S(2)}) collective-permute-start(bf16[1280,896]{1,0:T(8,128)(2,1)S(1)} %copy-done.9), channel_id=1, source_target_pairs={{0,64},{64,0},{1,65},{65,1},{2,66},{66,2},{3,67},{67,3},{4,68},{68... | collective-permute-start | bytes 6881288 | tf_op jit(solution)/shard_map/ppermute | solution.py:1127
  556.1 4.3 copy-start.11

commit v3 on v2

--- a/solution.py
+++ b/solution.py
@@ -105,7 +105,7 @@
     )
 
 
-def gather_kernel(win, sdw, out, osd, wsib, pw, pwx, blk, bsd, ssem, rsem, lsem):
+def gather_kernel(win, sdw, e0, e1, e2, out, osd, o0, o1, o2, wsib, pw, pwx, blk, bsd, ssem, rsem, lsem, esend, erecv, ekeep):
     hi, y, z, lo, c = place()
     sib = device(hi, y, z, lo, 1 - c)
     xn = device(hi, y, z, 1 - lo, c)
@@ -114,6 +114,29 @@
     wires = Sender(ssem, rsem, lsem)
     mul = pl.multiple_of
     j = lo * 2 + c
+    owner = c == hi
+
+    mine_e, used_e = (e0, e1, e2), (o0, o1, o2)
+
+    def keep_expert(k):
+        return pltpu.make_async_copy(mine_e[k], used_e[k], ekeep.at[k])
+
+    def pass_expert(k):
+        return pltpu.make_async_remote_copy(
+            src_ref=mine_e[k],
+            dst_ref=used_e[k],
+            send_sem=esend.at[k],
+            recv_sem=erecv.at[k],
+            device_id=sib,
+            device_id_type=MESH,
+        )
+
+    @pl.when(owner)
+    def _():
+        for k in range(3):
+            keep_expert(k).start()
+            pass_expert(k).start()
+
     other = pl.ds(mul((1 - c) * HALF, 128), HALF)
     mine = pl.ds(mul(c * HALF, 128), HALF)
     other2 = pl.ds(mul((1 - c) * 640, 128), 640)
@@ -217,20 +240,32 @@
     for copy in keep:
         copy.wait()
 
-
-def gather_weights(shard, down):
+    @pl.when(owner)
+    def _():
+        for k in range(3):
+            keep_expert(k).wait()
+            pass_expert(k).wait_send()
+
+    @pl.when(jnp.logical_not(owner))
+    def _():
+        for k in range(3):
+            pass_expert(k).wait_recv()
+
+
+def gather_weights(shard, down, experts):
     offset = 4 * lax.rem(lax.axis_index("exp"), 4)
     window = lax.dynamic_update_slice(jnp.zeros((32, WIDE * 128), BF16), shard, (offset, 0))
     down = jnp.pad(down, ((0, 2), (0, 0)))
     sems = 4 + 2 * 2 * 36
-    out, osd = pl.pallas_call(
+    out, osd, *mine = pl.pallas_call(
         gather_kernel,
         out_shape=(
             jax.ShapeDtypeStruct((4, 4, 80, WIDE * 128), BF16),
             jax.ShapeDtypeStruct((4, 4, 64, 1280), BF16),
+            *(jax.ShapeDtypeStruct(w.shape, BF16) for w in experts),
         ),
-        in_specs=[pl.BlockSpec(memory_space=pltpu.VMEM)] * 2,
-        out_specs=(pl.BlockSpec(memory_space=pl.ANY),) * 2,
+        in_specs=[pl.BlockSpec(memory_space=pltpu.VMEM)] * 2 + [pl.BlockSpec(memory_space=pl.ANY)] * 3,
+        out_specs=(pl.BlockSpec(memory_space=pl.ANY),) * 5,
         scratch_shapes=[
             pltpu.VMEM((32, HALF), BF16),
             pltpu.VMEM((48, HALF), BF16),
@@ -240,28 +275,64 @@
             pltpu.SemaphoreType.DMA((sems,)),
             pltpu.SemaphoreType.DMA((sems,)),
             pltpu.SemaphoreType.DMA((2,)),
-        ],
+        ]
+        + [pltpu.SemaphoreType.DMA((3,))] * 3,
         compiler_params=pltpu.CompilerParams(
             collective_id=1, has_side_effects=True, vmem_limit_bytes=40 << 20
         ),
         name="gather_weights",
-    )(window, down)
-    return out.reshape(1280, WIDE * 128), osd.reshape(1024, 1280)
-
-
-def scatter_kernel(gw, gsd, out, osd, *scratch):
+    )(window, down, *experts)
+    return out.reshape(1280, WIDE * 128), osd.reshape(1024, 1280), mine
+
+
+def scatter_kernel(gw, gsd, p0, p1, p2, out, osd, t0, t1, t2, *scratch):
     hold = [scratch[0:2], scratch[2:4]]
     from_sib = [scratch[4:6], scratch[6:8]]
     bufs = [[scratch[8 + 8 * u + 4 * a : 12 + 8 * u + 4 * a] for a in (0, 1)] for u in (0, 1)]
-    fin, fsd, wx, wxd, wh, whd, snd, sndd, acc, accd, ssem, rsem, lsem = scratch[24:]
+    fin, fsd, wx, wxd, wh, whd, snd, sndd, acc, accd, ssem, rsem, lsem = scratch[24:37]
+    part_own, part_sib, esend, erecv, ekeep = scratch[37:40], scratch[40:43], *scratch[43:]
     hi, y, z, lo, c = place()
     sib = device(hi, y, z, lo, 1 - c)
     xn = device(hi, y, z, 1 - lo, c)
     hn = device(1 - hi, y, z, lo, c)
     nb = ring_neighbours(hi, y, z, lo, c)
-    greet([sib, xn, hn] + list(nb.values()))
+    across = device(1 - hi, y, z, lo, hi)
+    greet([sib, xn, hn, device(1 - hi, y, z, lo, 1 - c)] + list(nb.values()))
     wires = Sender(ssem, rsem, lsem)
     mul = pl.multiple_of
+    owner = c == hi
+    parts, totals = (p0, p1, p2), (t0, t1, t2)
+
+    def remote(src, dst, k, tag, to):
+        return pltpu.make_async_remote_copy(
+            src_ref=src, dst_ref=dst, send_sem=esend.at[k], recv_sem=erecv.at[tag], device_id=to, device_id_type=MESH
+        )
+
+    def rows_of(ref, core):
+        half_rows = ref.shape[0] // 2
+        return ref.at[pl.ds(mul(core * half_rows, 16), half_rows)]
+
+    def own_part(k):
+        return pltpu.make_async_copy(rows_of(parts[k], c), part_own[k], ekeep.at[k])
+
+    def swap_part(k):
+        return remote(rows_of(parts[k], 1 - c), part_sib[k], k, k, sib)
+
+    def send_across(k):
+        return remote(part_own[k], rows_of(totals[k], c), 3 + k, 3 + 2 * k + c, across)
+
+    def keep_total(k):
+        return pltpu.make_async_copy(part_own[k], rows_of(totals[k], c), ekeep.at[3 + k])
+
+    def send_near(k):
+        return remote(part_own[k], rows_of(totals[k], c), 6 + k, 3 + 2 * k + c, sib)
+
+    def total_half(k, core):
+        return remote(rows_of(totals[k], core), rows_of(totals[k], core), 9 + k, 3 + 2 * k + core, sib)
+
+    for k in range(3):
+        own_part(k).start()
+        swap_part(k).start()
     first_pos, second_pos = (y, z), (z, y)
     first_axis, second_axis = ("y", "z"), ("z", "y")
 
@@ -316,6 +387,20 @@
 
     ring = {}
 
+    def add_parts(k):
+        own_part(k).wait()
+        swap_part(k).wait_recv()
+        add_in(part_own[k], part_sib[k])
+        send_across(k).start()
+
+        @pl.when(owner)
+        def _():
+            keep_total(k).start()
+
+        @pl.when(jnp.logical_not(owner))
+        def _():
+            send_near(k).start()
+
     def far_block(u, slot, blk, axis):
         ring[u, slot, 0] = pair(half(blk, u, 0), buffer(u, 0, slot), nb[axis, 1])
         ring[u, slot, 1] = pair(half(blk, u, 1), buffer(u, 1, slot), nb[axis, -1])
@@ -336,6 +421,8 @@
     for i in range(4):
         for u in (0, 1):
             far_block(u, i, ready(u, i), second_axis[u])
+        if i > 0:
+            add_parts(i - 1)
     for i in range(4):
         for u in (0, 1):
             near_block(u, i, ready(u, 4 + i), second_axis[u], 1)
@@ -373,10 +460,24 @@
     out[:, mine] = acc[pl.ds(r, 32), :]
     osd[:, mine2] = accd[pl.ds(r, 16), :]
     arrived(last)
+    for k in range(3):
+        swap_part(k).wait_send()
+        send_across(k).wait_send()
+        total_half(k, 1 - c).wait_recv()
+
+        @pl.when(owner)
+        def _(k=k):
+            keep_total(k).wait()
+
+        @pl.when(jnp.logical_not(owner))
+        def _(k=k):
+            send_near(k).wait_send()
+            total_half(k, c).wait_recv()
+
     wires.finish()
 
 
-def scatter_sums(gw, gsd):
+def scatter_sums(gw, gsd, parts):
     scratch = []
     for _ in (0, 1):
         for s, w, w0, s2, v, v0 in UNITS:
@@ -394,48 +495,105 @@
         pltpu.SemaphoreType.DMA((sems,)),
         pltpu.SemaphoreType.DMA((64,)),
     ]
-    out, osd = pl.pallas_call(
+    scratch += [pltpu.VMEM((p.shape[0] // 2, p.shape[1]), BF16) for p in parts] * 2
+    scratch += [pltpu.SemaphoreType.DMA((12,)), pltpu.SemaphoreType.DMA((9,)), pltpu.SemaphoreType.DMA((6,))]
+    out, osd, *totals = pl.pallas_call(
         scatter_kernel,
-        out_shape=(jax.ShapeDtypeStruct((32, WIDE * 128), F32), jax.ShapeDtypeStruct((16, 1280), F32)),
-        in_specs=[pl.BlockSpec(memory_space=pl.ANY)] * 2,
-        out_specs=(pl.BlockSpec(memory_space=pltpu.VMEM),) * 2,
+        out_shape=(
+            jax.ShapeDtypeStruct((32, WIDE * 128), F32),
+            jax.ShapeDtypeStruct((16, 1280), F32),
+            *(jax.ShapeDtypeStruct(p.shape, BF16) for p in parts),
+        ),
+        in_specs=[pl.BlockSpec(memory_space=pl.ANY)] * 5,
+        out_specs=(pl.BlockSpec(memory_space=pltpu.VMEM),) * 2 + (pl.BlockSpec(memory_space=pl.ANY),) * 3,
         scratch_shapes=scratch,
         compiler_params=pltpu.CompilerParams(
             collective_id=2, has_side_effects=True, vmem_limit_bytes=56 << 20
         ),
         name="scatter_sums",
-    )(gw.reshape(4, 4, 80, WIDE * 128), gsd.reshape(4, 4, 64, 1280))
+    )(gw.reshape(4, 4, 80, WIDE * 128), gsd.reshape(4, 4, 64, 1280), *parts)
     offset = 4 * lax.rem(lax.axis_index("exp"), 4)
-    return lax.dynamic_slice(out, (offset, 0), (20, WIDE * 128)), osd[:14]
-
-
-PART_AXES = (("y", "z", "g"), ("z", "g", "y"), ("g", "y", "z"))
-
-
-def exchange_kernel(cuts, work, counts, *refs):
+    return lax.dynamic_slice(out, (offset, 0), (20, WIDE * 128)), osd[:14], totals
+
+
+PART_AXES = (("y", "z", "g"), ("z", "g", "y"), ("g", "y", "z")) * 2
+PARTS = len(PART_AXES)
+
+
+def lane_cuts(*sizes):
+    return tuple((sum(sizes[:i]), n) for i, n in enumerate(sizes))
+
+
+ROW_CUTS = lane_cuts(4, 4, 3, 3, 3, 3)
+LAST_OUT_CUTS = lane_cuts(3, 3, 3, 3, 4, 5)
+LAST_BACK_CUTS = lane_cuts(3, 3, 3, 3, 4, 4)
+
+
+def exchange_kernel(cuts, outward, work, counts, *refs):
     n = len(cuts)
     n_in, n_out, n_scratch = counts
     work_in, refs = refs[n : n + n_in], refs[:n] + refs[n + n_in :]
     work_out, refs = refs[2 * n : 2 * n + n_out], refs[: 2 * n] + refs[2 * n + n_out :]
     work_scratch = refs[4 * n + 3 :]
     stages = [refs[0:n], refs[2 * n : 3 * n], refs[3 * n : 4 * n], refs[n : 2 * n]]
+    ssem, rsem, lsem = refs[4 * n : 4 * n + 3]
     hi, y, z, lo, c = place()
-    me = {"y": y, "z": z, "g": lo * 2 + c}
-    wires = Sender(*refs[4 * n : 4 * n + 3])
-
-    def peer(axis, k):
+    me = {"y": y, "z": z}
+
+    def along(axis, k):
         q = dict(me)
         q[axis] = lax.rem(me[axis] + k, 4)
-        return q[axis], device(hi, q["y"], q["z"], q["g"] // 2, lax.rem(q["g"], 2))
-
-    greet([peer(axis, k)[1] for axis in "yzg" for k in (1, 2, 3)])
+        return q[axis], device(hi, q["y"], q["z"], lo, c)
+
+    hi_or, c_or, lo_or = (hi, 1 - hi), (c, 1 - c), (lo, 1 - lo)
+
+    def target(d, b):
+        if outward:
+            return device(hi_or[b], y, z, lo_or[d], hi), lo_or[d] * 2 + hi_or[b], lo * 2 + c, 2 * d + c
+        return device(c, y, z, lo_or[d], c_or[b]), lo_or[d] * 2 + c_or[b], lo * 2 + hi, 2 * d + hi
+
+    def source(d, b):
+        if outward:
+            return device(c, y, z, lo_or[d], c_or[b]), lo_or[d] * 2 + c_or[b], 2 * d + c_or[b]
+        return device(hi_or[b], y, z, lo_or[d], hi), lo_or[d] * 2 + hi_or[b], 2 * d + hi_or[b]
+
+    corners = ((1, 1), (0, 1), (1, 0))
+    stays = c == hi
+    moves = jnp.logical_not(stays)
+    bar = pltpu.get_barrier_semaphore()
+
+    def greet_one(to):
+        pl.semaphore_signal(bar, inc=1, device_id=to, device_id_type=MESH)
+
+    for axis in "yz":
+        for k in (1, 2, 3):
+            greet_one(along(axis, k)[1])
+    for corner in corners:
+        greet_one(source(*corner)[0])
+
+    @pl.when(moves)
+    def _():
+        greet_one(source(0, 0)[0])
+        pl.semaphore_wait(bar, 10)
+
+    @pl.when(stays)
+    def _():
+        pl.semaphore_wait(bar, 9)
+
     every = slice(None)
 
     def view(ref, axis, v, lanes):
         index = {"y": (v, every, every), "z": (every, v, every), "g": (every, every, v)}[axis]
         return ref.at[index + (every, pl.ds(lanes[0] * 128, lanes[1] * 128))]
 
+    def remote(src, dst, k, tag, to):
+        return pltpu.make_async_remote_copy(
+            src_ref=src, dst_ref=dst, send_sem=ssem.at[k], recv_sem=rsem.at[tag], device_id=to, device_id_type=MESH
+        )
+
     pending = {}
+    sent = []
+    used = [0, 0]
 
     def go(part, phase):
         axis = PART_AXES[part][phase]
@@ -443,41 +601,91 @@
         for a in range(n):
             src, dst = stages[phase][a], stages[phase + 1][a]
             lanes = cuts[a][part]
-            own = view(dst, axis, me[axis], lanes)
-            for k in (2, 1, 3):
-                v, to = peer(axis, k)
-                waits.append(wires.remote(view(src, axis, v, lanes), own, to).wait_recv)
-            waits.append(wires.local(view(src, axis, me[axis], lanes), own).wait)
+            base, kept = used
+            used[0] += 4
+            used[1] += 1
+            if axis != "g":
+                own = view(dst, axis, me[axis], lanes)
+                for k in (2, 1, 3):
+                    v, to = along(axis, k)
+                    copy = remote(view(src, axis, v, lanes), own, base + k, base + k, to)
+                    copy.start()
+                    waits.append(copy.wait_recv)
+                    sent.append(copy.wait_send)
+                keep = pltpu.make_async_copy(view(src, axis, me[axis], lanes), own, lsem.at[kept])
+                keep.start()
+                waits.append(keep.wait)
+                continue
+            for d, b in corners:
+                to, there, here, tag = target(d, b)
+                copy = remote(view(src, axis, there, lanes), view(dst, axis, here, lanes), base + 2 * d + b, base + tag, to)
+                copy.start()
+                sent.append(copy.wait_send)
+                _from, place_, tag = source(d, b)
+                block = view(dst, axis, place_, lanes)
+                waits.append(remote(block, block, base + 2 * d + b, base + tag, _from).wait_recv)
+            to, there, here, tag = target(0, 0)
+            keep = pltpu.make_async_copy(view(src, axis, there, lanes), view(dst, axis, here, lanes), lsem.at[kept])
+            copy = remote(view(src, axis, there, lanes), view(dst, axis, here, lanes), base, base + tag, to)
+            _from, place_, tag = source(0, 0)
+            block = view(dst, axis, place_, lanes)
+            coming = remote(block, block, base, base + tag, _from)
+
+            @pl.when(stays)
+            def _(keep=keep):
+                keep.start()
+
+            @pl.when(moves)
+            def _(copy=copy):
+                copy.start()
+
+            def wait_corner(keep=keep, coming=coming):
+                @pl.when(stays)
+                def _():
+                    keep.wait()
+
+                @pl.when(moves)
+                def _():
+                    coming.wait_recv()
+
+            def wait_sent(copy=copy):
+                @pl.when(moves)
+                def _():
+                    copy.wait_send()
+
+            waits.append(wait_corner)
+            sent.append(wait_sent)
         pending[part, phase] = waits
 
     for phase in (0, 1, 2):
-        for part in range(3):
+        for part in range(PARTS):
             if phase > 0:
                 for wait in pending[part, phase - 1]:
                     wait()
             go(part, phase)
         work(phase, work_in, work_out, work_scratch)
-    for part in range(3):
+    for part in range(PARTS):
         for wait in pending[part, 2]:
             wait()
-    wires.finish()
-
-
-def exchange(collective_id, arrays, cuts, work, work_in, work_out, work_scratch=()):
+    for wait in sent:
+        wait()
+
+
+def exchange(collective_id, outward, arrays, cuts, work, work_in, work_out, work_scratch=()):
     n = len(arrays)
     split = [a.reshape((4, 4, 4) + a.shape[1:]) for a in arrays]
     shapes = [jax.ShapeDtypeStruct(a.shape, a.dtype) for a in split]
     vmem = pl.BlockSpec(memory_space=pltpu.VMEM)
     out = pl.pallas_call(
-        functools.partial(exchange_kernel, cuts, work, (len(work_in), len(work_out), len(work_scratch))),
+        functools.partial(exchange_kernel, cuts, outward, work, (len(work_in), len(work_out), len(work_scratch))),
         out_shape=tuple(shapes) + tuple(work_out),
         in_specs=[pl.BlockSpec(memory_space=pl.ANY)] * n + [vmem] * len(work_in),
         out_specs=(pl.BlockSpec(memory_space=pl.ANY),) * n + (vmem,) * len(work_out),
         scratch_shapes=[pltpu.VMEM(s.shape, s.dtype) for s in shapes] * 2
         + [
-            pltpu.SemaphoreType.DMA((27 * n,)),
-            pltpu.SemaphoreType.DMA((27 * n,)),
-            pltpu.SemaphoreType.DMA((9 * n,)),
+            pltpu.SemaphoreType.DMA((12 * PARTS * n,)),
+            pltpu.SemaphoreType.DMA((12 * PARTS * n,)),
+            pltpu.SemaphoreType.DMA((3 * PARTS * n,)),
         ]
         + list(work_scratch),
         compiler_params=pltpu.CompilerParams(
@@ -684,9 +892,9 @@
     return wide == place_of
 
 
-def dispatch_kernel(act, grad, gates, slot_t, out_x, out_g, out_l):
-    block, even, width = out_x.shape
-    rows = act.shape[0]
+def dispatch_kernel(act, grad, gates, slot_t, out_r, out_l):
+    block, even, _lanes = out_r.shape
+    rows, width = act.shape
     here = pl.ds(pl.multiple_of(pl.program_id(0) * block, block), block)
     slots = slot_t[here, :]
     places = even_places(slots)
@@ -694,8 +902,8 @@
     hot = places.astype(F32).reshape(block * even, rows).astype(BF16)
     last_hot = last.astype(BF16)
     x, g = act[...], grad[...]
-    out_x[...] = dot(hot, x).astype(BF16).reshape(block, even, width)
-    out_g[...] = dot(hot, g).astype(BF16).reshape(block, even, width)
+    out_r[:, :, :width] = dot(hot, x).astype(BF16).reshape(block, even, width)
+    out_r[:, :, width:] = dot(hot, g).astype(BF16).reshape(block, even, width)
     gt = gates[here, :]
     at_slot = jnp.sum(
         jnp.where(places, jnp.broadcast_to(gt[:, None, :], places.shape), 0.0).reshape(block * even, rows),
@@ -721,25 +929,24 @@
         dispatch_kernel,
         grid=(experts // block,),
         out_shape=(
-            shape(BF16, experts, EVEN, width),
-            shape(BF16, experts, EVEN, width),
+            shape(BF16, experts, EVEN, 2 * width),
             shape(F32, experts, 1, 2 * width + 128),
         ),
         in_specs=[whole(act), whole(grad), whole(gates_t), whole(slot_t)],
-        out_specs=(cut(EVEN, width), cut(EVEN, width), cut(1, 2 * width + 128)),
+        out_specs=(cut(EVEN, 2 * width), cut(1, 2 * width + 128)),
         compiler_params=pltpu.CompilerParams(vmem_limit_bytes=32 << 20),
         name="dispatch",
     )(act, grad, gates_t, slot_t)
 
 
-def expert_kernel(rows_x, rows_g, rows_l, w_gate, w_up, w_down, out_r, out_d, out_l, all_x, all_g, hidden, d_gate, d_up):
+def expert_kernel(rows_r, rows_l, w_gate, w_up, w_down, out_r, out_l, all_x, all_g, hidden, d_gate, d_up):
     sources, _one, _lanes = rows_l.shape
-    width = rows_x.shape[-1]
+    width = rows_r.shape[-1] // 2
     last = rows_l[...].reshape(sources, rows_l.shape[-1])
     even = sources * EVEN
-    x = jnp.concatenate([rows_x[...].reshape(even, width), last[:, :width].astype(BF16)], axis=0)
+    x = jnp.concatenate([rows_r[:, :, :width].reshape(even, width), last[:, :width].astype(BF16)], axis=0)
     g = jnp.concatenate(
-        [rows_g[...].reshape(even, width).astype(F32), last[:, width : 2 * width]], axis=0
+        [rows_r[:, :, width:].reshape(even, width).astype(F32), last[:, width : 2 * width]], axis=0
     )
     sent = last[:, 2 * width :]
     spread = jnp.broadcast_to(sent[:, None, :], (sources, EVEN, 128))
@@ -761,13 +968,14 @@
     d_up[...] = grad_up
     result = dot(low, w_down[...]).astype(BF16)
     grad_in = (dot_t(grad_gate, w_gate[...]) + dot_t(grad_up, w_up[...])).astype(BF16)
-    out_r[...] = result[:even].reshape(sources, EVEN, width)
-    out_d[...] = grad_in[:even].reshape(sources, EVEN, width)
+    out_r[:, :, :width] = result[:even].reshape(sources, EVEN, width)
+    out_r[:, :, width:] = grad_in[:even].reshape(sources, EVEN, width)
     out_l[...] = jnp.concatenate([result[even:], grad_in[even:]], axis=1).astype(F32).reshape(sources, 1, 2 * width)
 
 
-def expert(rows_x, rows_g, rows_l, w_gate, w_up, w_down):
-    devices, _even, width = rows_x.shape
+def expert(rows_r, rows_l, w_gate, w_up, w_down):
+    devices, _even, width = rows_r.shape
+    width = width // 2
     inner = w_gate.shape[1]
     steps = 4
     src = devices // steps
@@ -780,8 +988,7 @@
         expert_kernel,
         grid=(steps,),
         out_shape=(
-            shape(BF16, devices, EVEN, width),
-            shape(BF16, devices, EVEN, width),
+            shape(BF16, devices, EVEN, 2 * width),
             shape(F32, devices, 1, 2 * width),
             shape(BF16, total, width),
             shape(BF16, total, width),
@@ -789,10 +996,9 @@
             shape(BF16, total, inner),
             shape(BF16, total, inner),
         ),
-        in_specs=[cut(EVEN, width), cut(EVEN, width), cut(1, rows_l.shape[-1]), whole(w_gate), whole(w_up), whole(w_down)],
+        in_specs=[cut(EVEN, 2 * width), cut(1, rows_l.shape[-1]), whole(w_gate), whole(w_up), whole(w_down)],
         out_specs=(
-            cut(EVEN, width),
-            cut(EVEN, width),
+            cut(EVEN, 2 * width),
             cut(1, 2 * width),
             flat(width),
             flat(width),
@@ -802,7 +1008,7 @@
         ),
         compiler_params=pltpu.CompilerParams(vmem_limit_bytes=60 << 20),
         name="expert",
-    )(rows_x, rows_g, rows_l, w_gate, w_up, w_down)
+    )(rows_r, rows_l, w_gate, w_up, w_down)
 
 
 def shared_work(phase, ins, outs, scratch):
@@ -856,7 +1062,7 @@
 
 
 def combine_kernel(
-    back_r, back_d, back_l, slot_t, gates_t, grad, hidden_one, out_s, grad_in_s, router_w, out_w,
+    back_r, back_l, slot_t, gates_t, grad, hidden_one, out_s, grad_in_s, router_w, out_w,
     layer_out, grad_hidden, grad_low, grad_mixed, grad_logits, grad_gain,
 ):
     experts = back_r.shape[0]
@@ -864,7 +1070,7 @@
     slots = slot_t[0:experts, :]
     places = even_places(slots)
     last = slots == float(EVEN)
-    out_rows = back_r[...].reshape(experts * EVEN, width)
+    out_rows = back_r[:, :, :width].reshape(experts * EVEN, width)
     last_l = back_l[...].reshape(experts, 2 * width).astype(BF16)
     gt = gates_t[0:experts, :]
     even_w = jnp.where(places, jnp.broadcast_to(gt[:, None, :], places.shape), 0.0).reshape(experts * EVEN, rows)
@@ -882,7 +1088,7 @@
     low_logits = jnp.concatenate([logits_t, jnp.zeros((128 - experts, rows), F32)], axis=0).T.astype(BF16)
     grad_logits[...] = low_logits
     hot = places.astype(F32).reshape(experts * EVEN, rows).astype(BF16)
-    grad_routed = t_dot(hot, back_d[...].reshape(experts * EVEN, width)) + t_dot(last.astype(BF16), last_l[:, width:])
+    grad_routed = t_dot(hot, back_r[:, :, width:].reshape(experts * EVEN, width)) + t_dot(last.astype(BF16), last_l[:, width:])
     router = router_w[...]
     grad_act = grad_routed + dot_t(low_logits, router) + grad_in_s[...]
     gain = gain_rows(router)[1:2]
@@ -896,9 +1102,9 @@
     grad_mixed[...] = dot_t(low, out_w[...]).astype(BF16)
 
 
-def combine(back_r, back_d, back_l, slot_t, gates_t, grad, hidden_one, out_s, grad_in_s, weights):
+def combine(back_r, back_l, slot_t, gates_t, grad, hidden_one, out_s, grad_in_s, weights):
     rows, width = hidden_one.shape
-    operands = (back_r, back_d, back_l, slot_t, gates_t, grad, hidden_one, out_s, grad_in_s)
+    operands = (back_r, back_l, slot_t, gates_t, grad, hidden_one, out_s, grad_in_s)
     whole = lambda a: pl.BlockSpec(a.shape, lambda i: (0,) * len(a.shape))
     outs = (
         shape(BF16, rows, width),
@@ -1088,33 +1294,35 @@
         ],
         axis=1,
     )
-    weights, sdown_w = gather_weights(shard, shared_down)
+    weights, sdown_w, expert_w = gather_weights(shard, shared_down, (expert_gate[0], expert_up[0], expert_down[0]))
     cos, sin = rotary_tables(2 * rows)
     act_attn, q, kv = project(tokens, weights, cos, sin)
     prior = lax.ppermute(kv, "seq", [(0, 1)])
     mixed, hidden_one, act_ffn, gates_t, slot_t = attend(tokens, q, kv, prior, seg_row, seg_col, routes, weights)
 
-    rows_x, rows_g, rows_l = dispatch(act_ffn, grad, gates_t, slot_t, experts)
-    rows_x, rows_g, rows_l, out_s, grad_in_s, grad_gu, grad_sdown = exchange(
+    rows_r, rows_l = dispatch(act_ffn, grad, gates_t, slot_t, experts)
+    rows_r, rows_l, out_s, grad_in_s, grad_gu, grad_sdown = exchange(
         3,
-        (rows_x, rows_g, rows_l),
-        (((0, 4), (4, 3), (7, 3)), ((0, 3), (3, 4), (7, 3)), ((0, 6), (6, 6), (12, 9))),
+        True,
+        (rows_r, rows_l),
+        (ROW_CUTS, LAST_OUT_CUTS),
         shared_work,
         (act_ffn, grad, weights[:, 5120:7168], sdown_w),
         (shape(F32, rows, width), shape(F32, rows, width), shape(BF16, rows, 2048), shape(BF16, 1024, width)),
         (pltpu.VMEM((rows, 1024), BF16),),
     )
-    out_r, out_d, out_l, *kept = expert(rows_x, rows_g, rows_l, expert_gate[0], expert_up[0], expert_down[0])
-    back_r, back_d, back_l, *part_expert = exchange(
+    out_r, out_l, *kept = expert(rows_r, rows_l, *expert_w)
+    back_r, back_l, *part_expert = exchange(
         4,
-        (out_r, out_d, out_l),
-        (((0, 4), (4, 3), (7, 3)), ((0, 3), (3, 4), (7, 3)), ((0, 6), (6, 6), (12, 8))),
+        False,
+        (out_r, out_l),
+        (ROW_CUTS, LAST_BACK_CUTS),
         expert_work,
         tuple(kept),
         tuple(shape(BF16, *w.shape[1:]) for w in (expert_gate, expert_up, expert_down)),
     )
     layer_out, grad_hidden, grad_low, grad_mixed, grad_logits, gain_ffn = combine(
-        back_r, back_d, back_l, slot_t, gates_t, grad, hidden_one, out_s, grad_in_s, weights
+        back_r, back_l, slot_t, gates_t, grad, hidden_one, out_s, grad_in_s, weights
     )
     grad_q, grad_own, grad_prior = local_call(
         attend_back_kernel,
@@ -1123,16 +1331,14 @@
         q, kv, prior, seg_row, seg_col, grad_mixed, cos, sin,
     )
     later = lax.ppermute(grad_prior, "seq", [(1, 0)])
-    *part_expert, later = lax.optimization_barrier((*part_expert, later))
-    swapped = [lax.ppermute(g, "seq", [(0, 1), (1, 0)]) for g in part_expert]
     grad_qkv, grad_tokens, gain_attn = input_grads(tokens, cos, sin, grad_q, grad_own, later, grad_hidden, weights)
     grads = weight_grads(act_attn, mixed, act_ffn, grad_qkv, grad_low, grad_gu, grad_logits, gain_attn, gain_ffn)
-    own, own_down = scatter_sums(grads, grad_sdown)
+    own, own_down, sums = scatter_sums(grads, grad_sdown, part_expert)
 
     def gathered_hidden(w):
         return w.reshape(w.shape[0], experts, 16)[:, :, :14].reshape(w.shape[0], experts * 14)
 
-    expert_grads = [(a.astype(F32) + b.astype(F32))[None] for a, b in zip(part_expert, swapped)]
+    expert_grads = [a.astype(F32)[None] for a in sums]
     return (
         layer_out[None],
         grad_tokens[None],

time: 568 us -> 528 us (0.930)
  Pallas kernels: 479 us -> 443 us
    pallas_call x1, Pallas kernels: 141 us -> 114 us  [scatter_sums(): pl.pallas_call(scatter_kernel, out_shape=(jax.ShapeDtypeStruct((32, WIDE...]
    unnamed x46 -> x56, local copies, waits for them, and re-layouts: 10.3 us -> 16.3 us
    pallas_call x2, Pallas kernels: 164 us -> 158 us  [exchange(): pl.pallas_call(functools.partial(exchange_kernel, cuts, outward, work, (l...]
    broadcast_in_dim x3 -> x2, other arithmetic: 14.2 us -> 10.1 us  [per_device(): expert_grads = [a.astype(F32)[None] for a in sums]]
  transfers between devices with their start and end apart: 5 -> 2, of which waited for: 2 -> 2; matrix products, arithmetic and copies ran while one was open for 5% -> 1% of each run, Pallas kernels for 31% -> 0%
where the time goes in v3:
time: 528 us; the launch traced here: 520 us
  Pallas kernels  443 us (84%)
  local copies, waits for them, and re-layouts  36.1 us (7%)
  waiting for transfers between devices  24.7 us (5%)
  other arithmetic  10.1 us (2%)
    pallas_call x2, Pallas kernels, exchange(): pl.pallas_call(functools.partial(exchange_kernel, cuts, outward, work, (l...  158 us
    pallas_call x1, Pallas kernels, scatter_sums(): pl.pallas_call(scatter_kernel, out_shape=(jax.ShapeDtypeStruct((32, WIDE...  114 us
    pallas_call x1, Pallas kernels, gather_weights(): pl.pallas_call(gather_kernel, out_shape=(jax.ShapeDtypeStruct((4, 4, 80,...  82.6 us
    pallas_call x1, Pallas kernels, expert(): pl.pallas_call(expert_kernel, grid=(steps,), out_shape=(shape(BF16, devic...  23.4 us
    pallas_call x1, Pallas kernels, weight_grads(): pl.pallas_call(weight_grad_kernel, grid=(WIDE // 2,), out_shape=shape(BF1...  21.1 us
    ppermute x1, waiting for transfers between devices, per_device(): later = lax.ppermute(grad_prior, 'seq', [(1, 0)])  17.4 us
    unnamed x56, local copies, waits for them, and re-layouts  16.3 us
  transfers between devices with their start and end apart: 2, of which 2 were waited for; matrix products, arithmetic and copies ran while one was open for 1% of the time, Pallas kernels for 0%

profile of v3, /device:TPU:1, one launch (start us, length us, event | category | flops | bytes accessed | tf_op | source)
XLA Modules:
  0.0 519.9 jit_solution(14434972542513276040)
XLA Ops:
  0.7 1.5 reshape.93
  2.4 0.4 reshape.94
  2.8 1.6 reshape.95
  4.5 0.4 reshape.96
  4.9 0.1 copy.37
  5.4 2.1 dynamic_update_slice.3.win
  7.5 1.6 copy-done.4
  9.2 1.6 copy-done.5
  10.8 82.6 %gather_weights.1 = (bf16[4,4,80,7424]{3,2,1,0:T(8,128)(2,1)}, bf16[4,4,64,1280]{3,2,1,0:T(8,128)(2,1)}, bf16[1280,896]{1,0:T(8,128)(2,1)S(1)}, bf16[1280,896]{1,0:T(8,128)(2,1)S(1)}, bf16[896,1280]{1,0:T(8,128)(2,1)S(1)}) custom-call(bf16[32,7424]{1,0:T(8,128)(2,1)S(1)} %dynamic_update_slice.3.win, bf16[16,1280]{1,0:T(8,128)(2,1)S(1)} %pad.13.sdw, ...), custom_call_target="tpu_custom_call" | custom-call | tf_op jit(solution)/shard_map/gather_weights/pallas_call | solution.py:260
  93.4 1.4 copy-done.6
  94.8 1.4 copy-done.7
  96.2 1.4 copy-done.8
  97.6 8.1 %queries_keys_values.1 = (bf16[128,1280]{1,0:T(8,128)(2,1)}, bf16[128,1280]{1,0:T(8,128)(2,1)}, bf16[128,2560]{1,0:T(8,128)(2,1)}) custom-call(bf16[128,1280]{1,0:T(8,128)(2,1)} %bitcast.56, bf16[1280,7424]{1,0:T(8,128)(2,1)} %bitcast.43, f32[256,128]{1,0:T(8,128)} %constant.21.clone.cos, f32[256,128]{1,0:T(8,128)} %constant.22.clone.sin, ...), custom_call_target="tpu_custom_call" | custom-call | tf_op jit(solution)/shard_map/queries_keys_values/pallas_call | solution.py:791
  105.8 3.2 collective-permute-start
  109.0 5.6 %slice.52.refs_4_ = bf16[1280,2048]{1,0:T(8,128)(2,1)} slice(bf16[1280,7424]{1,0:T(8,128)(2,1)} %bitcast.45), slice={[0:1280], [5120:7168]} | slice | bytes 10485760 | tf_op jit(solution)/shard_map/slice | solution.py:1310
  114.7 0.8 copy.40.seg_col
  115.5 0.7 copy.39
  116.2 7.3 %collective-permute-done.prior = bf16[128,2560]{1,0:T(8,128)(2,1)S(1)} collective-permute-done((bf16[128,2560]{1,0:T(8,128)(2,1)}, bf16[128,2560]{1,0:T(8,128)(2,1)S(1)}, u32[]{:S(2)}, u32[]{:S(2)}) %collective-permute-start) | collective-permute-done | bytes 655392 | tf_op jit(solution)/shard_map/ppermute | solution.py:1300
  123.6 0.8 copy-done.12
  124.4 5.6 %attend.1 = (bf16[128,1280]{1,0:T(8,128)(2,1)}, f32[128,1280]{1,0:T(8,128)}, bf16[128,1280]{1,0:T(8,128)(2,1)}, f32[128,128]{1,0:T(8,128)}, f32[128,128]{1,0:T(8,128)}) custom-call(bf16[128,1280]{1,0:T(8,128)(2,1)} %bitcast.57, bf16[128,1280]{1,0:T(8,128)(2,1)} %get-tuple-element.66.q, bf16[128,2560]{1,0:T(8,128)(2,1)} %get-tuple-element.67.kv, ...), custom_call_target="tpu_custom_call" | custom-call | tf_op jit(solution)/shard_map/attend/pallas_call | solution.py:873
  130.0 1.0 copy-done.2
  131.0 0.8 copy-done.10
  131.9 0.8 copy-done.11
  132.7 3.2 dispatch.1
  135.9 2.2 copy-done
  138.1 0.8 copy-done.9
  139.0 78.8 %exchange_rows.2 = (bf16[4,4,4,16,2560]{4,3,2,1,0:T(8,128)(2,1)}, f32[4,4,4,1,2688]{4,3,2,1,0:T(1,128)}, f32[128,1280]{1,0:T(8,128)}, f32[128,1280]{1,0:T(8,128)...) custom-call(bf16[4,4,4,16,2560]{4,3,2,1,0:T(8,128)(2,1)} %bitcast.35, f32[4,4,4,1,2688]{4,3,2,1,0:T(1,128)} %bitcast.42, ...), custom_call_target="tpu_custom_call" | custom-call | tf_op jit(solution)/shard_map/exchange_rows/pallas_call | solution.py:679
  217.8 23.4 %expert.1 = (bf16[64,16,2560]{2,1,0:T(8,128)(2,1)}, f32[64,1,2560]{2,1,0:T(1,128)}, bf16[1088,1280]{1,0:T(8,128)(2,1)}, bf16[1088,1280]{1,0:T(8,128)(2,1)}, bf16...) custom-call(bf16[64,16,2560]{2,1,0:T(8,128)(2,1)} %bitcast.53, ...), custom_call_target="tpu_custom_call" | custom-call | tf_op jit(solution)/shard_map/expert/pallas_call | solution.py:987
  241.2 78.8 %exchange_rows.3 = (bf16[4,4,4,16,2560]{4,3,2,1,0:T(8,128)(2,1)}, f32[4,4,4,1,2560]{4,3,2,1,0:T(1,128)}, bf16[1280,896]{1,0:T(8,128)(2,1)}, bf16[1280,896]{1,0:T(8,128)(2,1)}, bf16[896,1280]{1,0:T(8,128)(2,1)}) custom-call(bf16[4,4,4,16,2560]{4,3,2,1,0:T(8,128)(2,1)} %bitcast.54, f32[4,4,4,1,2560]{4,3,2,1,0:T(1,128)} %bitcast.64, ...), custom_call_target="tpu_custom_call" | custom-call | tf_op jit(solution)/shard_map/exchange_rows/pallas_call | solution.py:679
  320.0 10.1 %combine.1 = (bf16[128,1280]{1,0:T(8,128)(2,1)}, f32[128,1280]{1,0:T(8,128)}, bf16[128,1280]{1,0:T(8,128)(2,1)}, bf16[128,1280]{1,0:T(8,128)(2,1)}, bf16[128,128]{1,0:T(8,128)(2,1)}, /*index=5*/f32[1,1280]{1,0:T(1,128)}) custom-call(bf16[64,16,2560]{2,1,0:T(8,128)(2,1)} %bitcast.55, f32[64,1,2560]{2,1,0:T(1,128)} %bitcast.65, ...), custom_call_target="tpu_custom_call" | custom-call | tf_op jit(solution)/shard_map/combine/pallas_call | solution.py:1117
  330.1 7.3 %attend_back.1 = (bf16[128,1280]{1,0:T(8,128)(2,1)}, f32[128,2560]{1,0:T(8,128)}, bf16[128,2560]{1,0:T(8,128)(2,1)}) custom-call(bf16[128,1280]{1,0:T(8,128)(2,1)} %get-tuple-element.66.q, bf16[128,2560]{1,0:T(8,128)(2,1)} %get-tuple-element.67.kv, bf16[128,2560]{1,0:T(8,128)(2,1)} %copy-done.12, s32[1,256]{1,0:T(1,128)} %seg_row.3, s32[256,1]{1,0:T(8,128)} %copy.40.seg_col, ...), custom_call_target="tpu_custom_call" | custom-call | tf_op jit(solution)/shard_map/attend_back/pallas_call | solution.py:720
  337.5 1.5 collective-permute-start.1
  339.0 17.4 %collective-permute-done.1.later = bf16[128,2560]{1,0:T(8,128)(2,1)S(1)} collective-permute-done((bf16[128,2560]{1,0:T(8,128)(2,1)}, bf16[128,2560]{1,0:T(8,128)(2,1)S(1)}, u32[]{:S(2)}, u32[]{:S(2)}) %collective-permute-start.1) | collective-permute-done | bytes 655392 | tf_op jit(solution)/shard_map/ppermute | solution.py:1333
  356.4 0.8 copy-done.14
  357.2 10.1 %input_grads.1 = (bf16[128,3840]{1,0:T(8,128)(2,1)}, f32[128,1280]{1,0:T(8,128)}, f32[1,1280]{1,0:T(1,128)}) custom-call(bf16[128,1280]{1,0:T(8,128)(2,1)} %bitcast.58, bf16[1280,7424]{1,0:T(8,128)(2,1)} %bitcast.50, f32[256,128]{1,0:T(8,128)} %constant.21.clone.cos, f32[256,128]{1,0:T(8,128)} %constant.22.clone.sin, ...), custom_call_target="tpu_custom_call" | custom-call | tf_op jit(solution)/shard_map/input_grads/pallas_call | solution.py:1188
  367.4 21.1 %weight_grads.1 = bf16[1280,7424]{1,0:T(8,128)(2,1)} custom-call(bf16[128,1280]{1,0:T(8,128)(2,1)} %get-tuple-element.98.act_attn, bf16[128,1280]{1,0:T(8,128)(2,1)} %get-tuple-element.99.mixed, bf16[128,1280]{1,0:T(8,128)(2,1)} %get-tuple-element.68.act.refs_2_.act_ffn, bf16[128,3840]{1,0:T(8,128)(2,1)} %get-tuple-element.100.grad_qkv, ...), custom_call_target="tpu_custom_call" | custom-call | tf_op jit(solution)/shard_map/weight_grads/pallas_call | solution.py:1241
  388.4 113.6 %scatter_sums.1 = (f32[32,7424]{1,0:T(8,128)}, f32[16,1280]{1,0:T(8,128)}, bf16[1280,896]{1,0:T(8,128)(2,1)}, bf16[1280,896]{1,0:T(8,128)(2,1)}, bf16[896,1280]{1,0:T(8,128)(2,1)}) custom-call(bf16[4,4,80,7424]{3,2,1,0:T(8,128)(2,1)} %bitcast.52, bf16[4,4,64,1280]{3,2,1,0:T(8,128)(2,1)} %bitcast.59, bf16[1280,896]{1,0:T(8,128)(2,1)} %get-tuple-element.107.p0, ...), custom_call_target="tpu_custom_call" | custom-call | tf_op jit(solution)/shard_map/scatter_sums/pallas_call | solution.py:500
  502.1 4.1 bitcast_convert_fusion
  506.2 1.2 fusion
  507.4 0.2 reshape.110
  507.7 1.0 reshape.111
  508.7 0.2 reshape.112
  508.9 1.0 reshape.113
  509.9 1.4 dynamic-slice.6
  511.3 6.0 %bitcast_convert_fusion.1 = (f32[1,1280,896]{2,1,0:T(8,128)}, f32[1,1280,896]{2,1,0:T(8,128)}) fusion(bf16[1280,896]{1,0:T(8,128)(2,1)} %get-tuple-element.113, bf16[1280,896]{1,0:T(8,128)(2,1)S(1)} %copy-done.13), kind=kLoop, calls=%fused_computation.1 | loop fusion | flops 2293760 | bytes 13762560 | tf_op jit(solution)/shard_map/broadcast_in_dim | solution.py:1341
  517.3 0.7 dynamic-slice_reduce_fusion
  518.0 0.9 fusion.1
  518.9 0.6 copy.44
  (49 shorter events, 0.5 us)
Async XLA Ops:
  0.7 4.3 copy-start.25
  0.7 4.4 copy-start.26
  0.7 4.5 copy-start.21
  0.7 4.5 copy-start.17
  0.7 4.5 copy-start.18
  0.7 4.5 copy-start.19
  0.7 4.5 copy-start.20
  0.7 4.5 copy-start.23
  2.3 5.2 %copy-start.3 = (bf16[1,1280,896]{2,1,0:T(8,128)(2,1)S(1)}, bf16[1,1280,896]{2,1,0:T(8,128)(2,1)}, u32[]{:S(2)}) copy-start(bf16[1,1280,896]{2,1,0:T(8,128)(2,1)} %param.33) | copy-start | bytes 6881284
  7.5 1.6 copy-start.4
  9.2 1.6 copy-start.5
  93.4 1.4 copy-start.6
  94.8 1.4 copy-start.7
  96.2 1.4 copy-start.8
  105.8 8.9 %copy-start.22 = (s32[1,256]{1,0:T(1,128)S(1)}, s32[1,256]{1,0:T(1,128)}, u32[]{:S(2)}) copy-start(s32[1,256]{1,0:T(1,128)} %seg_row.3) | copy-start | bytes 3076
  105.8 9.7 %copy-start.24 = (s32[1,128,7]{1,0,2:T(1,128)S(1)}, s32[1,128,7]{1,0,2:T(1,128)}, u32[]{:S(2)}) copy-start(s32[1,128,7]{1,0,2:T(1,128)} %param.22) | copy-start | bytes 10756
  105.8 17.8 %collective-permute-start = (bf16[128,2560]{1,0:T(8,128)(2,1)}, bf16[128,2560]{1,0:T(8,128)(2,1)S(1)}, u32[]{:S(2)}, u32[]{:S(2)}) collective-permute-start(bf16[128,2560]{1,0:T(8,128)(2,1)} %get-tuple-element.67.kv), channel_id=1, source_target_pairs={{0,64},{1,65},{2,66},{3,67},{4,68},{5,69},{6,70},{7,71},{8,72},{9,... | collective-permute-start | bytes 1966088 | tf_op jit(solution)/shard_map/ppermute | solution.py:1300
  123.6 0.8 copy-start.12
  124.4 5.7 %copy-start.1 = (bf16[1,128,1280]{2,1,0:T(8,128)(2,1)S(1)}, bf16[1,128,1280]{2,1,0:T(8,128)(2,1)}, u32[]{:S(2)}) copy-start(bf16[1,128,1280]{2,1,0:T(8,128)(2,1)} %param.20) | copy-start | bytes 983044
  130.0 1.0 copy-start.2
  131.0 0.8 copy-start.10
  131.9 0.8 copy-start.11
  135.9 2.3 copy-start
  138.1 0.8 copy-start.9
  337.5 18.9 %collective-permute-start.1 = (bf16[128,2560]{1,0:T(8,128)(2,1)}, bf16[128,2560]{1,0:T(8,128)(2,1)S(1)}, u32[]{:S(2)}, u32[]{:S(2)}) collective-permute-start(bf16[128,2560]{1,0:T(8,128)(2,1)} %get-tuple-element.95), channel_id=1, source_target_pairs={{64,0},{65,1},{66,2},{67,3},{68,4},{69,5},{70,6},{71,7},{72,8},{73... | collective-permute-start | bytes 1966088 | tf_op jit(solution)/shard_map/ppermute | solution.py:1333
  356.4 0.8 copy-start.14
  506.2 5.1 copy-start.13
  511.3 6.0 %copy-start.15 = (f32[32,7424]{1,0:T(8,128)S(1)}, f32[32,7424]{1,0:T(8,128)}, u32[]{:S(2)}) copy-start(f32[32,7424]{1,0:T(8,128)} %get-tuple-element.110) | copy-start | bytes 2850820
  511.3 7.6 %copy-start.16 = (f32[16,1280]{1,0:T(8,128)S(1)}, f32[16,1280]{1,0:T(8,128)}, u32[]{:S(2)}) copy-start(f32[16,1280]{1,0:T(8,128)} %get-tuple-element.111) | copy-start | bytes 245764

commit v4 on v3

v4 whole, which is shorter than its diff:
```python
import functools
import jax
import jax.numpy as jnp
import numpy as np
from jax import lax
from jax.experimental import pallas as pl
from jax.experimental.pallas import tpu as pltpu
from jax.sharding import PartitionSpec as P

HEADS = 10
EPSILON = 1e-06
NEG_BIG = -1e30
F32 = jnp.float32
BF16 = jnp.bfloat16
MESH = pl.DeviceIdType.MESH

PIECES = {
    "q": (80, 16, ((0, 8, 4), (8, 8, 4))),
    "r": (80, 14, ((0, 7, 4), (7, 7, 4))),
    "d": (64, 5, ((0, 3, 2), (3, 2, 1))),
}
Q_WIDE, R_WIDE, D_WIDE = 4096, 3584, 1280
GAINS = 30
ROUTER = 26
UNITS = (0, 1)


def place():
    hi = lax.axis_index("seq")
    e = lax.axis_index("exp")
    return hi, e // 16, lax.rem(e // 4, 4), lax.rem(e // 2, 2), lax.rem(e, 2)


def device(hi, y, z, lo, c):
    return (hi, ((y * 4 + z) * 2 + lo) * 2 + c)


def up(v):
    return lax.rem(v + 1, 4)


def dn(v):
    return lax.rem(v + 3, 4)


def opp(v):
    return lax.rem(v + 2, 4)


def mul(v, m=128):
    return pl.multiple_of(v, m)


def greet(devices):
    bar = pltpu.get_barrier_semaphore()
    for to in devices:
        pl.semaphore_signal(bar, inc=1, device_id=to, device_id_type=MESH)
    pl.semaphore_wait(bar, len(devices))


class Sender:
    def __init__(self, send_sem, recv_sem, local_sem):
        self.sems = (send_sem, recv_sem, local_sem)
        self.sent = []
        self.kept = 0

    def describe(self, src, dst, to):
        k = len(self.sent)
        self.sent.append(None)
        return pltpu.make_async_remote_copy(
            src_ref=src,
            dst_ref=dst,
            send_sem=self.sems[0].at[k],
            recv_sem=self.sems[1].at[k],
            device_id=to,
            device_id_type=MESH,
        )

    def remote(self, src, dst, to):
        copy = self.describe(src, dst, to)
        copy.start()
        self.sent[-1] = copy
        return copy

    def local(self, src, dst):
        copy = pltpu.make_async_copy(src, dst, self.sems[2].at[self.kept])
        self.kept += 1
        copy.start()
        return copy

    def settle(self, copy):
        copy.wait_send()
        self.sent = [None if one is copy else one for one in self.sent]

    def finish(self):
        for copy in self.sent:
            if copy is not None:
                copy.wait_send()


def arrived(copies):
    for copy in copies:
        copy.wait_recv()


def ring_neighbours(hi, y, z, lo, c):
    return {
        ("y", 1): device(hi, up(y), z, lo, c),
        ("y", -1): device(hi, dn(y), z, lo, c),
        ("z", 1): device(hi, y, up(z), lo, c),
        ("z", -1): device(hi, y, dn(z), lo, c),
        ("y", 2): device(hi, opp(y), z, lo, c),
        ("z", 2): device(hi, y, opp(z), lo, c),
    }


def unit_tiles(piece, u, half):
    s, w, w0 = PIECES[piece][2][u]
    return ((s, w0), (s + w0, w - w0))[half] if half is not None else (s, w)


def lanes(piece, u, half, core):
    s, w = unit_tiles(piece, u, half)
    return pl.ds(mul(core * (PIECES[piece][1] * 128) + s * 128), w * 128)


def core_lanes(piece, core):
    n = PIECES[piece][1] * 128
    return pl.ds(mul(core * n), n)


def interleave(steps, work):
    for step in steps:
        step()
        next(work, None)
    for _ in work:
        pass


def dot(a, b):
    return jnp.dot(a, b, preferred_element_type=F32)


def dot_t(a, b):
    return lax.dot_general(a, b, (((1,), (1,)), ((), ())), preferred_element_type=F32)


def t_dot(a, b):
    return lax.dot_general(a, b, (((0,), (0,)), ((), ())), preferred_element_type=F32)


def iota(shape, dim):
    return lax.broadcasted_iota(jnp.int32, shape, dim)


def shape(dtype, *dims):
    return jax.ShapeDtypeStruct(dims, dtype)


def gain_rows(tile):
    pick = (iota((8, 128), 1) == iota((8, 128), 0)).astype(BF16)
    return dot_t(pick, tile)


def rms_forward(values, gain):
    inv_rms = lax.rsqrt(jnp.mean(values * values, axis=-1, keepdims=True) + EPSILON)
    return values * inv_rms * gain, inv_rms


def rms_backward(values, inv_rms, gain, upstream):
    weighted = upstream * gain
    inner = jnp.mean(weighted * values, axis=-1, keepdims=True)
    grad_in = inv_rms * weighted - values * (inv_rms * inv_rms * inv_rms) * inner
    grad_gain = jnp.sum(upstream * values * inv_rms, axis=0, keepdims=True)
    return grad_in, grad_gain


def rotary_tables(rows):
    freq = np.power(10000.0, -2.0 * np.arange(64) / 128)
    angles = np.arange(rows)[:, None] * freq[None, :]
    cos, sin = np.cos(angles), np.sin(angles)
    return (
        jnp.asarray(np.concatenate([cos, cos], axis=1), F32),
        jnp.asarray(np.concatenate([-sin, sin], axis=1), F32),
    )


def silu_parts(pre_act):
    sigma = jax.nn.sigmoid(pre_act)
    return (pre_act * sigma, sigma * (1.0 + pre_act * (1.0 - sigma)))


def seq_rows():
    return pl.ds(mul(lax.axis_index("seq") * 128), 128)


def allowed_keys(seg_row, seg_col):
    hi = lax.axis_index("seq")
    here = seq_rows()
    mine = seg_col[here, :]
    rows = mine.shape[0]
    own = (seg_row[:, here] == mine) & (iota((rows, rows), 1) <= iota((rows, rows), 0))
    prior = (seg_row[:, 0:rows] == mine) & (hi == 1)
    return own, prior


def head_probs(h, q, kv, prior, own_ok, prior_ok, width):
    here = slice(h * 128, (h + 1) * 128)
    behind = slice(width + h * 128, width + (h + 1) * 128)
    query = q[:, here]
    keys = jnp.concatenate([prior[:, here], kv[:, here]], axis=0)
    values = jnp.concatenate([prior[:, behind], kv[:, behind]], axis=0)
    scores = dot_t(query, keys) * (128.0**-0.5)
    rows = query.shape[0]
    scores = jnp.concatenate(
        [jnp.where(prior_ok, scores[:, :rows], NEG_BIG), jnp.where(own_ok, scores[:, rows:], NEG_BIG)], axis=1
    )
    expo = jnp.exp(scores - jnp.max(scores, axis=-1, keepdims=True))
    return query, keys, values, expo / jnp.sum(expo, axis=-1, keepdims=True)


class Gather:
    def __init__(self, wires, names, blocks, outs, spot):
        hi, y, z, lo, c = spot
        self.wires, self.names, self.outs, self.core = wires, names, outs, c
        self.sib = device(hi, y, z, lo, 1 - c)
        nb = ring_neighbours(hi, y, z, lo, c)
        self.keep = []
        units = []
        for u in UNITS:
            a1, a2 = ("y", "z") if u == 0 else ("z", "y")
            p1, p2 = (y, z) if u == 0 else (z, y)
            units.append(
                dict(p1=p1, p2=p2, up1=nb[a1, 1], dn1=nb[a1, -1], up2=nb[a2, 1], dn2=nb[a2, -1], got={}, second=[], sib=[])
            )
        self.units = units
        self.steps = [functools.partial(self.own_block, blocks, y, z)]
        for u in UNITS:
            self.steps.append(functools.partial(self.first_axis, u, "up1", 0))
        for u in UNITS:
            self.steps.append(functools.partial(self.first_axis, u, "dn1", 1))
        for u in UNITS:
            self.steps.append(functools.partial(self.first_far, u))
        turn = (lambda p: p, dn, up, opp)
        self.near, self.far = [], []
        for k in range(4):
            for u in UNITS:
                q1 = turn[k](units[u]["p1"])
                self.near.append(functools.partial(self.second_axis, u, k, q1))
                self.far.append(functools.partial(self.second_far, u, k, q1))

    def region(self, name, u, half, q1, q2):
        by, bz = (q1, q2) if u == 0 else (q2, q1)
        return self.outs[name].at[by, bz, :, lanes(name, u, half, self.core)]

    def send(self, u, half, q1, q2, to, src=None):
        copies = []
        for name in self.names:
            dst = self.region(name, u, half, q1, q2)
            copies.append(self.wires.remote(src[name] if src else dst, dst, to))
        return copies

    def spread(self, u, q1, src=None):
        unit = self.units[u]
        at = (q1, unit["p2"])
        unit["second"].append((self.send(u, None, *at, unit["up2"], src), self.send(u, None, *at, unit["dn2"], src)))
        unit["sib"].append(self.send(u, None, *at, self.sib, src))

    def own_block(self, blocks, y, z):
        for name in self.names:
            self.keep.append(self.wires.local(blocks[name], self.outs[name].at[y, z, :, core_lanes(name, self.core)]))
        for u, unit in enumerate(self.units):
            src = {}
            for name in self.names:
                s, w = unit_tiles(name, u, None)
                src[name] = blocks[name].at[:, pl.ds(s * 128, w * 128)]
            at = (unit["p1"], unit["p2"])
            unit["got"]["up1"] = self.send(u, None, *at, unit["up1"], src)
            unit["got"]["dn1"] = self.send(u, None, *at, unit["dn1"], src)
            self.spread(u, unit["p1"], src)

    def first_axis(self, u, way, half):
        unit = self.units[u]
        arrived(unit["got"][way])
        q1 = dn(unit["p1"]) if way == "up1" else up(unit["p1"])
        unit["got"]["far", half] = self.send(u, half, q1, unit["p2"], unit[way])
        self.spread(u, q1)

    def first_far(self, u):
        unit = self.units[u]
        arrived(unit["got"]["far", 0])
        arrived(unit["got"]["far", 1])
        self.spread(u, opp(unit["p1"]))

    def second_axis(self, u, k, q1):
        unit = self.units[u]
        for half, way, turn in ((0, "up2", dn), (1, "dn2", up)):
            arrived(unit["second"][k][half])
            at = (q1, turn(unit["p2"]))
            unit["got"][k, half] = self.send(u, half, *at, unit[way])
            unit["sib"].append(self.send(u, None, *at, self.sib))

    def second_far(self, u, k, q1):
        unit = self.units[u]
        arrived(unit["got"][k, 0])
        arrived(unit["got"][k, 1])
        unit["sib"].append(self.send(u, None, q1, opp(unit["p2"]), self.sib))

    def finish(self):
        for unit in self.units:
            for copies in unit["sib"]:
                arrived(copies)
        for copy in self.keep:
            copy.wait()


def window_block(first, second, shift):
    n = first.shape[0]
    return first[0:shift], first[shift:n] + second[0 : n - shift], second[n - shift : n]


def forward_kernel(
    win_q, win_r, win_d, e0, e1, e2, tok, cos, sin, seg_row, seg_col,
    out_q, out_r, out_d, o0, o1, o2, act, q, kv, prior, mixed,
    sib_q, sib_r, pair_q, pair_r, side_q, side_r, blk_q, blk_r, blk_d, w_buf, ssem, rsem, lsem, esem, wsem,
):
    spot = place()
    hi, y, z, lo, c = spot
    sib = device(hi, y, z, lo, 1 - c)
    xn = device(hi, y, z, 1 - lo, c)
    hn = device(1 - hi, y, z, lo, c)
    greet([sib, xn, hn] + list(ring_neighbours(*spot).values()))
    wires = Sender(ssem, rsem, lsem)
    width = tok.shape[1]
    owner = c == hi

    @pl.when(hi == 0)
    def _():
        prior[...] = jnp.zeros_like(prior)

    j = lo * 2 + c
    windows = {"q": (win_q, sib_q, pair_q, side_q, blk_q), "r": (win_r, sib_r, pair_r, side_r, blk_r)}
    swaps = {}
    for name in "qr":
        win, from_sib = windows[name][:2]
        swaps[name] = wires.remote(win.at[:, core_lanes(name, 1 - c)], from_sib, sib)
    r16 = pl.ds(mul(j * 16, 16), 16)
    swap_d = wires.remote(win_d.at[:, core_lanes("d", 1 - c)], blk_d.at[r16], sib)
    blk_d[r16, :] = win_d[:, core_lanes("d", c)]
    across = {}
    for name in "qr":
        win, from_sib, pair, side, _blk = windows[name]
        own = win[:, core_lanes(name, c)]
        swaps[name].wait_recv()
        got = from_sib[...]
        pair[0:16], pair[16:32], pair[32:48] = window_block(
            jnp.where(c == 0, own, got), jnp.where(c == 0, got, own), 16
        )
        across[name] = wires.remote(pair, side, xn)
    swap_d.wait_recv()
    r32 = pl.ds(mul(lo * 32, 16), 32)
    across_d = wires.remote(blk_d.at[r32], blk_d.at[r32], xn)

    def pass_expert(k):
        return pltpu.make_async_remote_copy(
            src_ref=(e0, e1, e2)[k],
            dst_ref=(o0, o1, o2)[k],
            send_sem=esem.at[0, k],
            recv_sem=esem.at[1, k],
            device_id=sib,
            device_id_type=MESH,
        )

    blocks = {"q": blk_q, "r": blk_r, "d": blk_d}
    outs = {"q": out_q, "r": out_r, "d": out_d}
    group_q = Gather(wires, "q", blocks, outs, spot)
    group_r = Gather(wires, "rd", blocks, outs, spot)

    def whole_block(name):
        _win, _sib, pair, side, blk = windows[name]
        across[name].wait_recv()
        own, got = pair[...], side[...]
        blk[0:32], blk[32:48], blk[48:80] = window_block(
            jnp.where(lo == 0, own, got), jnp.where(lo == 0, got, own), 32
        )

    whole_block("q")
    for step in group_q.steps:
        step()
    whole_block("r")
    across_d.wait_recv()
    for step in group_q.near:
        step()
    group_r.steps[0]()
    for step in group_q.far:
        step()
    group_q.finish()

    @pl.when(owner)
    def _():
        for k in range(3):
            pass_expert(k).start()

    def load(i, slot):
        return pltpu.make_async_copy(out_q.at[:, :, :, pl.ds(i * 512, 512)], w_buf.at[slot], wsem.at[slot])

    later = wires.describe(kv, prior, hn)

    def work():
        order = (7, 2, 3, 4, 5, 6, 0, 1)
        here = seq_rows()
        cosine, sine = cos[here, :], sin[here, :]
        load(order[0], 0).start()
        for n, i in enumerate(order):
            slot = n % 2
            load(i, slot).wait()
            if n + 1 < len(order):
                load(order[n + 1], 1 - slot).start()
            w = w_buf[slot].reshape(width, 512)
            if n == 0:
                gains = gain_rows(w[:, (GAINS - 28) * 128 : (GAINS - 27) * 128])
                normed, _inv = rms_forward(tok[...].astype(F32), gains[0:1])
                act[...] = normed.astype(BF16)
                w = w[:, :256]
            x = dot(act[...], w)
            for t in range(w.shape[1] // 128):
                tile = 4 * i + t
                v = x[:, t * 128 : (t + 1) * 128]
                if tile < 20:
                    v = v * cosine + pltpu.roll(v, 64, 1) * sine
                if tile < 10:
                    q[:, tile * 128 : (tile + 1) * 128] = v.astype(BF16)
                else:
                    kv[:, (tile - 10) * 128 : (tile - 9) * 128] = v.astype(BF16)
            if i == 6:

                @pl.when(hi == 0)
                def _():
                    later.start()

            yield
        for _ in range(4):
            yield

        @pl.when(hi == 1)
        def _():
            later.wait_recv()

        own_ok, prior_ok = allowed_keys(seg_row, seg_col)
        for h in range(HEADS):
            _query, _keys, values, probs = head_probs(h, q, kv, prior, own_ok, prior_ok, width)
            mixed[:, h * 128 : (h + 1) * 128] = dot(probs.astype(BF16), values).astype(BF16)
            yield

    interleave(group_r.steps[1:] + group_r.near + group_r.far + [group_r.finish], work())

    @pl.when(hi == 0)
    def _():
        later.wait_send()

    @pl.when(owner)
    def _():
        for k in range(3):
            pass_expert(k).wait_send()

    @pl.when(jnp.logical_not(owner))
    def _():
        for k in range(3):
            pass_expert(k).wait_recv()

    wires.finish()


def forward(shard_q, shard_r, down, experts, tokens, cos, sin, seg_row, seg_col):
    rows, width = tokens.shape
    offset = 4 * lax.rem(lax.axis_index("exp"), 4)
    window = lambda s: lax.dynamic_update_slice(jnp.zeros((32, s.shape[1]), BF16), s, (offset, 0))
    down = jnp.pad(down, ((0, 2), (0, 0)))
    sems = 2 + 1 + 3 + 36 * 2 * 3 + 8
    vmem, anywhere = pl.BlockSpec(memory_space=pltpu.VMEM), pl.BlockSpec(memory_space=pl.ANY)
    half = {name: PIECES[name][1] * 128 for name in PIECES}
    out = pl.pallas_call(
        forward_kernel,
        out_shape=(
            shape(BF16, 4, 4, 80, Q_WIDE),
            shape(BF16, 4, 4, 80, R_WIDE),
            shape(BF16, 4, 4, 64, D_WIDE),
            *(shape(BF16, *w.shape) for w in experts),
            shape(BF16, rows, width),
            shape(BF16, rows, width),
            shape(BF16, rows, 2 * width),
            shape(BF16, rows, 2 * width),
            shape(BF16, rows, width),
        ),
        in_specs=[vmem] * 3 + [anywhere] * 3 + [vmem] * 5,
        out_specs=(anywhere,) * 6 + (vmem,) * 5,
        scratch_shapes=[pltpu.VMEM((n, half[name]), BF16) for n in (32, 48, 48, 80) for name in "qr"]
        + [
            pltpu.VMEM((64, half["d"]), BF16),
            pltpu.VMEM((2, 4, 4, 80, 512), BF16),
            pltpu.SemaphoreType.DMA((sems,)),
            pltpu.SemaphoreType.DMA((sems,)),
            pltpu.SemaphoreType.DMA((3,)),
            pltpu.SemaphoreType.DMA((2, 3)),
            pltpu.SemaphoreType.DMA((2,)),
        ],
        compiler_params=pltpu.CompilerParams(collective_id=1, has_side_effects=True, vmem_limit_bytes=56 << 20),
        name="gather_attend",
    )(window(shard_q), window(shard_r), down, *experts, tokens, cos, sin, seg_row, seg_col)
    w_q, w_r, w_d = (out[k].reshape(16 * out[k].shape[2], out[k].shape[3]) for k in range(3))
    return (w_q, w_r, w_d, out[3:6]) + tuple(out[6:])


class RingSum:
    def __init__(self, wires, names, hold, from_sib, bufs, to_sib, spot):
        hi, y, z, lo, c = spot
        self.wires, self.names, self.hold, self.from_sib, self.bufs, self.to_sib = (
            wires, names, hold, from_sib, bufs, to_sib,
        )
        self.sib = device(hi, y, z, lo, 1 - c)
        self.nb = ring_neighbours(hi, y, z, lo, c)
        self.first_axis, self.second_axis = ("y", "z"), ("z", "y")
        self.ring, self.coming = {}, {}
        orders = []
        for u in UNITS:
            p1, p2 = (y, z) if u == 0 else (z, y)
            ones = (opp(p1), up(p1), dn(p1), p1)
            orders.append([(q1, q2) if u == 0 else (q2, q1) for q2 in (opp(p2), up(p2), dn(p2), p2) for q1 in ones])
        self.orders = orders
        self.steps = []
        for i in range(4):
            for u in UNITS:
                self.steps.append(functools.partial(self.far_step, u, i))
        for i in range(4):
            for u in UNITS:
                self.steps.append(functools.partial(self.near_step, u, i, 1))
            for u in UNITS:
                self.steps.append(functools.partial(self.near_step, u, i, -1))
        for i in range(4):
            for u in UNITS:
                self.steps.append(functools.partial(self.own_step, u, i))
        for u in UNITS:
            self.steps.append(functools.partial(self.last_step, u))

    def blocks(self, refs, u, index):
        return {name: refs[name][u].at[index] for name in self.names}

    def start(self):
        for k in range(16):
            for u in UNITS:
                at = self.orders[u][k]
                src, dst = self.blocks(self.to_sib, u, at), self.blocks(self.from_sib, u, at)
                self.coming[u, k] = self.pair(src, dst, self.sib)

    def pair(self, src, dst, to):
        return [self.wires.remote(src[name], dst[name], to) for name in self.names]

    def add_in(self, dst, *more):
        @pl.loop(0, dst.shape[-2] // 16)
        def _(i):
            r = pl.ds(mul(i * 16, 16), 16)
            value = dst[r, :].astype(F32)
            for ref in more:
                value = value + ref[r, :].astype(F32)
            dst[r, :] = value.astype(BF16)

    def ready(self, u, k):
        arrived(self.coming[u, k])
        at = self.orders[u][k]
        blk, more = self.blocks(self.hold, u, at), self.blocks(self.from_sib, u, at)
        for name in self.names:
            self.add_in(blk[name], more[name])
        return blk

    def half(self, blk, u, h):
        cut = {}
        for name in self.names:
            s, w, w0 = PIECES[name][2][u]
            cut[name] = blk[name].at[:, pl.ds(0, w0 * 128) if h == 0 else pl.ds(w0 * 128, (w - w0) * 128)]
        return cut

    def buffer(self, u, i, slot):
        return {name: self.bufs[name][u][i].at[slot] for name in self.names}

    def far_block(self, u, slot, blk, axis):
        self.ring[u, slot, 0] = self.pair(self.half(blk, u, 0), self.buffer(u, 0, slot), self.nb[axis, 1])
        self.ring[u, slot, 1] = self.pair(self.half(blk, u, 1), self.buffer(u, 1, slot), self.nb[axis, -1])

    def near_block(self, u, slot, blk, axis, way):
        h = 0 if way == 1 else 1
        arrived(self.ring[u, slot, h])
        dst, more = self.half(blk, u, h), self.buffer(u, h, slot)
        for name in self.names:
            self.add_in(dst[name], more[name])
        self.ring[u, slot, 2 + h] = self.pair(blk, self.buffer(u, 2 + h, slot), self.nb[axis, way])

    def own_block(self, u, slot, blk):
        arrived(self.ring[u, slot, 2])
        arrived(self.ring[u, slot, 3])
        one, two = self.buffer(u, 2, slot), self.buffer(u, 3, slot)
        for name in self.names:
            self.add_in(blk[name], one[name], two[name])

    def far_step(self, u, i):
        self.far_block(u, i, self.ready(u, i), self.second_axis[u])

    def near_step(self, u, i, way):
        self.near_block(u, i, self.ready(u, (4 if way == 1 else 8) + i), self.second_axis[u], way)

    def own_step(self, u, i):
        blk = self.ready(u, 12 + i)
        self.own_block(u, i, blk)
        axis = self.first_axis[u]
        if i == 0:
            for h in (0, 1):
                self.ring[u, 4, h] = self.pair(self.half(blk, u, h), self.buffer(u, h, 4), self.nb[axis, 2])
        elif i < 3:
            self.ring[u, 4, 1 + i] = self.pair(blk, self.buffer(u, 1 + i, 4), self.nb[axis, 1 if i == 1 else -1])

    def last_step(self, u):
        blk = self.blocks(self.hold, u, self.orders[u][15])
        self.own_block(u, 4, blk)
        for h in (0, 1):
            arrived(self.ring[u, 4, h])
            dst, more = self.half(blk, u, h), self.buffer(u, h, 4)
            for name in self.names:
                self.add_in(dst[name], more[name])


def sum_scratch():
    scratch = []
    for rows, _tiles, units in PIECES.values():
        for s, w, w0 in units:
            scratch += [pltpu.VMEM((4, 4, rows, w * 128), BF16)] * 2
            scratch += [pltpu.VMEM((5, rows, t * 128), BF16) for t in (w0, w - w0, w, w)]
    return scratch


def backward_kernel(
    left_r, right_r, sdown, act, q, kv, prior, seg_row, seg_col, grad_mixed, cos, sin, tok, grad_hidden, gain_f, w_q,
    p0, p1, p2,
    fin_q, fin_r, fin_d, t0, t1, t2, grad_tokens,
    *scratch,
):
    names = list(PIECES)
    hold, from_sib, bufs = {}, {}, {}
    scratch = list(scratch)
    for name in names:
        hold[name], from_sib[name], bufs[name] = [], [], []
        for u in UNITS:
            hold[name].append(scratch.pop(0))
            from_sib[name].append(scratch.pop(0))
            bufs[name].append([scratch.pop(0) for _ in range(4)])
    sums, sides, mids, fars = ({name: scratch.pop(0) for name in names} for _ in range(4))
    accs = {name: scratch.pop(0) for name in names}
    sent = [scratch.pop(0) for _ in UNITS]
    grad_own, grad_prior, later, left_q, right_q, total, w_buf, gain_tile = scratch[:8]
    ssem, rsem, lsem, esend, erecv, wsem, piece_sem = scratch[8:]
    spot = place()
    hi, y, z, lo, c = spot
    sib = device(hi, y, z, lo, 1 - c)
    xn = device(hi, y, z, 1 - lo, c)
    hn = device(1 - hi, y, z, lo, c)
    greet([sib, xn, hn, device(1 - hi, y, z, lo, 1 - c)] + list(ring_neighbours(*spot).values()))
    wires = Sender(ssem, rsem, lsem)
    rows, width = tok.shape

    owner = c == hi
    parts, totals = (p0, p1, p2), (t0, t1, t2)
    across = device(1 - hi, y, z, lo, hi)

    def rows_of(ref, core):
        n = ref.shape[0] // 2
        return ref.at[pl.ds(mul(core * n, 16), n)]

    def expert_copy(src, dst, k, tag, to):
        return pltpu.make_async_remote_copy(
            src_ref=src, dst_ref=dst, send_sem=esend.at[k], recv_sem=erecv.at[tag], device_id=to, device_id_type=MESH
        )

    def across_piece(k, i):
        n = parts[k].shape[0]
        return pltpu.make_async_remote_copy(
            src_ref=parts[k].at[pl.ds(i * 64, 64)],
            dst_ref=totals[k].at[pl.ds(mul(c * n + i * 64, 16), 64)],
            send_sem=piece_sem.at[0, k, i],
            recv_sem=piece_sem.at[1, k, 10 * c + i],
            device_id=across,
            device_id_type=MESH,
        )

    def coming_piece(k, i, core):
        n = parts[k].shape[0]
        rows_ = totals[k].at[pl.ds(mul(core * n + i * 64, 16), 64)]
        return pltpu.make_async_remote_copy(
            src_ref=rows_,
            dst_ref=rows_,
            send_sem=piece_sem.at[0, k, i],
            recv_sem=piece_sem.at[1, k, 10 * core + i],
            device_id=across,
            device_id_type=MESH,
        )

    pieces = [(k, i) for k in range(3) for i in range(parts[k].shape[0] // 64)]

    def send_near(k):
        return expert_copy(parts[k], rows_of(totals[k], c), k, k, sib)

    def near_half(k):
        return expert_copy(rows_of(totals[k], 1 - c), rows_of(totals[k], 1 - c), k, k, sib)

    def expert_steps():
        for n, (k, i) in enumerate(pieces):
            across_piece(k, i).start()
            if n == len(pieces) // 2:

                @pl.when(jnp.logical_not(owner))
                def _():
                    for k in range(3):
                        send_near(k).start()

            yield

    own_d = []
    for u in UNITS:
        s, w = unit_tiles("d", u, None)
        own_d.append(wires.local(sdown.at[:, :, :, lanes("d", u, None, c)], hold["d"][u]))

    def products(left, right, name, core, refs):
        for u in UNITS:
            r = right[:, lanes(name, u, None, core)]
            for m in (0, 1):
                v = t_dot(left[:, m * 640 : (m + 1) * 640], r).astype(BF16)
                for b in range(8):
                    refs[u][2 * m + b // 4, b % 4] = v[b * 80 : (b + 1) * 80]

    def views(name, refs):
        return [ref.at[:, :, :, pl.ds(0, PIECES[name][2][u][1] * 128)] for u, ref in enumerate(refs)]

    to_sib_r = views("r", sent)
    products(left_r, right_r, "r", 1 - c, to_sib_r)
    to_sib_d = [sdown.at[:, :, :, lanes("d", u, None, 1 - c)] for u in UNITS]
    group_r = RingSum(wires, "rd", hold, from_sib, bufs, {"r": to_sib_r, "d": to_sib_d}, spot)
    group_r.start()
    products(left_r, right_r, "r", c, hold["r"])
    for copy in own_d:
        copy.wait()

    def load(i):
        return pltpu.make_async_copy(w_q.at[:, pl.ds(i * 512, 512)], w_buf.at[i % 2], wsem.at[i % 2])

    load_gains = pltpu.make_async_copy(w_q.at[:, pl.ds(GAINS * 128, 128)], gain_tile, wsem.at[2])
    exchange_kv = wires.describe(grad_prior, later, hn)
    to_sib_q = views("q", sent)
    group_q = RingSum(wires, "q", hold, from_sib, bufs, {"q": to_sib_q}, spot)

    def work():
        load(0).start()
        load_gains.start()
        here = seq_rows()
        cosine, sine = cos[here, :], sin[here, :]
        own_ok, prior_ok = allowed_keys(seg_row, seg_col)
        inv_root = 128.0**-0.5

        @pl.when(hi == 1)
        def _():
            later[...] = jnp.zeros_like(later)

        for h in range(HEADS):
            query, keys, values, probs = head_probs(h, q, kv, prior, own_ok, prior_ok, width)
            mine = slice(h * 128, (h + 1) * 128)
            behind = slice(width + h * 128, width + (h + 1) * 128)
            gm = grad_mixed[:, mine]
            grad_probs = dot_t(gm, values)
            inner = jnp.sum(probs * grad_probs, axis=-1, keepdims=True)
            grad_scores = (probs * (grad_probs - inner)).astype(BF16)
            grad_values = t_dot(probs.astype(BF16), gm)
            gq = dot(grad_scores, keys) * inv_root
            grad_keys = t_dot(grad_scores, query) * inv_root
            right_q[0:rows, mine] = (gq * cosine - pltpu.roll(gq, 64, 1) * sine).astype(BF16)
            grad_own[:, mine] = grad_keys[rows:]
            grad_own[:, behind] = grad_values[rows:]
            grad_prior[:, mine] = grad_keys[:rows].astype(BF16)
            grad_prior[:, behind] = grad_values[:rows].astype(BF16)
            yield

        @pl.when(hi == 1)
        def _():
            exchange_kv.start()

        right_q[0:rows, 3 * width :] = jnp.zeros((rows, Q_WIDE - 3 * width), BF16)
        right_q[rows:, :] = (iota((16, Q_WIDE), 1) == iota((16, Q_WIDE), 0) + GAINS * 128).astype(BF16)
        left_q[0:rows, :] = act[...]
        total[...] = jnp.zeros_like(total)

        def add_chunk(i):
            load(i).wait()
            if i < 7:
                load(i + 1).start()
            total[...] += dot_t(right_q[0:rows, i * 512 : (i + 1) * 512], w_buf[i % 2])

        for i in (0, 1):
            add_chunk(i)
            yield

        @pl.when(hi == 0)
        def _():
            exchange_kv.wait_recv()

        for h in range(HEADS):
            mine = slice(h * 128, (h + 1) * 128)
            gk = grad_own[:, mine] + later[:, mine].astype(F32)
            right_q[0:rows, width + h * 128 : width + (h + 1) * 128] = (
                gk * cosine - pltpu.roll(gk, 64, 1) * sine
            ).astype(BF16)
        right_q[0:rows, 2 * width : 3 * width] = (grad_own[:, width:] + later[:, width:].astype(F32)).astype(BF16)
        yield
        for i in range(2, 8):
            add_chunk(i)
            yield
        load_gains.wait()
        gain = gain_rows(gain_tile[...])[0:1]
        values = tok[...].astype(F32)
        _normed, inv = rms_forward(values, gain)
        grad_norm, gain_sum = rms_backward(values, inv, gain, total[...])
        grad_tokens[...] = grad_hidden[...] + grad_norm
        row = iota((16, width), 0)
        left_q[rows:, :] = jnp.where(row == 0, gain_sum, jnp.where(row == 1, gain_f[...], 0.0)).astype(BF16)
        yield
        for k in range(16):
            for u in UNITS:
                wires.settle(group_r.coming[u, k][0])
        products(left_q, right_q, "q", 1 - c, to_sib_q)
        group_q.start()
        yield
        products(left_q, right_q, "q", c, hold["q"])
        yield

    def window_sums(group):
        copies = {}
        for name in group:
            n = PIECES[name][0]
            for u in UNITS:
                s, w = unit_tiles(name, u, None)
                sums[name][:, s * 128 : (s + w) * 128] = hold[name][u][y, z]
            window = 48 if n == 80 else 32
            copies[name] = wires.remote(sums[name].at[pl.ds(mul((1 - lo) * 32, 16), window)], sides[name], xn)
        yield
        for name in group:
            copies[name].wait_recv()
            window = sides[name].shape[0]
            r = pl.ds(mul(lo * 32, 16), window)
            mids[name][...] = (sums[name][r, :].astype(F32) + sides[name][...].astype(F32)).astype(BF16)
            copies[name] = wires.remote(mids[name], fars[name], hn)
        yield
        fins = {"q": fin_q, "r": fin_r, "d": fin_d}
        for name in group:
            copies[name].wait_recv()
            accs[name][...] = mids[name][...].astype(F32) + fars[name][...].astype(F32)
            n = fins[name].shape[0]
            mine = core_lanes(name, c)
            copies[name] = wires.remote(
                accs[name].at[pl.ds(mul((1 - c) * 16, 16), n)], fins[name].at[:, mine], sib
            )
            fins[name][:, mine] = accs[name][pl.ds(mul(c * 16, 16), n), :]
        yield
        for name in group:
            copies[name].wait_recv()

    experts = expert_steps()
    busy = work()
    for step in group_r.steps[:24]:
        step()
        next(busy, None)
        next(experts, None)
    for _ in busy:
        next(experts, None)
    rest = list(group_r.steps[24:])
    for step in group_q.steps[:24]:
        step()
        next(experts, None)
        if rest:
            rest.pop(0)()
    for _ in experts:
        pass
    interleave(group_q.steps[24:], window_sums("rd"))
    for _ in window_sums("q"):
        pass
    for k, i in pieces:
        across_piece(k, i).wait_send()

    @pl.when(owner)
    def _():
        for k in range(3):
            near_half(k).wait_recv()

    @pl.when(jnp.logical_not(owner))
    def _():
        for k in range(3):
            send_near(k).wait_send()
        for k, i in pieces:
            for core in (0, 1):
                coming_piece(k, i, core).wait_recv()

    @pl.when(hi == 1)
    def _():
        exchange_kv.wait_send()

    wires.finish()


def backward(operands, parts):
    rows, width = operands[12].shape
    vmem, anywhere = pl.BlockSpec(memory_space=pltpu.VMEM), pl.BlockSpec(memory_space=pl.ANY)
    half = {name: PIECES[name][1] * 128 for name in PIECES}
    window = {"q": 48, "r": 48, "d": 32}
    fin = {"q": (32, Q_WIDE), "r": (32, R_WIDE), "d": (16, D_WIDE)}
    scratch = sum_scratch()
    scratch += [pltpu.VMEM((PIECES[name][0], half[name]), BF16) for name in PIECES]
    scratch += [pltpu.VMEM((window[name], half[name]), BF16) for _ in range(3) for name in PIECES]
    scratch += [pltpu.VMEM((window[name], half[name]), F32) for name in PIECES]
    scratch += [pltpu.VMEM((4, 4, 80, 1024), BF16)] * 2
    scratch += [
        pltpu.VMEM((rows, 2 * width), F32),
        pltpu.VMEM((rows, 2 * width), BF16),
        pltpu.VMEM((rows, 2 * width), BF16),
        pltpu.VMEM((rows + 16, width), BF16),
        pltpu.VMEM((rows + 16, Q_WIDE), BF16),
        pltpu.VMEM((rows, width), F32),
        pltpu.VMEM((2, width, 512), BF16),
        pltpu.VMEM((width, 128), BF16),
    ]
    sems = 1 + 3 * (32 + 2 * 4 * 5 + 3)
    scratch += [pltpu.SemaphoreType.DMA((n,)) for n in (sems, sems, 2, 3, 3, 3)]
    scratch += [pltpu.SemaphoreType.DMA((2, 3, 20))]
    spec = [vmem] * len(operands)
    spec[2] = spec[15] = anywhere
    return pl.pallas_call(
        backward_kernel,
        out_shape=tuple(shape(F32, *fin[name]) for name in PIECES)
        + tuple(shape(BF16, 2 * p.shape[0], p.shape[1]) for p in parts)
        + (shape(F32, rows, width),),
        in_specs=spec + [anywhere] * 3,
        out_specs=(vmem,) * 3 + (anywhere,) * 3 + (vmem,),
        scratch_shapes=scratch,
        compiler_params=pltpu.CompilerParams(collective_id=2, has_side_effects=True, vmem_limit_bytes=60 << 20),
        name="attend_back_sums",
    )(*operands, *parts)


PART_AXES = (("y", "z", "g"), ("z", "g", "y"), ("g", "y", "z")) * 2
PARTS = len(PART_AXES)


def lane_cuts(*sizes):
    return tuple((sum(sizes[:i]), n) for i, n in enumerate(sizes))


ROW_CUTS = lane_cuts(4, 4, 3, 3, 3, 3)
LAST_OUT_CUTS = lane_cuts(3, 3, 3, 3, 4, 5)
LAST_BACK_CUTS = lane_cuts(3, 3, 3, 3, 4, 4)


def exchange_kernel(cuts, outward, work, counts, *refs):
    n = len(cuts)
    n_in, n_out, n_scratch = counts
    work_in, refs = refs[n : n + n_in], refs[:n] + refs[n + n_in :]
    work_out, refs = refs[2 * n : 2 * n + n_out], refs[: 2 * n] + refs[2 * n + n_out :]
    work_scratch = refs[4 * n + 3 :]
    stages = [refs[0:n], refs[2 * n : 3 * n], refs[3 * n : 4 * n], refs[n : 2 * n]]
    ssem, rsem, lsem = refs[4 * n : 4 * n + 3]
    hi, y, z, lo, c = place()
    me = {"y": y, "z": z}

    def along(axis, k):
        q = dict(me)
        q[axis] = lax.rem(me[axis] + k, 4)
        return q[axis], device(hi, q["y"], q["z"], lo, c)

    hi_or, c_or, lo_or = (hi, 1 - hi), (c, 1 - c), (lo, 1 - lo)

    def target(d, b):
        if outward:
            return device(hi_or[b], y, z, lo_or[d], hi), lo_or[d] * 2 + hi_or[b], lo * 2 + c, 2 * d + c
        return device(c, y, z, lo_or[d], c_or[b]), lo_or[d] * 2 + c_or[b], lo * 2 + hi, 2 * d + hi

    def source(d, b):
        if outward:
            return device(c, y, z, lo_or[d], c_or[b]), lo_or[d] * 2 + c_or[b], 2 * d + c_or[b]
        return device(hi_or[b], y, z, lo_or[d], hi), lo_or[d] * 2 + hi_or[b], 2 * d + hi_or[b]

    corners = ((1, 1), (0, 1), (1, 0))
    stays = c == hi
    moves = jnp.logical_not(stays)
    bar = pltpu.get_barrier_semaphore()

    def greet_one(to):
        pl.semaphore_signal(bar, inc=1, device_id=to, device_id_type=MESH)

    for axis in "yz":
        for k in (1, 2, 3):
            greet_one(along(axis, k)[1])
    for corner in corners:
        greet_one(source(*corner)[0])

    @pl.when(moves)
    def _():
        greet_one(source(0, 0)[0])
        pl.semaphore_wait(bar, 10 if outward else 11)

    @pl.when(stays)
    def _():
        if not outward:
            greet_one(device(hi, y, z, lo, 1 - c))
        pl.semaphore_wait(bar, 9)

    every = slice(None)

    def view(ref, axis, v, lanes):
        index = {"y": (v, every, every), "z": (every, v, every), "g": (every, every, v)}[axis]
        return ref.at[index + (every, pl.ds(lanes[0] * 128, lanes[1] * 128))]

    def remote(src, dst, k, tag, to):
        return pltpu.make_async_remote_copy(
            src_ref=src, dst_ref=dst, send_sem=ssem.at[k], recv_sem=rsem.at[tag], device_id=to, device_id_type=MESH
        )

    pending = {}
    sent = []
    used = [0, 0]

    def go(part, phase):
        axis = PART_AXES[part][phase]
        waits = []
        for a in range(n):
            src, dst = stages[phase][a], stages[phase + 1][a]
            lanes = cuts[a][part]
            base, kept = used
            used[0] += 4
            used[1] += 1
            if axis != "g":
                own = view(dst, axis, me[axis], lanes)
                for k in (2, 1, 3):
                    v, to = along(axis, k)
                    copy = remote(view(src, axis, v, lanes), own, base + k, base + k, to)
                    copy.start()
                    waits.append(copy.wait_recv)
                    sent.append(copy.wait_send)
                keep = pltpu.make_async_copy(view(src, axis, me[axis], lanes), own, lsem.at[kept])
                keep.start()
                waits.append(keep.wait)
                continue
            for d, b in corners:
                to, there, here, tag = target(d, b)
                copy = remote(view(src, axis, there, lanes), view(dst, axis, here, lanes), base + 2 * d + b, base + tag, to)
                copy.start()
                sent.append(copy.wait_send)
                _from, place_, tag = source(d, b)
                block = view(dst, axis, place_, lanes)
                waits.append(remote(block, block, base + 2 * d + b, base + tag, _from).wait_recv)
            to, there, here, tag = target(0, 0)
            keep = pltpu.make_async_copy(view(src, axis, there, lanes), view(dst, axis, here, lanes), lsem.at[kept])
            copy = remote(view(src, axis, there, lanes), view(dst, axis, here, lanes), base, base + tag, to)
            _from, place_, tag = source(0, 0)
            block = view(dst, axis, place_, lanes)
            coming = remote(block, block, base, base + tag, _from)

            @pl.when(stays)
            def _(keep=keep):
                keep.start()

            @pl.when(moves)
            def _(copy=copy):
                copy.start()

            def wait_corner(keep=keep, coming=coming):
                @pl.when(stays)
                def _():
                    keep.wait()

                @pl.when(moves)
                def _():
                    coming.wait_recv()

            def wait_sent(copy=copy):
                @pl.when(moves)
                def _():
                    copy.wait_send()

            waits.append(wait_corner)
            sent.append(wait_sent)
        pending[part, phase] = waits

    work(-1, work_in, work_out, work_scratch)
    for phase in (0, 1, 2):
        for part in range(PARTS):
            if phase > 0:
                for wait in pending[part, phase - 1]:
                    wait()
            go(part, phase)
        work(phase, work_in, work_out, work_scratch)
    for part in range(PARTS):
        for wait in pending[part, 2]:
            wait()
    work(3, work_in, work_out, work_scratch)
    for wait in sent:
        wait()


def exchange(collective_id, outward, arrays, cuts, work, work_in, work_out, work_scratch=()):
    n = len(arrays)
    split = [a.reshape((4, 4, 4) + a.shape[1:]) for a in arrays]
    shapes = [jax.ShapeDtypeStruct(a.shape, a.dtype) for a in split]
    vmem = pl.BlockSpec(memory_space=pltpu.VMEM)
    out = pl.pallas_call(
        functools.partial(exchange_kernel, cuts, outward, work, (len(work_in), len(work_out), len(work_scratch))),
        out_shape=tuple(shapes) + tuple(work_out),
        in_specs=[pl.BlockSpec(memory_space=pl.ANY)] * (n + len(work_in)),
        out_specs=(pl.BlockSpec(memory_space=pl.ANY),) * n + (vmem,) * len(work_out),
        scratch_shapes=[pltpu.VMEM(s.shape, s.dtype) for s in shapes] * 2
        + [
            pltpu.SemaphoreType.DMA((12 * PARTS * n,)),
            pltpu.SemaphoreType.DMA((12 * PARTS * n,)),
            pltpu.SemaphoreType.DMA((3 * PARTS * n,)),
        ]
        + list(work_scratch),
        compiler_params=pltpu.CompilerParams(
            collective_id=collective_id, has_side_effects=True, vmem_limit_bytes=56 << 20
        ),
        name="exchange_rows",
    )(*split, *work_in)
    return [o.reshape(a.shape) for o, a in zip(out, arrays)] + list(out[n:])


def route_kernel(tok, mixed, routes, out_w, router_w, gains, hidden_one, act, gates_t, slot_t):
    rows, width = tok.shape
    hidden = tok[...].astype(F32) + dot(mixed[...], out_w[...])
    hidden_one[...] = hidden
    router = router_w[...]
    normed, _inv = rms_forward(hidden, gain_rows(gains[...])[1:2])
    low = normed.astype(BF16)
    act[...] = low
    expert = iota((rows, 128), 1)
    named = routes[...]
    member = named[:, 0:1] == expert
    for k in range(1, named.shape[1]):
        member = member | (named[:, k : k + 1] == expert)
    logits = jnp.where(member, dot(low, router), NEG_BIG)
    expo = jnp.where(member, jnp.exp(logits - jnp.max(logits, axis=-1, keepdims=True)), 0.0)
    gates_t[...] = (expo / jnp.sum(expo, axis=-1, keepdims=True)).T
    before = (iota((rows, rows), 1) < iota((rows, rows), 0)).astype(BF16)
    rank = dot(before, member.astype(BF16))
    slot_t[...] = jnp.where(member, rank, -1.0).T


def route(tokens, mixed, routes, w_r, w_q):
    rows, width = tokens.shape
    whole = lambda a: pl.BlockSpec(a.shape, lambda i: (0, 0))
    operands = (tokens, mixed, routes)
    outs = (
        shape(F32, rows, width),
        shape(BF16, rows, width),
        shape(F32, 128, rows),
        shape(F32, 128, rows),
    )
    return pl.pallas_call(
        route_kernel,
        grid=(1,),
        out_shape=outs,
        in_specs=[whole(a) for a in operands]
        + [
            pl.BlockSpec((width, 1280), lambda i: (0, 0)),
            pl.BlockSpec((width, 128), lambda i: (0, ROUTER)),
            pl.BlockSpec((width, 128), lambda i: (0, GAINS)),
        ],
        out_specs=tuple(whole(a) for a in outs),
        compiler_params=pltpu.CompilerParams(vmem_limit_bytes=56 << 20),
        name="route",
    )(*operands, w_r, w_r, w_q)


EVEN = 16


def even_places(slot_t):
    experts, rows = slot_t.shape
    wide = jnp.broadcast_to(slot_t[:, None, :], (experts, EVEN, rows))
    place_of = iota((experts, EVEN, rows), 1).astype(F32)
    return wide == place_of


def dispatch_kernel(act, grad, gates, slot_t, out_r, out_l):
    block, even, _lanes = out_r.shape
    rows, width = act.shape
    here = pl.ds(pl.multiple_of(pl.program_id(0) * block, block), block)
    slots = slot_t[here, :]
    places = even_places(slots)
    last = slots == float(EVEN)
    hot = places.astype(F32).reshape(block * even, rows).astype(BF16)
    last_hot = last.astype(BF16)
    x, g = act[...], grad[...]
    out_r[:, :, :width] = dot(hot, x).astype(BF16).reshape(block, even, width)
    out_r[:, :, width:] = dot(hot, g).astype(BF16).reshape(block, even, width)
    gt = gates[here, :]
    at_slot = jnp.sum(
        jnp.where(places, jnp.broadcast_to(gt[:, None, :], places.shape), 0.0).reshape(block * even, rows),
        axis=-1,
        keepdims=True,
    )
    spread = jnp.broadcast_to(at_slot, (block * even, 128)).reshape(block, even, 128)
    lane_of = iota((block, even, 128), 1) == iota((block, even, 128), 2)
    even_gates = jnp.sum(jnp.where(lane_of, spread, 0.0), axis=1)
    last_gates = jnp.sum(jnp.where(last, gt, 0.0), axis=-1, keepdims=True)
    slot_gates = jnp.where(iota((block, 128), 1) == EVEN, last_gates, even_gates)
    out_l[...] = jnp.concatenate([dot(last_hot, x), dot(last_hot, g), slot_gates], axis=1).reshape(
        block, 1, 2 * width + 128
    )


def dispatch(act, grad, gates_t, slot_t, experts):
    width = act.shape[1]
    block = 8
    whole = lambda a: pl.BlockSpec(a.shape, lambda i: (0, 0))
    cut = lambda n, lanes: pl.BlockSpec((block, n, lanes), lambda i: (i, 0, 0))
    return pl.pallas_call(
        dispatch_kernel,
        grid=(experts // block,),
        out_shape=(
            shape(BF16, experts, EVEN, 2 * width),
            shape(F32, experts, 1, 2 * width + 128),
        ),
        in_specs=[whole(act), whole(grad), whole(gates_t), whole(slot_t)],
        out_specs=(cut(EVEN, 2 * width), cut(1, 2 * width + 128)),
        compiler_params=pltpu.CompilerParams(vmem_limit_bytes=32 << 20),
        name="dispatch",
    )(act, grad, gates_t, slot_t)


def expert_kernel(rows_r, rows_l, o0, o1, o2, e0, e1, e2, out_r, out_l, all_x, all_g, hidden, d_gate, d_up, w_gate, w_up, w_down, sem):
    hi, _y, _z, _lo, c = place()

    def take(sources):
        copies = loads(sources, (w_gate, w_up, w_down), sem)
        for copy in copies:
            copy.start()
        for copy in copies:
            copy.wait()

    @pl.when((pl.program_id(0) == 0) & (c == hi))
    def _():
        take((e0, e1, e2))

    @pl.when((pl.program_id(0) == 0) & (c != hi))
    def _():
        take((o0, o1, o2))

    sources, _one, _lanes = rows_l.shape
    width = rows_r.shape[-1] // 2
    last = rows_l[...].reshape(sources, rows_l.shape[-1])
    even = sources * EVEN
    x = jnp.concatenate([rows_r[:, :, :width].reshape(even, width), last[:, :width].astype(BF16)], axis=0)
    g = jnp.concatenate(
        [rows_r[:, :, width:].reshape(even, width).astype(F32), last[:, width : 2 * width]], axis=0
    )
    sent = last[:, 2 * width :]
    spread = jnp.broadcast_to(sent[:, None, :], (sources, EVEN, 128))
    own = iota((sources, EVEN, 128), 1) == iota((sources, EVEN, 128), 2)
    even_gates = jnp.sum(jnp.where(own, spread, 0.0).reshape(even, 128), axis=-1, keepdims=True)
    last_gates = jnp.sum(jnp.where(iota((sources, 128), 1) == EVEN, sent, 0.0), axis=-1, keepdims=True)
    grad_result = (jnp.concatenate([even_gates, last_gates], axis=0) * g).astype(BF16)
    all_x[...] = x
    all_g[...] = grad_result
    gate = dot(x, w_gate[...])
    up_ = dot(x, w_up[...])
    silu, slope = silu_parts(gate)
    low = (silu * up_).astype(BF16)
    hidden[...] = low
    grad_hidden = dot_t(grad_result, w_down[...])
    grad_gate = (grad_hidden * up_ * slope).astype(BF16)
    grad_up = (grad_hidden * silu).astype(BF16)
    d_gate[...] = grad_gate
    d_up[...] = grad_up
    result = dot(low, w_down[...]).astype(BF16)
    grad_in = (dot_t(grad_gate, w_gate[...]) + dot_t(grad_up, w_up[...])).astype(BF16)
    out_r[:, :, :width] = result[:even].reshape(sources, EVEN, width)
    out_r[:, :, width:] = grad_in[:even].reshape(sources, EVEN, width)
    out_l[...] = jnp.concatenate([result[even:], grad_in[even:]], axis=1).astype(F32).reshape(sources, 1, 2 * width)


def expert(rows_r, rows_l, passed, own):
    devices, _even, width = rows_r.shape
    width = width // 2
    inner = own[0].shape[1]
    steps = 4
    src = devices // steps
    rows = src * (EVEN + 1)
    total = rows * steps
    cut = lambda n, lanes: pl.BlockSpec((src, n, lanes), lambda i: (i, 0, 0))
    flat = lambda lanes: pl.BlockSpec((rows, lanes), lambda i: (i, 0))
    return pl.pallas_call(
        expert_kernel,
        grid=(steps,),
        out_shape=(
            shape(BF16, devices, EVEN, 2 * width),
            shape(F32, devices, 1, 2 * width),
            shape(BF16, total, width),
            shape(BF16, total, width),
            shape(BF16, total, inner),
            shape(BF16, total, inner),
            shape(BF16, total, inner),
        ),
        in_specs=[cut(EVEN, 2 * width), cut(1, rows_l.shape[-1])] + [pl.BlockSpec(memory_space=pl.ANY)] * 6,
        scratch_shapes=[pltpu.VMEM(w.shape, BF16) for w in own] + [pltpu.SemaphoreType.DMA((3,))],
        out_specs=(
            cut(EVEN, 2 * width),
            cut(1, 2 * width),
            flat(width),
            flat(width),
            flat(inner),
            flat(inner),
            flat(inner),
        ),
        compiler_params=pltpu.CompilerParams(vmem_limit_bytes=60 << 20),
        name="expert",
    )(rows_r, rows_l, *passed, *own)


def loads(ins, bufs, sem):
    return [pltpu.make_async_copy(src, dst, sem.at[k]) for k, (src, dst) in enumerate(zip(ins, bufs))]


def shared_work(phase, ins, outs, scratch):
    w_r, *others = ins
    out_s, grad_in, grad_gu, grad_down = outs
    sgu, sdown, act, grad, hidden, sem = scratch
    inner = sdown.shape[0]
    copies = loads([w_r.at[:, pl.ds(1280, 2 * inner)]] + others, (sgu, sdown, act, grad), sem) if phase < 1 else []
    if phase == -1:
        for copy in copies:
            copy.start()
    elif phase == 0:
        for copy in copies:
            copy.wait()
        gate = dot(act[...], sgu[:, :inner])
        up_ = dot(act[...], sgu[:, inner:])
        silu, slope = silu_parts(gate)
        hidden[...] = (silu * up_).astype(BF16)
        grad_hidden = dot_t(grad[...], sdown[...])
        grad_gu[:, :inner] = (grad_hidden * up_ * slope).astype(BF16)
        grad_gu[:, inner:] = (grad_hidden * silu).astype(BF16)
    elif phase == 1:
        out_s[...] = dot(hidden[...], sdown[...])
        grad_in[...] = dot_t(grad_gu[...], sgu[...])
    elif phase == 2:

        @pl.loop(0, inner // 256)
        def _(i):
            r = pl.ds(mul(i * 256, 256), 256)
            grad_down[r, :] = t_dot(hidden[:, r], grad[...]).astype(BF16)


def expert_work(phase, ins, outs, scratch):
    bufs, products, from_sib = scratch[0:5], scratch[5:8], scratch[8:11]
    load_sem, send_sem, recv_sem = scratch[11:]
    all_x, all_g, hidden, d_gate, d_up = bufs
    hi, y, z, lo, c = place()
    copies = loads(ins, bufs, load_sem) if phase < 1 else []

    def swap(k):
        n = products[k].shape[0] // 2
        return pltpu.make_async_remote_copy(
            src_ref=products[k].at[pl.ds(mul((1 - c) * n, 16), n)],
            dst_ref=from_sib[k],
            send_sem=send_sem.at[k],
            recv_sem=recv_sem.at[k],
            device_id=device(hi, y, z, lo, 1 - c),
            device_id_type=MESH,
        )

    def add(k):
        swap(k).wait_recv()
        n = products[k].shape[0] // 2

        @pl.loop(0, n // 64)
        def _(i):
            r = pl.ds(mul(i * 64, 64), 64)
            own = products[k][pl.ds(mul(c * n + i * 64, 64), 64), :]
            outs[k][r, :] = (own.astype(F32) + from_sib[k][r, :].astype(F32)).astype(BF16)

    if phase == -1:
        for copy in copies:
            copy.start()
    elif phase < 2:
        if phase == 0:
            for copy in copies:
                copy.wait()
        grad, out = (d_gate, products[0]) if phase == 0 else (d_up, products[1])

        @pl.loop(0, out.shape[0] // 256)
        def _(i):
            r = pl.ds(mul(i * 256, 256), 256)
            out[r, :] = t_dot(all_x[:, r], grad[...]).astype(BF16)

        swap(phase).start()
    elif phase == 2:

        @pl.loop(0, products[2].shape[0] // 128)
        def _(i):
            r = pl.ds(mul(i * 128, 128), 128)
            products[2][r, :] = t_dot(hidden[:, r], all_g[...]).astype(BF16)

        swap(2).start()
        add(0)
        add(1)
    else:
        add(2)
        for k in range(3):
            swap(k).wait_send()


def split_terms(w):
    top = w.astype(BF16)
    rest = w - top.astype(F32)
    mid = rest.astype(BF16)
    return top, mid, (rest - mid.astype(F32)).astype(BF16)


def combine_kernel(
    back_r, back_l, slot_t, gates_t, grad, hidden_one, out_s, grad_in_s, mixed, act, grad_gu, router_w, out_w, gains,
    layer_out, grad_hidden, grad_mixed, left, right, grad_gain,
):
    experts = back_r.shape[0]
    rows, width = hidden_one.shape
    slots = slot_t[0:experts, :]
    places = even_places(slots)
    last = slots == float(EVEN)
    out_rows = back_r[:, :, :width].reshape(experts * EVEN, width)
    last_l = back_l[...].reshape(experts, 2 * width).astype(BF16)
    gt = gates_t[0:experts, :]
    even_w = jnp.where(places, jnp.broadcast_to(gt[:, None, :], places.shape), 0.0).reshape(experts * EVEN, rows)
    last_w = jnp.where(last, gt, 0.0)
    routed = jnp.zeros((rows, width), F32)
    for e_term, l_term in zip(split_terms(even_w), split_terms(last_w)):
        routed = routed + t_dot(e_term, out_rows) + t_dot(l_term, last_l[:, :width])
    hidden = hidden_one[...]
    layer_out[...] = (hidden + out_s[...] + routed).astype(BF16)
    g = grad[...]
    dots = dot_t(out_rows, g).reshape(experts, EVEN, rows)
    dots_last = dot_t(last_l[:, :width], g)
    grad_gates = jnp.sum(jnp.where(places, dots, 0.0), axis=1) + jnp.where(last, dots_last, 0.0)
    logits_t = gt * (grad_gates - jnp.sum(gt * grad_gates, axis=0, keepdims=True))
    low_logits = jnp.concatenate([logits_t, jnp.zeros((128 - experts, rows), F32)], axis=0).T.astype(BF16)
    hot = places.astype(F32).reshape(experts * EVEN, rows).astype(BF16)
    grad_routed = t_dot(hot, back_r[:, :, width:].reshape(experts * EVEN, width)) + t_dot(last.astype(BF16), last_l[:, width:])
    router = router_w[...]
    grad_act = grad_routed + dot_t(low_logits, router) + grad_in_s[...]
    gain = gain_rows(gains[...])[1:2]
    _normed, inv = rms_forward(hidden, gain)
    grad_norm, gain_sum = rms_backward(hidden, inv, gain, grad_act)
    grad_gain[...] = gain_sum
    total = g.astype(F32) + grad_norm
    grad_hidden[...] = total
    low = total.astype(BF16)
    left[0:rows, :] = mixed[...]
    left[rows:, :] = act[...]
    right[0:rows, :width] = low
    right[0:rows, width:] = jnp.zeros((rows, R_WIDE - width), BF16)
    right[rows:, :width] = jnp.zeros((rows, width), BF16)
    right[rows:, width : ROUTER * 128] = grad_gu[...]
    right[rows:, ROUTER * 128 : (ROUTER + 1) * 128] = low_logits
    right[rows:, (ROUTER + 1) * 128 :] = jnp.zeros((rows, R_WIDE - (ROUTER + 1) * 128), BF16)
    grad_mixed[...] = dot_t(low, out_w[...]).astype(BF16)


def combine(operands, w_r, w_q):
    rows, width = operands[5].shape
    whole = lambda a: pl.BlockSpec(a.shape, lambda i: (0,) * len(a.shape))
    outs = (
        shape(BF16, rows, width),
        shape(F32, rows, width),
        shape(BF16, rows, width),
        shape(BF16, 2 * rows, width),
        shape(BF16, 2 * rows, R_WIDE),
        shape(F32, 1, width),
    )
    return pl.pallas_call(
        combine_kernel,
        grid=(1,),
        out_shape=outs,
        in_specs=[whole(a) for a in operands]
        + [
            pl.BlockSpec((width, 128), lambda i: (0, ROUTER)),
            pl.BlockSpec((width, 1280), lambda i: (0, 0)),
            pl.BlockSpec((width, 128), lambda i: (0, GAINS)),
        ],
        out_specs=tuple(whole(a) for a in outs),
        compiler_params=pltpu.CompilerParams(vmem_limit_bytes=56 << 20),
        name="combine",
    )(*operands, w_r, w_r, w_q)


def per_device(
    tokens,
    cotangent,
    segments,
    routes,
    norm_gain_attn,
    w_query,
    w_key,
    w_value,
    w_out,
    norm_gain_ffn,
    w_router,
    shared_gate,
    shared_up,
    shared_down,
    expert_gate,
    expert_up,
    expert_down,
):
    rows = tokens.shape[1]
    width = tokens.shape[2]
    experts = w_router.shape[1]
    tokens, grad, routes = tokens[0], cotangent[0], routes[0]
    seg_row = segments
    seg_col = segments.reshape(-1, 1)
    own_experts = (expert_gate[0], expert_up[0], expert_down[0])

    def spread(w):
        w = w.reshape(w.shape[0], experts, w.shape[1] // experts)
        return jnp.pad(w, ((0, 0), (0, 0), (0, 2))).reshape(w.shape[0], experts * 16)

    own_rows = w_query.shape[0]
    zeros = lambda n: jnp.zeros((own_rows, n), BF16)
    shard_q = jnp.concatenate(
        [w_query, w_key, w_value, norm_gain_attn[:, None], norm_gain_ffn[:, None], zeros(254)], axis=1
    )
    shard_r = jnp.concatenate([w_out, spread(shared_gate), spread(shared_up), w_router, zeros(256 - experts)], axis=1)
    cos, sin = rotary_tables(2 * rows)
    w_q, w_r, w_d, expert_w, act_attn, q, kv, prior, mixed = forward(
        shard_q, shard_r, shared_down, own_experts, tokens, cos, sin, seg_row, seg_col
    )
    hidden_one, act_ffn, gates_t, slot_t = route(tokens, mixed, routes, w_r, w_q)
    rows_r, rows_l = dispatch(act_ffn, grad, gates_t, slot_t, experts)
    rows_r, rows_l, out_s, grad_in_s, grad_gu, grad_sdown = exchange(
        3,
        True,
        (rows_r, rows_l),
        (ROW_CUTS, LAST_OUT_CUTS),
        shared_work,
        (w_r, w_d, act_ffn, grad),
        (shape(F32, rows, width), shape(F32, rows, width), shape(BF16, rows, 2048), shape(BF16, 1024, width)),
        (
            pltpu.VMEM((width, 2048), BF16),
            pltpu.VMEM((1024, width), BF16),
            pltpu.VMEM((rows, width), BF16),
            pltpu.VMEM((rows, width), BF16),
            pltpu.VMEM((rows, 1024), BF16),
            pltpu.SemaphoreType.DMA((4,)),
        ),
    )
    out_r, out_l, *kept = expert(rows_r, rows_l, expert_w, own_experts)
    back_r, back_l, *parts = exchange(
        4,
        False,
        (out_r, out_l),
        (ROW_CUTS, LAST_BACK_CUTS),
        expert_work,
        tuple(kept),
        tuple(shape(BF16, w.shape[0] // 2, w.shape[1]) for w in own_experts),
        [pltpu.VMEM(a.shape, BF16) for a in kept]
        + [pltpu.VMEM(w.shape, BF16) for w in own_experts]
        + [pltpu.VMEM((w.shape[0] // 2, w.shape[1]), BF16) for w in own_experts]
        + [pltpu.SemaphoreType.DMA((n,)) for n in (5, 3, 3)],
    )
    layer_out, grad_hidden, grad_mixed, left_r, right_r, gain_ffn = combine(
        (back_r, back_l, slot_t, gates_t, grad, hidden_one, out_s, grad_in_s, mixed, act_ffn, grad_gu), w_r, w_q
    )
    fin_q, fin_r, fin_d, *sums, grad_tokens = backward(
        (left_r, right_r, grad_sdown.reshape(4, 4, 64, width), act_attn, q, kv, prior, seg_row, seg_col)
        + (grad_mixed, cos, sin, tokens, grad_hidden, gain_ffn, w_q),
        parts,
    )
    offset = 4 * lax.rem(lax.axis_index("exp"), 4)
    own_q = lax.dynamic_slice(fin_q, (offset, 0), (own_rows, Q_WIDE))
    own_r = lax.dynamic_slice(fin_r, (offset, 0), (own_rows, R_WIDE))

    def gathered_hidden(w):
        return w.reshape(w.shape[0], experts, 16)[:, :, :14].reshape(w.shape[0], experts * 14)

    core = lax.rem(lax.axis_index("exp"), 2)
    kept_here = (core == lax.axis_index("seq")) & (jnp.arange(2) == core)
    expert_grads = [
        jnp.where(kept_here[:, None, None], own[None], total.reshape((2,) + own.shape)).astype(F32).reshape(1, *total.shape)
        for own, total in zip(parts, sums)
    ]
    router = ROUTER * 128
    return (
        layer_out[None],
        grad_tokens[None],
        own_q[:, GAINS * 128],
        own_q[:, :1280],
        own_q[:, 1280:2560],
        own_q[:, 2560:3840],
        own_r[:, :1280],
        own_q[:, GAINS * 128 + 1],
        own_r[:, router : router + experts],
        gathered_hidden(own_r[:, 1280:2304]),
        gathered_hidden(own_r[:, 2304:3328]),
        fin_d[:14],
        *expert_grads,
    )


def solution(mesh):
    rows = P("exp", None)
    deep = P("exp", None, None)
    split = P("exp", "seq", None)
    gain = P("exp")
    in_specs = (split, split, rows, split, gain, rows, rows, rows, rows, gain) + (rows,) * 4 + (deep,) * 3
    out_specs = (split, split, gain, rows, rows, rows, rows, gain) + (rows,) * 4 + (deep,) * 3
    return jax.shard_map(per_device, mesh=mesh, in_specs=in_specs, out_specs=out_specs, check_vma=False)
```

time: 528 us -> 460 us (0.87)
  waiting for transfers between devices: 24.7 us -> 0 us
  Pallas kernels: 443 us -> 419 us
  local copies, waits for them, and re-layouts: 36.1 us -> 25 us
    ppermute x2 -> x0, waiting for transfers between devices: 24.7 us -> none  [the longest x1 17.4 us: per_device(): later = lax.ppermute(grad_prior, 'seq', [(1, 0)])]
    pallas_call x7 -> x3, Pallas kernels: 249 us -> 225 us  [the longest x1 136 us: backward(): pl.pallas_call(backward_kernel, out_shape=tuple((shape(F32, *fin[name]) f...]
    convert_element_type x0 -> x2, other arithmetic: none -> 11.2 us  [per_device(): jnp.where(kept_here[:, None, None], own[None], total.reshape((2,) + own.s...]
    broadcast_in_dim x2 -> x0, other arithmetic: 10.1 us -> none  [per_device(): expert_grads = [a.astype(F32)[None] for a in sums]]
    unnamed x56 -> x51, local copies, waits for them, and re-layouts: 16.3 us -> 8.21 us
  transfers between devices with their start and end apart: 2 -> 0, of which waited for: 2 -> 0; matrix products, arithmetic and copies ran while one was open for 1% -> 0% of each run, Pallas kernels for 0% -> 0%
where the time goes in v4:
time: 460 us; the launch traced here: 456 us
  Pallas kernels  419 us (91%)
  local copies, waits for them, and re-layouts  25 us (5%)
  other arithmetic  11.2 us (2%)
    pallas_call x2, Pallas kernels, exchange(): pl.pallas_call(functools.partial(exchange_kernel, cuts, outward, work, (l...  154 us
    pallas_call x1, Pallas kernels, backward(): pl.pallas_call(backward_kernel, out_shape=tuple((shape(F32, *fin[name]) f...  136 us
    pallas_call x1, Pallas kernels, forward(): pl.pallas_call(forward_kernel, out_shape=(shape(BF16, 4, 4, 80, Q_WIDE),...  85.2 us
    pallas_call x1, Pallas kernels, expert(): pl.pallas_call(expert_kernel, grid=(steps,), out_shape=(shape(BF16, devic...  24.4 us
    pallas_call x1, Pallas kernels, combine(): pl.pallas_call(combine_kernel, grid=(1,), out_shape=outs, in_specs=[whole...  11.3 us
    convert_element_type x2, other arithmetic, per_device(): jnp.where(kept_here[:, None, None], own[None], total.reshape((2,) + own.s...  11.2 us

profile of v4, /device:TPU:1, one launch (start us, length us, event | category | flops | bytes accessed | tf_op | source)
XLA Modules:
  0.0 456.0 jit_solution(6565999136088097843)
XLA Ops:
  0.7 1.5 reshape.134
  2.3 0.0 copy-start.19
  2.3 0.0 copy-start.18
  2.3 0.1 pad.11
  2.4 0.4 reshape.135
  2.8 1.4 reshape.136
  4.2 0.1 pad.12
  4.3 0.4 reshape.137
  4.8 0.1 concatenate.7
  4.9 1.2 dynamic_update_slice.7.win_r
  6.1 0.0 copy-start.10
  6.2 0.1 copy.37
  6.3 0.1 copy.38
  6.4 0.1 concatenate.6
  6.5 1.2 dynamic_update_slice.6.win_q
  7.7 0.0 copy-start.9
  7.7 0.8 copy.39.seg_col
  8.5 0.6 pad.13.win_d
  9.2 0.0 copy-done.9
  9.2 85.2 %gather_attend.1 = (bf16[4,4,80,4096]{3,2,1,0:T(8,128)(2,1)}, bf16[4,4,80,3584]{3,2,1,0:T(8,128)(2,1)}, bf16[4,4,64,1280]{3,2,1,0:T(8,128)(2,1)}, bf16[1280,896]...) custom-call(bf16[32,4096]{1,0:T(8,128)(2,1)} %copy-done.9, ...), custom_call_target="tpu_custom_call" | custom-call | tf_op jit(solution)/shard_map/gather_attend/pallas_call | solution.py:482
  94.4 0.7 copy.40
  95.1 4.2 route.1
  99.4 1.0 copy-done.2
  100.3 0.8 copy-done.4
  101.2 0.8 copy-done.5
  102.0 3.2 dispatch.1
  105.2 2.4 copy-done
  107.6 0.8 copy-done.3
  108.5 80.4 %exchange_rows.2 = (bf16[4,4,4,16,2560]{4,3,2,1,0:T(8,128)(2,1)}, f32[4,4,4,1,2688]{4,3,2,1,0:T(1,128)}, f32[128,1280]{1,0:T(8,128)}, f32[128,1280]{1,0:T(8,128)...) custom-call(bf16[4,4,4,16,2560]{4,3,2,1,0:T(8,128)(2,1)} %bitcast.47, f32[4,4,4,1,2688]{4,3,2,1,0:T(1,128)} %bitcast.51, ...), custom_call_target="tpu_custom_call" | custom-call | tf_op jit(solution)/shard_map/exchange_rows/pallas_call | solution.py:1115
  188.8 24.4 %expert.1 = (bf16[64,16,2560]{2,1,0:T(8,128)(2,1)}, f32[64,1,2560]{2,1,0:T(1,128)}, bf16[1088,1280]{1,0:T(8,128)(2,1)}, bf16[1088,1280]{1,0:T(8,128)(2,1)}, bf16...) custom-call(bf16[64,16,2560]{2,1,0:T(8,128)(2,1)} %bitcast.68, ...), custom_call_target="tpu_custom_call" | custom-call | tf_op jit(solution)/shard_map/expert/pallas_call | solution.py:1300
  213.3 73.9 %exchange_rows.3 = (bf16[4,4,4,16,2560]{4,3,2,1,0:T(8,128)(2,1)}, f32[4,4,4,1,2560]{4,3,2,1,0:T(1,128)}, bf16[640,896]{1,0:T(8,128)(2,1)}, bf16[640,896]{1,0:T(8,128)(2,1)}, bf16[448,1280]{1,0:T(8,128)(2,1)}) custom-call(bf16[4,4,4,16,2560]{4,3,2,1,0:T(8,128)(2,1)} %bitcast.67, f32[4,4,4,1,2560]{4,3,2,1,0:T(1,128)} %bitcast.77, ...), custom_call_target="tpu_custom_call" | custom-call | tf_op jit(solution)/shard_map/exchange_rows/pallas_call | solution.py:1115
  287.2 11.3 %combine.1 = (bf16[128,1280]{1,0:T(8,128)(2,1)}, f32[128,1280]{1,0:T(8,128)}, bf16[128,1280]{1,0:T(8,128)(2,1)}, bf16[256,1280]{1,0:T(8,128)(2,1)}, bf16[256,3584]{1,0:T(8,128)(2,1)}, /*index=5*/f32[1,1280]{1,0:T(1,128)}) custom-call(bf16[64,16,2560]{2,1,0:T(8,128)(2,1)} %bitcast.66, f32[64,1,2560]{2,1,0:T(1,128)} %bitcast.79, ...), custom_call_target="tpu_custom_call" | custom-call | tf_op jit(solution)/shard_map/combine/pallas_call | solution.py:1486
  298.5 135.9 %attend_back_sums.1 = (f32[32,4096]{1,0:T(8,128)}, f32[32,3584]{1,0:T(8,128)}, f32[16,1280]{1,0:T(8,128)}, bf16[1280,896]{1,0:T(8,128)(2,1)}, bf16[1280,896]{1,0...) custom-call(bf16[256,1280]{1,0:T(8,128)(2,1)} %get-tuple-element.91.left_r, ...), custom_call_target="tpu_custom_call" | custom-call | tf_op jit(solution)/shard_map/attend_back_sums/pallas_call | solution.py:938
  434.5 0.1 broadcast_in_dim.99
  434.6 0.1 broadcast_in_dim.100
  434.7 4.3 bitcast_convert_fusion
  439.0 0.1 broadcast_in_dim.92
  439.1 6.9 %bitcast_convert_fusion.1 = (f32[1,1280,896]{2,1,0:T(8,128)}, f32[1,1280,896]{2,1,0:T(8,128)}) fusion(bf16[1280,896]{1,0:T(8,128)(2,1)} %get-tuple-element.109, pred[1280]{0:T(1024)(128)(4,1)S(1)} %broadcast_in_dim.93, bf16[640,896]{1,0:T(8,128)(2,1)S(1)} %copy-done.7, bf16[1280,896]{1,0:T(8,128)(2,1)} %get-tuple-element.108, bf16[640,896]{1,0:T(8,128)(2,1)S(1)} %copy-done.6), kind=kLoop, calls=%fused_computation.1 | loop fusion | flops 4587520 | bytes 16057600 | tf_op jit(solution)/shard_map/convert_element_type | solution.py:1594
  446.0 1.8 fusion
  447.8 1.1 fusion.1
  448.9 0.2 reshape.151
  449.1 1.0 reshape.152
  450.1 0.2 reshape.153
  450.4 1.0 reshape.154
  451.4 1.4 dynamic-slice.6
  452.7 1.5 dynamic-slice_reduce_fusion
  454.2 0.8 copy.46
  455.1 0.6 copy.47
  (44 shorter events, 0.1 us)
Async XLA Ops:
  0.6 4.1 copy-start.17
  0.7 4.1 copy-start.20
  0.7 5.5 %copy-start.22 = (bf16[20]{0:T(256)(128)(2,1)S(1)}, bf16[20]{0:T(256)(128)(2,1)}, u32[]{:S(2)}) copy-start(bf16[20]{0:T(256)(128)(2,1)} %param.23) | copy-start | bytes 124
  0.7 5.6 %copy-start.23 = (bf16[20]{0:T(256)(128)(2,1)S(1)}, bf16[20]{0:T(256)(128)(2,1)}, u32[]{:S(2)}) copy-start(bf16[20]{0:T(256)(128)(2,1)} %param.28) | copy-start | bytes 124
  0.7 5.7 %copy-start.14 = (bf16[20,1280]{1,0:T(8,128)(2,1)S(1)}, bf16[20,1280]{1,0:T(8,128)(2,1)}, u32[]{:S(2)}) copy-start(bf16[20,1280]{1,0:T(8,128)(2,1)} %param.24) | copy-start | bytes 153604
  0.7 5.7 %copy-start.15 = (bf16[20,1280]{1,0:T(8,128)(2,1)S(1)}, bf16[20,1280]{1,0:T(8,128)(2,1)}, u32[]{:S(2)}) copy-start(bf16[20,1280]{1,0:T(8,128)(2,1)} %param.25) | copy-start | bytes 153604
  0.7 5.7 %copy-start.16 = (bf16[20,1280]{1,0:T(8,128)(2,1)S(1)}, bf16[20,1280]{1,0:T(8,128)(2,1)}, u32[]{:S(2)}) copy-start(bf16[20,1280]{1,0:T(8,128)(2,1)} %param.26) | copy-start | bytes 153604
  2.3 5.5 %copy-start.19 = (s32[1,256]{1,0:T(1,128)S(1)}, s32[1,256]{1,0:T(1,128)}, u32[]{:S(2)}) copy-start(s32[1,256]{1,0:T(1,128)} %seg_row.3) | copy-start | bytes 3076
  2.3 6.3 %copy-start.18 = (bf16[14,1280]{1,0:T(8,128)(2,1)S(1)}, bf16[14,1280]{1,0:T(8,128)(2,1)}, u32[]{:S(2)}) copy-start(bf16[14,1280]{1,0:T(8,128)(2,1)} %param.32) | copy-start | bytes 107524
  6.1 3.0 copy-start.10
  7.7 1.5 copy-start.9
  9.2 85.2 %copy-start.21 = (s32[1,128,7]{1,0,2:T(1,128)S(1)}, s32[1,128,7]{1,0,2:T(1,128)}, u32[]{:S(2)}) copy-start(s32[1,128,7]{1,0,2:T(1,128)} %param.22) | copy-start | bytes 10756
  95.1 4.2 copy-start.1
  99.4 1.0 copy-start.2
  100.3 0.8 copy-start.4
  101.2 0.8 copy-start.5
  105.2 2.4 copy-start
  107.6 0.8 copy-start.3
  298.5 136.1 %copy-start.8 = (bf16[448,1280]{1,0:T(8,128)(2,1)S(1)}, bf16[448,1280]{1,0:T(8,128)(2,1)}, u32[]{:S(2)}) copy-start(bf16[448,1280]{1,0:T(8,128)(2,1)} %get-tuple-element.103.p2) | copy-start | bytes 3440644
  434.7 4.4 copy-start.6
  434.7 4.4 copy-start.7
  439.1 6.9 %copy-start.12 = (f32[32,4096]{1,0:T(8,128)S(1)}, f32[32,4096]{1,0:T(8,128)}, u32[]{:S(2)}) copy-start(f32[32,4096]{1,0:T(8,128)} %get-tuple-element.105) | copy-start | bytes 1572868
  446.0 8.3 %copy-start.11 = (f32[128,1280]{1,0:T(8,128)S(1)}, f32[128,1280]{1,0:T(8,128)}, u32[]{:S(2)}) copy-start(f32[128,1280]{1,0:T(8,128)} %get-tuple-element.104) | copy-start | bytes 1966084
  448.9 6.2 %copy-start.13 = (f32[16,1280]{1,0:T(8,128)S(1)}, f32[16,1280]{1,0:T(8,128)}, u32[]{:S(2)}) copy-start(f32[16,1280]{1,0:T(8,128)} %get-tuple-element.107) | copy-start | bytes 245764

commit v5 on v4

--- a/solution.py
+++ b/solution.py
@@ -950,6 +950,7 @@
 
 PART_AXES = (("y", "z", "g"), ("z", "g", "y"), ("g", "y", "z")) * 2
 PARTS = len(PART_AXES)
+TURNS = (2, 1, 3, 0)
 
 
 def lane_cuts(*sizes):
@@ -961,179 +962,209 @@
 LAST_BACK_CUTS = lane_cuts(3, 3, 3, 3, 4, 4)
 
 
-def exchange_kernel(cuts, outward, work, counts, *refs):
-    n = len(cuts)
-    n_in, n_out, n_scratch = counts
-    work_in, refs = refs[n : n + n_in], refs[:n] + refs[n + n_in :]
-    work_out, refs = refs[2 * n : 2 * n + n_out], refs[: 2 * n] + refs[2 * n + n_out :]
-    work_scratch = refs[4 * n + 3 :]
-    stages = [refs[0:n], refs[2 * n : 3 * n], refs[3 * n : 4 * n], refs[n : 2 * n]]
-    ssem, rsem, lsem = refs[4 * n : 4 * n + 3]
-    hi, y, z, lo, c = place()
-    me = {"y": y, "z": z}
-
-    def along(axis, k):
-        q = dict(me)
-        q[axis] = lax.rem(me[axis] + k, 4)
+class Exchange:
+    def __init__(self, outward, cuts, stages, sems, spot):
+        self.outward, self.cuts, self.stages, self.spot = outward, cuts, stages, spot
+        self.ssem, self.rsem, self.lsem = sems
+        hi, y, z, lo, c = spot
+        self.stays = c == hi
+        self.moves = jnp.logical_not(self.stays)
+        self.pending, self.sent, self.used = {}, [], [0, 0]
+
+    def along(self, axis, k):
+        hi, y, z, lo, c = self.spot
+        q = {"y": y, "z": z}
+        q[axis] = lax.rem(q[axis] + k, 4)
         return q[axis], device(hi, q["y"], q["z"], lo, c)
 
-    hi_or, c_or, lo_or = (hi, 1 - hi), (c, 1 - c), (lo, 1 - lo)
-
-    def target(d, b):
-        if outward:
-            return device(hi_or[b], y, z, lo_or[d], hi), lo_or[d] * 2 + hi_or[b], lo * 2 + c, 2 * d + c
-        return device(c, y, z, lo_or[d], c_or[b]), lo_or[d] * 2 + c_or[b], lo * 2 + hi, 2 * d + hi
-
-    def source(d, b):
-        if outward:
-            return device(c, y, z, lo_or[d], c_or[b]), lo_or[d] * 2 + c_or[b], 2 * d + c_or[b]
-        return device(hi_or[b], y, z, lo_or[d], hi), lo_or[d] * 2 + hi_or[b], 2 * d + hi_or[b]
+    def target(self, d, b):
+        hi, y, z, lo, c = self.spot
+        lo_, hi_, c_ = (lo, 1 - lo)[d], (hi, 1 - hi)[b], (c, 1 - c)[b]
+        if self.outward:
+            return device(hi_, y, z, lo_, hi), lo_ * 2 + hi_, lo * 2 + c, 2 * d + c
+        return device(c, y, z, lo_, c_), lo_ * 2 + c_, lo * 2 + hi, 2 * d + hi
+
+    def source(self, d, b):
+        hi, y, z, lo, c = self.spot
+        lo_, hi_, c_ = (lo, 1 - lo)[d], (hi, 1 - hi)[b], (c, 1 - c)[b]
+        if self.outward:
+            return device(c, y, z, lo_, c_), lo_ * 2 + c_, 2 * d + c_
+        return device(hi_, y, z, lo_, hi), lo_ * 2 + hi_, 2 * d + hi_
 
     corners = ((1, 1), (0, 1), (1, 0))
-    stays = c == hi
-    moves = jnp.logical_not(stays)
-    bar = pltpu.get_barrier_semaphore()
-
-    def greet_one(to):
-        pl.semaphore_signal(bar, inc=1, device_id=to, device_id_type=MESH)
-
-    for axis in "yz":
-        for k in (1, 2, 3):
-            greet_one(along(axis, k)[1])
-    for corner in corners:
-        greet_one(source(*corner)[0])
-
-    @pl.when(moves)
-    def _():
-        greet_one(source(0, 0)[0])
-        pl.semaphore_wait(bar, 10 if outward else 11)
-
-    @pl.when(stays)
-    def _():
-        if not outward:
-            greet_one(device(hi, y, z, lo, 1 - c))
-        pl.semaphore_wait(bar, 9)
-
-    every = slice(None)
-
-    def view(ref, axis, v, lanes):
-        index = {"y": (v, every, every), "z": (every, v, every), "g": (every, every, v)}[axis]
-        return ref.at[index + (every, pl.ds(lanes[0] * 128, lanes[1] * 128))]
-
-    def remote(src, dst, k, tag, to):
+
+    def greet(self):
+        hi, y, z, lo, c = self.spot
+        bar = pltpu.get_barrier_semaphore()
+
+        def greet_one(to):
+            pl.semaphore_signal(bar, inc=1, device_id=to, device_id_type=MESH)
+
+        for axis in "yz":
+            for k in (1, 2, 3):
+                greet_one(self.along(axis, k)[1])
+        for corner in self.corners:
+            greet_one(self.source(*corner)[0])
+
+        @pl.when(self.moves)
+        def _():
+            greet_one(self.source(0, 0)[0])
+            pl.semaphore_wait(bar, 10 if self.outward else 11)
+
+        @pl.when(self.stays)
+        def _():
+            if not self.outward:
+                greet_one(device(hi, y, z, lo, 1 - c))
+            pl.semaphore_wait(bar, 9)
+
+    def view(self, ref, axis, v, cut, at):
+        every = slice(None)
+        first = every if at is None else at
+        index = {"y": (v, every, every), "z": (first, v, every), "g": (first, every, v)}[axis]
+        return ref.at[index + (every, pl.ds(cut[0] * 128, cut[1] * 128))]
+
+    def remote(self, src, dst, k, tag, to):
         return pltpu.make_async_remote_copy(
-            src_ref=src, dst_ref=dst, send_sem=ssem.at[k], recv_sem=rsem.at[tag], device_id=to, device_id_type=MESH
+            src_ref=src,
+            dst_ref=dst,
+            send_sem=self.ssem.at[k],
+            recv_sem=self.rsem.at[tag],
+            device_id=to,
+            device_id_type=MESH,
         )
 
-    pending = {}
-    sent = []
-    used = [0, 0]
-
-    def go(part, phase):
+    def go(self, part, phase, turn=None, at=None):
         axis = PART_AXES[part][phase]
-        waits = []
-        for a in range(n):
-            src, dst = stages[phase][a], stages[phase + 1][a]
-            lanes = cuts[a][part]
-            base, kept = used
-            used[0] += 4
-            used[1] += 1
+        hi, y, z, lo, c = self.spot
+        waits = self.pending.setdefault((part, phase), [])
+        for a, cuts in enumerate(self.cuts):
+            src, dst = self.stages[phase][a], self.stages[phase + 1][a]
+            cut = cuts[part]
+            base, kept = self.used
+            self.used[0] += 4
+            self.used[1] += 1
             if axis != "g":
-                own = view(dst, axis, me[axis], lanes)
-                for k in (2, 1, 3):
-                    v, to = along(axis, k)
-                    copy = remote(view(src, axis, v, lanes), own, base + k, base + k, to)
+                here = y if axis == "y" else z
+                rows = at if axis == "z" else None
+                own = self.view(dst, axis, here, cut, rows)
+                for k in (turn,) if axis == "y" and turn is not None else TURNS:
+                    v, to = self.along(axis, k)
+                    if k == 0:
+                        keep = pltpu.make_async_copy(self.view(src, axis, here, cut, rows), own, self.lsem.at[kept])
+                        keep.start()
+                        waits.append(keep.wait)
+                        continue
+                    copy = self.remote(self.view(src, axis, v, cut, rows), own, base + k, base + k, to)
                     copy.start()
                     waits.append(copy.wait_recv)
-                    sent.append(copy.wait_send)
-                keep = pltpu.make_async_copy(view(src, axis, me[axis], lanes), own, lsem.at[kept])
-                keep.start()
-                waits.append(keep.wait)
+                    self.sent.append(copy.wait_send)
                 continue
-            for d, b in corners:
-                to, there, here, tag = target(d, b)
-                copy = remote(view(src, axis, there, lanes), view(dst, axis, here, lanes), base + 2 * d + b, base + tag, to)
+            for d, b in self.corners:
+                to, there, here, tag = self.target(d, b)
+                copy = self.remote(
+                    self.view(src, axis, there, cut, at), self.view(dst, axis, here, cut, at), base + 2 * d + b, base + tag, to
+                )
                 copy.start()
-                sent.append(copy.wait_send)
-                _from, place_, tag = source(d, b)
-                block = view(dst, axis, place_, lanes)
-                waits.append(remote(block, block, base + 2 * d + b, base + tag, _from).wait_recv)
-            to, there, here, tag = target(0, 0)
-            keep = pltpu.make_async_copy(view(src, axis, there, lanes), view(dst, axis, here, lanes), lsem.at[kept])
-            copy = remote(view(src, axis, there, lanes), view(dst, axis, here, lanes), base, base + tag, to)
-            _from, place_, tag = source(0, 0)
-            block = view(dst, axis, place_, lanes)
-            coming = remote(block, block, base, base + tag, _from)
-
-            @pl.when(stays)
-            def _(keep=keep):
-                keep.start()
-
-            @pl.when(moves)
-            def _(copy=copy):
-                copy.start()
-
-            def wait_corner(keep=keep, coming=coming):
-                @pl.when(stays)
-                def _():
-                    keep.wait()
-
-                @pl.when(moves)
-                def _():
-                    coming.wait_recv()
-
-            def wait_sent(copy=copy):
-                @pl.when(moves)
-                def _():
-                    copy.wait_send()
-
-            waits.append(wait_corner)
-            sent.append(wait_sent)
-        pending[part, phase] = waits
-
-    work(-1, work_in, work_out, work_scratch)
-    for phase in (0, 1, 2):
+                self.sent.append(copy.wait_send)
+                sender, place_, tag = self.source(d, b)
+                block = self.view(dst, axis, place_, cut, at)
+                waits.append(self.remote(block, block, base + 2 * d + b, base + tag, sender).wait_recv)
+            self.go_corner(src, dst, cut, at, base, kept, waits)
+
+    def go_corner(self, src, dst, cut, at, base, kept, waits):
+        to, there, here, tag = self.target(0, 0)
+        mine, landing = self.view(src, "g", there, cut, at), self.view(dst, "g", here, cut, at)
+        keep = pltpu.make_async_copy(mine, landing, self.lsem.at[kept])
+        copy = self.remote(mine, landing, base, base + tag, to)
+        sender, place_, tag = self.source(0, 0)
+        block = self.view(dst, "g", place_, cut, at)
+        coming = self.remote(block, block, base, base + tag, sender)
+
+        @pl.when(self.stays)
+        def _():
+            keep.start()
+
+        @pl.when(self.moves)
+        def _():
+            copy.start()
+
+        def wait_corner():
+            @pl.when(self.stays)
+            def _():
+                keep.wait()
+
+            @pl.when(self.moves)
+            def _():
+                coming.wait_recv()
+
+        def wait_sent():
+            @pl.when(self.moves)
+            def _():
+                copy.wait_send()
+
+        waits.append(wait_corner)
+        self.sent.append(wait_sent)
+
+    def first(self, turn, at):
         for part in range(PARTS):
-            if phase > 0:
-                for wait in pending[part, phase - 1]:
-                    wait()
-            go(part, phase)
-        work(phase, work_in, work_out, work_scratch)
-    for part in range(PARTS):
-        for wait in pending[part, 2]:
+            self.go(part, 0, turn, at)
+
+    def next(self, phase):
+        for part in range(PARTS):
+            self.wait(part, phase - 1)
+            self.go(part, phase)
+
+    def wait(self, part, phase):
+        for wait in self.pending[part, phase]:
             wait()
-    work(3, work_in, work_out, work_scratch)
-    for wait in sent:
-        wait()
-
-
-def exchange(collective_id, outward, arrays, cuts, work, work_in, work_out, work_scratch=()):
-    n = len(arrays)
-    split = [a.reshape((4, 4, 4) + a.shape[1:]) for a in arrays]
-    shapes = [jax.ShapeDtypeStruct(a.shape, a.dtype) for a in split]
-    vmem = pl.BlockSpec(memory_space=pltpu.VMEM)
-    out = pl.pallas_call(
-        functools.partial(exchange_kernel, cuts, outward, work, (len(work_in), len(work_out), len(work_scratch))),
-        out_shape=tuple(shapes) + tuple(work_out),
-        in_specs=[pl.BlockSpec(memory_space=pl.ANY)] * (n + len(work_in)),
-        out_specs=(pl.BlockSpec(memory_space=pl.ANY),) * n + (vmem,) * len(work_out),
-        scratch_shapes=[pltpu.VMEM(s.shape, s.dtype) for s in shapes] * 2
-        + [
-            pltpu.SemaphoreType.DMA((12 * PARTS * n,)),
-            pltpu.SemaphoreType.DMA((12 * PARTS * n,)),
-            pltpu.SemaphoreType.DMA((3 * PARTS * n,)),
-        ]
-        + list(work_scratch),
-        compiler_params=pltpu.CompilerParams(
-            collective_id=collective_id, has_side_effects=True, vmem_limit_bytes=56 << 20
-        ),
-        name="exchange_rows",
-    )(*split, *work_in)
-    return [o.reshape(a.shape) for o, a in zip(out, arrays)] + list(out[n:])
-
-
-def route_kernel(tok, mixed, routes, out_w, router_w, gains, hidden_one, act, gates_t, slot_t):
+
+    def finish(self):
+        for part in range(PARTS):
+            self.wait(part, 2)
+        for wait in self.sent:
+            wait()
+
+
+def exchange_sems(arrays):
+    return [pltpu.SemaphoreType.DMA((n * arrays,)) for n in (160, 160, 40)]
+
+
+EVEN = 16
+
+
+def even_places(slot_t):
+    experts, rows = slot_t.shape
+    wide = jnp.broadcast_to(slot_t[:, None, :], (experts, EVEN, rows))
+    return wide == iota((experts, EVEN, rows), 1).astype(F32)
+
+
+def loads(ins, bufs, sem, start=0):
+    return [pltpu.make_async_copy(src, dst, sem.at[start + k]) for k, (src, dst) in enumerate(zip(ins, bufs))]
+
+
+def route_kernel(
+    tok, mixed, routes, grad, w_q, w_r, w_d,
+    out_r, out_l, hidden_one, act, gates_t, slot_t, out_s, grad_in, grad_gu, grad_down,
+    src_r, src_l, b1_r, b1_l, b2_r, b2_l, out_w, router_w, gains, sgu, sdown, hidden_s, ssem, rsem, lsem, wsem,
+):
+    spot = place()
+    y = spot[1]
     rows, width = tok.shape
+    inner = sdown.shape[0]
+    first_loads = loads(
+        (w_r.at[:, pl.ds(0, width)], w_r.at[:, pl.ds(ROUTER * 128, 128)], w_q.at[:, pl.ds(GAINS * 128, 128)]),
+        (out_w, router_w, gains),
+        wsem,
+    )
+    later_loads = loads((w_r.at[:, pl.ds(width, 2 * inner)], w_d), (sgu, sdown), wsem, 3)
+    for copy in first_loads + later_loads:
+        copy.start()
+    swap = Exchange(
+        True, (ROW_CUTS, LAST_OUT_CUTS), ((src_r, src_l), (b1_r, b1_l), (b2_r, b2_l), (out_r, out_l)), (ssem, rsem, lsem), spot
+    )
+    swap.greet()
+    for copy in first_loads:
+        copy.wait()
     hidden = tok[...].astype(F32) + dot(mixed[...], out_w[...])
     hidden_one[...] = hidden
     router = router_w[...]
@@ -1152,270 +1183,247 @@
     rank = dot(before, member.astype(BF16))
     slot_t[...] = jnp.where(member, rank, -1.0).T
 
-
-def route(tokens, mixed, routes, w_r, w_q):
+    block = 16
+    g = grad[...]
+    for turn in TURNS:
+        v = lax.rem(y + turn, 4)
+        here = pl.ds(mul(v * block, block), block)
+        slots = slot_t[here, :]
+        places = even_places(slots)
+        last = slots == float(EVEN)
+        hot = places.astype(F32).reshape(block * EVEN, rows).astype(BF16)
+        last_hot = last.astype(BF16)
+        src_r[v, :, :, :, 0:width] = dot(hot, low).astype(BF16).reshape(4, 4, EVEN, width)
+        src_r[v, :, :, :, width:] = dot(hot, g).astype(BF16).reshape(4, 4, EVEN, width)
+        gt = gates_t[here, :]
+        at_slot = jnp.sum(
+            jnp.where(places, jnp.broadcast_to(gt[:, None, :], places.shape), 0.0).reshape(block * EVEN, rows),
+            axis=-1,
+            keepdims=True,
+        )
+        spread = jnp.broadcast_to(at_slot, (block * EVEN, 128)).reshape(block, EVEN, 128)
+        lane_of = iota((block, EVEN, 128), 1) == iota((block, EVEN, 128), 2)
+        even_gates = jnp.sum(jnp.where(lane_of, spread, 0.0), axis=1)
+        last_gates = jnp.sum(jnp.where(last, gt, 0.0), axis=-1, keepdims=True)
+        slot_gates = jnp.where(iota((block, 128), 1) == EVEN, last_gates, even_gates)
+        src_l[v] = jnp.concatenate([dot(last_hot, low), dot(last_hot, g), slot_gates], axis=1).reshape(
+            4, 4, 1, 2 * width + 128
+        )
+        swap.first(turn, v)
+
+    for copy in later_loads:
+        copy.wait()
+    gate = dot(low, sgu[:, :inner])
+    up_ = dot(low, sgu[:, inner:])
+    silu, slope = silu_parts(gate)
+    hidden_s[...] = (silu * up_).astype(BF16)
+    grad_hidden = dot_t(g, sdown[...])
+    grad_gu[:, :inner] = (grad_hidden * up_ * slope).astype(BF16)
+    grad_gu[:, inner:] = (grad_hidden * silu).astype(BF16)
+    swap.next(1)
+    out_s[...] = dot(hidden_s[...], sdown[...])
+    grad_in[...] = dot_t(grad_gu[...], sgu[...])
+    swap.next(2)
+
+    @pl.loop(0, inner // 256)
+    def _(i):
+        r = pl.ds(mul(i * 256, 256), 256)
+        grad_down[r, :] = t_dot(hidden_s[:, r], grad[...]).astype(BF16)
+
+    swap.finish()
+
+
+def route(tokens, mixed, routes, grad, w_q, w_r, w_d):
     rows, width = tokens.shape
-    whole = lambda a: pl.BlockSpec(a.shape, lambda i: (0, 0))
-    operands = (tokens, mixed, routes)
-    outs = (
-        shape(F32, rows, width),
-        shape(BF16, rows, width),
-        shape(F32, 128, rows),
-        shape(F32, 128, rows),
-    )
+    vmem, anywhere = pl.BlockSpec(memory_space=pltpu.VMEM), pl.BlockSpec(memory_space=pl.ANY)
+    r, last = (4, 4, 4, EVEN, 2 * width), (4, 4, 4, 1, 2 * width + 128)
     return pl.pallas_call(
         route_kernel,
-        grid=(1,),
-        out_shape=outs,
-        in_specs=[whole(a) for a in operands]
+        out_shape=(
+            shape(BF16, *r),
+            shape(F32, *last),
+            shape(F32, rows, width),
+            shape(BF16, rows, width),
+            shape(F32, 128, rows),
+            shape(F32, 128, rows),
+            shape(F32, rows, width),
+            shape(F32, rows, width),
+            shape(BF16, rows, 2048),
+            shape(BF16, 1024, width),
+        ),
+        in_specs=[vmem] * 4 + [anywhere] * 3,
+        out_specs=(anywhere,) * 2 + (vmem,) * 8,
+        scratch_shapes=[pltpu.VMEM(r, BF16), pltpu.VMEM(last, F32)] * 3
         + [
-            pl.BlockSpec((width, 1280), lambda i: (0, 0)),
-            pl.BlockSpec((width, 128), lambda i: (0, ROUTER)),
-            pl.BlockSpec((width, 128), lambda i: (0, GAINS)),
-        ],
-        out_specs=tuple(whole(a) for a in outs),
-        compiler_params=pltpu.CompilerParams(vmem_limit_bytes=56 << 20),
-        name="route",
-    )(*operands, w_r, w_r, w_q)
-
-
-EVEN = 16
-
-
-def even_places(slot_t):
-    experts, rows = slot_t.shape
-    wide = jnp.broadcast_to(slot_t[:, None, :], (experts, EVEN, rows))
-    place_of = iota((experts, EVEN, rows), 1).astype(F32)
-    return wide == place_of
-
-
-def dispatch_kernel(act, grad, gates, slot_t, out_r, out_l):
-    block, even, _lanes = out_r.shape
-    rows, width = act.shape
-    here = pl.ds(pl.multiple_of(pl.program_id(0) * block, block), block)
-    slots = slot_t[here, :]
-    places = even_places(slots)
-    last = slots == float(EVEN)
-    hot = places.astype(F32).reshape(block * even, rows).astype(BF16)
-    last_hot = last.astype(BF16)
-    x, g = act[...], grad[...]
-    out_r[:, :, :width] = dot(hot, x).astype(BF16).reshape(block, even, width)
-    out_r[:, :, width:] = dot(hot, g).astype(BF16).reshape(block, even, width)
-    gt = gates[here, :]
-    at_slot = jnp.sum(
-        jnp.where(places, jnp.broadcast_to(gt[:, None, :], places.shape), 0.0).reshape(block * even, rows),
-        axis=-1,
-        keepdims=True,
-    )
-    spread = jnp.broadcast_to(at_slot, (block * even, 128)).reshape(block, even, 128)
-    lane_of = iota((block, even, 128), 1) == iota((block, even, 128), 2)
-    even_gates = jnp.sum(jnp.where(lane_of, spread, 0.0), axis=1)
-    last_gates = jnp.sum(jnp.where(last, gt, 0.0), axis=-1, keepdims=True)
-    slot_gates = jnp.where(iota((block, 128), 1) == EVEN, last_gates, even_gates)
-    out_l[...] = jnp.concatenate([dot(last_hot, x), dot(last_hot, g), slot_gates], axis=1).reshape(
-        block, 1, 2 * width + 128
-    )
-
-
-def dispatch(act, grad, gates_t, slot_t, experts):
-    width = act.shape[1]
-    block = 8
-    whole = lambda a: pl.BlockSpec(a.shape, lambda i: (0, 0))
-    cut = lambda n, lanes: pl.BlockSpec((block, n, lanes), lambda i: (i, 0, 0))
-    return pl.pallas_call(
-        dispatch_kernel,
-        grid=(experts // block,),
-        out_shape=(
-            shape(BF16, experts, EVEN, 2 * width),
-            shape(F32, experts, 1, 2 * width + 128),
-        ),
-        in_specs=[whole(act), whole(grad), whole(gates_t), whole(slot_t)],
-        out_specs=(cut(EVEN, 2 * width), cut(1, 2 * width + 128)),
-        compiler_params=pltpu.CompilerParams(vmem_limit_bytes=32 << 20),
-        name="dispatch",
-    )(act, grad, gates_t, slot_t)
-
-
-def expert_kernel(rows_r, rows_l, o0, o1, o2, e0, e1, e2, out_r, out_l, all_x, all_g, hidden, d_gate, d_up, w_gate, w_up, w_down, sem):
-    hi, _y, _z, _lo, c = place()
-
-    def take(sources):
-        copies = loads(sources, (w_gate, w_up, w_down), sem)
-        for copy in copies:
-            copy.start()
-        for copy in copies:
-            copy.wait()
-
-    @pl.when((pl.program_id(0) == 0) & (c == hi))
-    def _():
-        take((e0, e1, e2))
-
-    @pl.when((pl.program_id(0) == 0) & (c != hi))
-    def _():
-        take((o0, o1, o2))
-
-    sources, _one, _lanes = rows_l.shape
-    width = rows_r.shape[-1] // 2
-    last = rows_l[...].reshape(sources, rows_l.shape[-1])
+            pltpu.VMEM((width, width), BF16),
+            pltpu.VMEM((width, 128), BF16),
+            pltpu.VMEM((width, 128), BF16),
+            pltpu.VMEM((width, 2048), BF16),
+            pltpu.VMEM((1024, width), BF16),
+            pltpu.VMEM((rows, 1024), BF16),
+        ]
+        + exchange_sems(2)
+        + [pltpu.SemaphoreType.DMA((5,))],
+        compiler_params=pltpu.CompilerParams(collective_id=3, has_side_effects=True, vmem_limit_bytes=56 << 20),
+        name="route_shared",
+    )(tokens, mixed, routes, grad, w_q, w_r, w_d)
+
+
+def expert_rows(rows_r, rows_l, width):
+    sources = 16
+    last = rows_l.reshape(sources, rows_l.shape[-1])
     even = sources * EVEN
-    x = jnp.concatenate([rows_r[:, :, :width].reshape(even, width), last[:, :width].astype(BF16)], axis=0)
-    g = jnp.concatenate(
-        [rows_r[:, :, width:].reshape(even, width).astype(F32), last[:, width : 2 * width]], axis=0
-    )
+    both = rows_r.reshape(even, 2 * width)
+    x = jnp.concatenate([both[:, :width], last[:, :width].astype(BF16)], axis=0)
+    g = jnp.concatenate([both[:, width:].astype(F32), last[:, width : 2 * width]], axis=0)
     sent = last[:, 2 * width :]
     spread = jnp.broadcast_to(sent[:, None, :], (sources, EVEN, 128))
     own = iota((sources, EVEN, 128), 1) == iota((sources, EVEN, 128), 2)
     even_gates = jnp.sum(jnp.where(own, spread, 0.0).reshape(even, 128), axis=-1, keepdims=True)
     last_gates = jnp.sum(jnp.where(iota((sources, 128), 1) == EVEN, sent, 0.0), axis=-1, keepdims=True)
-    grad_result = (jnp.concatenate([even_gates, last_gates], axis=0) * g).astype(BF16)
-    all_x[...] = x
-    all_g[...] = grad_result
-    gate = dot(x, w_gate[...])
-    up_ = dot(x, w_up[...])
-    silu, slope = silu_parts(gate)
-    low = (silu * up_).astype(BF16)
-    hidden[...] = low
-    grad_hidden = dot_t(grad_result, w_down[...])
-    grad_gate = (grad_hidden * up_ * slope).astype(BF16)
-    grad_up = (grad_hidden * silu).astype(BF16)
-    d_gate[...] = grad_gate
-    d_up[...] = grad_up
-    result = dot(low, w_down[...]).astype(BF16)
-    grad_in = (dot_t(grad_gate, w_gate[...]) + dot_t(grad_up, w_up[...])).astype(BF16)
-    out_r[:, :, :width] = result[:even].reshape(sources, EVEN, width)
-    out_r[:, :, width:] = grad_in[:even].reshape(sources, EVEN, width)
-    out_l[...] = jnp.concatenate([result[even:], grad_in[even:]], axis=1).astype(F32).reshape(sources, 1, 2 * width)
-
-
-def expert(rows_r, rows_l, passed, own):
-    devices, _even, width = rows_r.shape
-    width = width // 2
-    inner = own[0].shape[1]
-    steps = 4
-    src = devices // steps
-    rows = src * (EVEN + 1)
-    total = rows * steps
-    cut = lambda n, lanes: pl.BlockSpec((src, n, lanes), lambda i: (i, 0, 0))
-    flat = lambda lanes: pl.BlockSpec((rows, lanes), lambda i: (i, 0))
-    return pl.pallas_call(
-        expert_kernel,
-        grid=(steps,),
-        out_shape=(
-            shape(BF16, devices, EVEN, 2 * width),
-            shape(F32, devices, 1, 2 * width),
-            shape(BF16, total, width),
-            shape(BF16, total, width),
-            shape(BF16, total, inner),
-            shape(BF16, total, inner),
-            shape(BF16, total, inner),
-        ),
-        in_specs=[cut(EVEN, 2 * width), cut(1, rows_l.shape[-1])] + [pl.BlockSpec(memory_space=pl.ANY)] * 6,
-        scratch_shapes=[pltpu.VMEM(w.shape, BF16) for w in own] + [pltpu.SemaphoreType.DMA((3,))],
-        out_specs=(
-            cut(EVEN, 2 * width),
-            cut(1, 2 * width),
-            flat(width),
-            flat(width),
-            flat(inner),
-            flat(inner),
-            flat(inner),
-        ),
-        compiler_params=pltpu.CompilerParams(vmem_limit_bytes=60 << 20),
-        name="expert",
-    )(rows_r, rows_l, *passed, *own)
-
-
-def loads(ins, bufs, sem):
-    return [pltpu.make_async_copy(src, dst, sem.at[k]) for k, (src, dst) in enumerate(zip(ins, bufs))]
-
-
-def shared_work(phase, ins, outs, scratch):
-    w_r, *others = ins
-    out_s, grad_in, grad_gu, grad_down = outs
-    sgu, sdown, act, grad, hidden, sem = scratch
-    inner = sdown.shape[0]
-    copies = loads([w_r.at[:, pl.ds(1280, 2 * inner)]] + others, (sgu, sdown, act, grad), sem) if phase < 1 else []
-    if phase == -1:
-        for copy in copies:
+    return x, (jnp.concatenate([even_gates, last_gates], axis=0) * g).astype(BF16)
+
+
+def expert_kernel(
+    rows_r, rows_l, o0, o1, o2, e0, e1, e2,
+    back_r, back_l, p0, p1, p2,
+    src_r, src_l, b1_r, b1_l, b2_r, b2_l, in_r, in_l, w_gate, w_up, w_down, all_x, all_g, hidden, d_gate, d_up,
+    g_gate, g_up, g_down, s_gate, s_up, s_down, ssem, rsem, lsem, wsem, isem, osem, xsem,
+):
+    spot = place()
+    hi, y, z, lo, c = spot
+    width = all_x.shape[1]
+    outs, products, from_sib = (p0, p1, p2), (g_gate, g_up, g_down), (s_gate, s_up, s_down)
+    weights = (w_gate, w_up, w_down)
+    owner = c == hi
+    swap = Exchange(
+        False, (ROW_CUTS, LAST_BACK_CUTS), ((src_r, src_l), (b1_r, b1_l), (b2_r, b2_l), (back_r, back_l)), (ssem, rsem, lsem), spot
+    )
+
+    @pl.when(owner)
+    def _():
+        for copy in loads((e0, e1, e2), weights, wsem):
             copy.start()
-    elif phase == 0:
-        for copy in copies:
+
+    @pl.when(jnp.logical_not(owner))
+    def _():
+        for copy in loads((o0, o1, o2), weights, wsem):
+            copy.start()
+
+    def block(n):
+        v = lax.rem(y + TURNS[n], 4)
+        return v, loads((rows_r.at[v], rows_l.at[v]), (in_r.at[n % 2], in_l.at[n % 2]), isem.at[n % 2])
+
+    coming = {0: block(0)[1]}
+    for copy in coming[0]:
+        copy.start()
+    swap.greet()
+    for copy in loads((e0, e1, e2), weights, wsem):
+        copy.wait()
+    step = all_x.shape[0] // 4
+    even = 16 * EVEN
+    for n, turn in enumerate(TURNS):
+        v = lax.rem(y + turn, 4)
+        if n + 1 < 4:
+            coming[n + 1] = block(n + 1)[1]
+            for copy in coming[n + 1]:
+                copy.start()
+        for copy in coming[n]:
             copy.wait()
-        gate = dot(act[...], sgu[:, :inner])
-        up_ = dot(act[...], sgu[:, inner:])
+        here = slice(n * step, (n + 1) * step)
+        x, grad_result = expert_rows(in_r[n % 2], in_l[n % 2], width)
+        all_x[here, :] = x
+        all_g[here, :] = grad_result
+        gate = dot(x, w_gate[...])
+        up_ = dot(x, w_up[...])
         silu, slope = silu_parts(gate)
-        hidden[...] = (silu * up_).astype(BF16)
-        grad_hidden = dot_t(grad[...], sdown[...])
-        grad_gu[:, :inner] = (grad_hidden * up_ * slope).astype(BF16)
-        grad_gu[:, inner:] = (grad_hidden * silu).astype(BF16)
-    elif phase == 1:
-        out_s[...] = dot(hidden[...], sdown[...])
-        grad_in[...] = dot_t(grad_gu[...], sgu[...])
-    elif phase == 2:
-
-        @pl.loop(0, inner // 256)
-        def _(i):
-            r = pl.ds(mul(i * 256, 256), 256)
-            grad_down[r, :] = t_dot(hidden[:, r], grad[...]).astype(BF16)
-
-
-def expert_work(phase, ins, outs, scratch):
-    bufs, products, from_sib = scratch[0:5], scratch[5:8], scratch[8:11]
-    load_sem, send_sem, recv_sem = scratch[11:]
-    all_x, all_g, hidden, d_gate, d_up = bufs
-    hi, y, z, lo, c = place()
-    copies = loads(ins, bufs, load_sem) if phase < 1 else []
-
-    def swap(k):
+        low = (silu * up_).astype(BF16)
+        hidden[here, :] = low
+        grad_hidden = dot_t(grad_result, w_down[...])
+        grad_gate = (grad_hidden * up_ * slope).astype(BF16)
+        grad_up = (grad_hidden * silu).astype(BF16)
+        d_gate[here, :] = grad_gate
+        d_up[here, :] = grad_up
+        result = dot(low, w_down[...]).astype(BF16)
+        grad_in = (dot_t(grad_gate, w_gate[...]) + dot_t(grad_up, w_up[...])).astype(BF16)
+        src_r[v, :, :, :, 0:width] = result[:even].reshape(4, 4, EVEN, width)
+        src_r[v, :, :, :, width:] = grad_in[:even].reshape(4, 4, EVEN, width)
+        src_l[v] = jnp.concatenate([result[even:], grad_in[even:]], axis=1).astype(F32).reshape(4, 4, 1, 2 * width)
+        swap.first(turn, v)
+
+    def half(k, core):
         n = products[k].shape[0] // 2
+        return products[k].at[pl.ds(mul(core * n, 16), n)]
+
+    def trade(k):
         return pltpu.make_async_remote_copy(
-            src_ref=products[k].at[pl.ds(mul((1 - c) * n, 16), n)],
+            src_ref=half(k, 1 - c),
             dst_ref=from_sib[k],
-            send_sem=send_sem.at[k],
-            recv_sem=recv_sem.at[k],
+            send_sem=xsem.at[0, k],
+            recv_sem=xsem.at[1, k],
             device_id=device(hi, y, z, lo, 1 - c),
             device_id_type=MESH,
         )
 
+    def product(k, left, right, wide):
+        out = products[k]
+
+        @pl.loop(0, out.shape[0] // wide)
+        def _(i):
+            r = pl.ds(mul(i * wide, wide), wide)
+            out[r, :] = t_dot(left[:, r], right[...]).astype(BF16)
+
+        trade(k).start()
+
     def add(k):
-        swap(k).wait_recv()
+        trade(k).wait_recv()
         n = products[k].shape[0] // 2
 
         @pl.loop(0, n // 64)
         def _(i):
-            r = pl.ds(mul(i * 64, 64), 64)
-            own = products[k][pl.ds(mul(c * n + i * 64, 64), 64), :]
-            outs[k][r, :] = (own.astype(F32) + from_sib[k][r, :].astype(F32)).astype(BF16)
-
-    if phase == -1:
-        for copy in copies:
-            copy.start()
-    elif phase < 2:
-        if phase == 0:
-            for copy in copies:
-                copy.wait()
-        grad, out = (d_gate, products[0]) if phase == 0 else (d_up, products[1])
-
-        @pl.loop(0, out.shape[0] // 256)
-        def _(i):
-            r = pl.ds(mul(i * 256, 256), 256)
-            out[r, :] = t_dot(all_x[:, r], grad[...]).astype(BF16)
-
-        swap(phase).start()
-    elif phase == 2:
-
-        @pl.loop(0, products[2].shape[0] // 128)
-        def _(i):
-            r = pl.ds(mul(i * 128, 128), 128)
-            products[2][r, :] = t_dot(hidden[:, r], all_g[...]).astype(BF16)
-
-        swap(2).start()
-        add(0)
-        add(1)
-    else:
-        add(2)
-        for k in range(3):
-            swap(k).wait_send()
+            own = pl.ds(mul(c * n + i * 64, 64), 64)
+            more = from_sib[k][pl.ds(mul(i * 64, 64), 64), :].astype(F32)
+            products[k][own, :] = (products[k][own, :].astype(F32) + more).astype(BF16)
+
+        copy = pltpu.make_async_copy(half(k, c), outs[k], osem.at[k])
+        copy.start()
+        return copy
+
+    product(0, all_x, d_gate, 256)
+    swap.next(1)
+    product(1, all_x, d_up, 256)
+    product(2, hidden, all_g, 128)
+    kept = [add(0)]
+    swap.next(2)
+    kept += [add(1), add(2)]
+    swap.finish()
+    for k in range(3):
+        trade(k).wait_send()
+        kept[k].wait()
+
+
+def expert(rows_r, rows_l, passed, own):
+    width = rows_r.shape[-1] // 2
+    inner = own[0].shape[1]
+    total = 64 * (EVEN + 1)
+    anywhere = pl.BlockSpec(memory_space=pl.ANY)
+    r, last = (4, 4, 4, EVEN, 2 * width), (4, 4, 4, 1, 2 * width)
+    return pl.pallas_call(
+        expert_kernel,
+        out_shape=(shape(BF16, *r), shape(F32, *last)) + tuple(shape(BF16, w.shape[0] // 2, w.shape[1]) for w in own),
+        in_specs=[anywhere] * 8,
+        out_specs=(anywhere,) * 5,
+        scratch_shapes=[pltpu.VMEM(r, BF16), pltpu.VMEM(last, F32)] * 3
+        + [pltpu.VMEM((2,) + rows_r.shape[1:], BF16), pltpu.VMEM((2,) + rows_l.shape[1:], F32)]
+        + [pltpu.VMEM(w.shape, BF16) for w in own]
+        + [pltpu.VMEM((total, n), BF16) for n in (width, width, inner, inner, inner)]
+        + [pltpu.VMEM(w.shape, BF16) for w in own]
+        + [pltpu.VMEM((w.shape[0] // 2, w.shape[1]), BF16) for w in own]
+        + exchange_sems(2)
+        + [pltpu.SemaphoreType.DMA(n) for n in ((3,), (2, 2), (3,), (2, 3))],
+        compiler_params=pltpu.CompilerParams(collective_id=4, has_side_effects=True, vmem_limit_bytes=62 << 20),
+        name="expert_back",
+    )(rows_r, rows_l, *passed, *own)
 
 
 def split_terms(w):
@@ -1540,39 +1548,11 @@
     w_q, w_r, w_d, expert_w, act_attn, q, kv, prior, mixed = forward(
         shard_q, shard_r, shared_down, own_experts, tokens, cos, sin, seg_row, seg_col
     )
-    hidden_one, act_ffn, gates_t, slot_t = route(tokens, mixed, routes, w_r, w_q)
-    rows_r, rows_l = dispatch(act_ffn, grad, gates_t, slot_t, experts)
-    rows_r, rows_l, out_s, grad_in_s, grad_gu, grad_sdown = exchange(
-        3,
-        True,
-        (rows_r, rows_l),
-        (ROW_CUTS, LAST_OUT_CUTS),
-        shared_work,
-        (w_r, w_d, act_ffn, grad),
-        (shape(F32, rows, width), shape(F32, rows, width), shape(BF16, rows, 2048), shape(BF16, 1024, width)),
-        (
-            pltpu.VMEM((width, 2048), BF16),
-            pltpu.VMEM((1024, width), BF16),
-            pltpu.VMEM((rows, width), BF16),
-            pltpu.VMEM((rows, width), BF16),
-            pltpu.VMEM((rows, 1024), BF16),
-            pltpu.SemaphoreType.DMA((4,)),
-        ),
+    rows_r, rows_l, hidden_one, act_ffn, gates_t, slot_t, out_s, grad_in_s, grad_gu, grad_sdown = route(
+        tokens, mixed, routes, grad, w_q, w_r, w_d
     )
-    out_r, out_l, *kept = expert(rows_r, rows_l, expert_w, own_experts)
-    back_r, back_l, *parts = exchange(
-        4,
-        False,
-        (out_r, out_l),
-        (ROW_CUTS, LAST_BACK_CUTS),
-        expert_work,
-        tuple(kept),
-        tuple(shape(BF16, w.shape[0] // 2, w.shape[1]) for w in own_experts),
-        [pltpu.VMEM(a.shape, BF16) for a in kept]
-        + [pltpu.VMEM(w.shape, BF16) for w in own_experts]
-        + [pltpu.VMEM((w.shape[0] // 2, w.shape[1]), BF16) for w in own_experts]
-        + [pltpu.SemaphoreType.DMA((n,)) for n in (5, 3, 3)],
-    )
+    back_r, back_l, *parts = expert(rows_r, rows_l, expert_w, own_experts)
+    back_r, back_l = (a.reshape((experts,) + a.shape[3:]) for a in (back_r, back_l))
     layer_out, grad_hidden, grad_mixed, left_r, right_r, gain_ffn = combine(
         (back_r, back_l, slot_t, gates_t, grad, hidden_one, out_s, grad_in_s, mixed, act_ffn, grad_gu), w_r, w_q
     )

time: 460 us -> 446 us (0.970)
  Pallas kernels: 419 us -> 407 us
  local copies, waits for them, and re-layouts: 25 us -> 19.1 us
    pallas_call x5 -> x2, Pallas kernels: 186 us -> 175 us  [the longest x1 90.2 us: route(): pl.pallas_call(route_kernel, out_shape=(shape(BF16, *r), shape(F32, *last...]
    unnamed x51 -> x39, local copies, waits for them, and re-layouts: 8.21 us -> 2.29 us
where the time goes in v5:
time: 446 us; the launch traced here: 438 us
  Pallas kernels  407 us (91%)
  local copies, waits for them, and re-layouts  19.1 us (4%)
  other arithmetic  11.2 us (3%)
    pallas_call x1, Pallas kernels, backward(): pl.pallas_call(backward_kernel, out_shape=tuple((shape(F32, *fin[name]) f...  136 us
    pallas_call x1, Pallas kernels, route(): pl.pallas_call(route_kernel, out_shape=(shape(BF16, *r), shape(F32, *last...  90.2 us
    pallas_call x1, Pallas kernels, forward(): pl.pallas_call(forward_kernel, out_shape=(shape(BF16, 4, 4, 80, Q_WIDE),...  84.9 us
    pallas_call x1, Pallas kernels, expert(): pl.pallas_call(expert_kernel, out_shape=(shape(BF16, *r), shape(F32, *las...  84.4 us
    pallas_call x1, Pallas kernels, combine(): pl.pallas_call(combine_kernel, grid=(1,), out_shape=outs, in_specs=[whole...  11.2 us
    convert_element_type x2, other arithmetic, per_device(): jnp.where(kept_here[:, None, None], own[None], total.reshape((2,) + own.s...  11.2 us

profile of v5, /device:TPU:1, one launch (start us, length us, event | category | flops | bytes accessed | tf_op | source)
XLA Modules:
  0.0 438.0 jit_solution(14911591112693855135)
XLA Ops:
  0.6 0.0 copy-start.11
  0.7 0.0 copy-start.14
  0.7 0.0 copy-start.16
  0.7 0.0 copy-start.17
  0.7 0.0 copy-start.8
  0.7 0.0 copy-start.9
  0.7 1.5 reshape.116
  2.3 0.0 copy-start.13
  2.3 0.0 copy-start.12
  2.3 0.1 pad.11
  2.4 0.4 reshape.117
  2.8 1.4 reshape.118
  4.2 0.1 pad.12
  4.3 0.4 reshape.119
  4.8 0.1 concatenate.7
  4.9 1.2 dynamic_update_slice.7.win_r
  6.1 0.0 copy-start.4
  6.2 0.1 copy.37
  6.3 0.1 copy.38
  6.4 0.1 concatenate.6
  6.5 1.2 dynamic_update_slice.6.win_q
  7.7 0.0 copy-start.3
  7.7 0.8 copy.39.seg_col
  8.5 0.0 copy-done.12
  8.5 0.6 pad.13.win_d
  9.2 0.0 copy-done.4
  9.2 84.9 %gather_attend.1 = (bf16[4,4,80,4096]{3,2,1,0:T(8,128)(2,1)}, bf16[4,4,80,3584]{3,2,1,0:T(8,128)(2,1)}, bf16[4,4,64,1280]{3,2,1,0:T(8,128)(2,1)}, bf16[1280,896]...) custom-call(bf16[32,4096]{1,0:T(8,128)(2,1)} %copy-done.3, ...), custom_call_target="tpu_custom_call" | custom-call | tf_op jit(solution)/shard_map/gather_attend/pallas_call | solution.py:482
  94.1 0.7 copy.40
  94.8 90.2 %route_shared.1 = (bf16[4,4,4,16,2560]{4,3,2,1,0:T(8,128)(2,1)}, f32[4,4,4,1,2688]{4,3,2,1,0:T(1,128)}, f32[128,1280]{1,0:T(8,128)}, bf16[128,1280]{1,0:T(8,128)...) custom-call(bf16[128,1280]{1,0:T(8,128)(2,1)} %bitcast.55, ...), custom_call_target="tpu_custom_call" | custom-call | tf_op jit(solution)/shard_map/route_shared/pallas_call | solution.py:1240
  185.0 84.4 %expert_back.1 = (bf16[4,4,4,16,2560]{4,3,2,1,0:T(8,128)(2,1)}, f32[4,4,4,1,2560]{4,3,2,1,0:T(1,128)}, bf16[640,896]{1,0:T(8,128)(2,1)}, bf16[640,896]{1,0:T(8,128)(2,1)}, bf16[448,1280]{1,0:T(8,128)(2,1)}) custom-call(bf16[4,4,4,16,2560]{4,3,2,1,0:T(8,128)(2,1)} %get-tuple-element.58.rows_r, f32[4,4,4,1,2688]{4,3,2,1,0:T(1,128)} %get-tuple-element.59.rows_l, ...), custom_call_target="tpu_custom_call" | custom-call | tf_op jit(solution)/shard_map/expert_back/pallas_call | solution.py:1411
  269.4 11.2 %combine.1 = (bf16[128,1280]{1,0:T(8,128)(2,1)}, f32[128,1280]{1,0:T(8,128)}, bf16[128,1280]{1,0:T(8,128)(2,1)}, bf16[256,1280]{1,0:T(8,128)(2,1)}, bf16[256,3584]{1,0:T(8,128)(2,1)}, /*index=5*/f32[1,1280]{1,0:T(1,128)}) custom-call(bf16[64,16,2560]{2,1,0:T(8,128)(2,1)} %bitcast.53, f32[64,1,2560]{2,1,0:T(1,128)} %bitcast.64, ...), custom_call_target="tpu_custom_call" | custom-call | tf_op jit(solution)/shard_map/combine/pallas_call | solution.py:1494
  280.6 136.0 %attend_back_sums.1 = (f32[32,4096]{1,0:T(8,128)}, f32[32,3584]{1,0:T(8,128)}, f32[16,1280]{1,0:T(8,128)}, bf16[1280,896]{1,0:T(8,128)(2,1)}, bf16[1280,896]{1,0...) custom-call(bf16[256,1280]{1,0:T(8,128)(2,1)} %get-tuple-element.73.left_r, ...), custom_call_target="tpu_custom_call" | custom-call | tf_op jit(solution)/shard_map/attend_back_sums/pallas_call | solution.py:938
  416.6 0.1 broadcast_in_dim.99
  416.6 0.1 broadcast_in_dim.100
  416.7 4.3 bitcast_convert_fusion
  421.0 0.1 broadcast_in_dim.92
  421.1 0.0 copy-done.1
  421.2 6.9 %bitcast_convert_fusion.1 = (f32[1,1280,896]{2,1,0:T(8,128)}, f32[1,1280,896]{2,1,0:T(8,128)}) fusion(bf16[1280,896]{1,0:T(8,128)(2,1)} %get-tuple-element.91, pred[1280]{0:T(1024)(128)(4,1)S(1)} %broadcast_in_dim.93, bf16[640,896]{1,0:T(8,128)(2,1)S(1)} %copy-done.1, bf16[1280,896]{1,0:T(8,128)(2,1)} %get-tuple-element.90, bf16[640,896]{1,0:T(8,128)(2,1)S(1)} %copy-done), kind=kLoop, calls=%fused_computation.1 | loop fusion | flops 4587520 | bytes 16057600 | tf_op jit(solution)/shard_map/convert_element_type | solution.py:1574
  428.0 1.8 fusion
  429.9 1.1 fusion.1
  431.0 0.2 reshape.127
  431.2 1.0 reshape.128
  432.2 0.2 reshape.129
  432.4 1.0 reshape.130
  433.4 1.4 dynamic-slice.6
  434.8 1.5 dynamic-slice_reduce_fusion
  436.3 0.8 copy.46
  437.2 0.6 copy.47
  (29 shorter events, 0.1 us)
Async XLA Ops:
  0.6 4.1 copy-start.11
  0.7 4.1 copy-start.14
  0.7 5.5 %copy-start.16 = (bf16[20]{0:T(256)(128)(2,1)S(1)}, bf16[20]{0:T(256)(128)(2,1)}, u32[]{:S(2)}) copy-start(bf16[20]{0:T(256)(128)(2,1)} %param.23) | copy-start | bytes 124
  0.7 5.6 %copy-start.17 = (bf16[20]{0:T(256)(128)(2,1)S(1)}, bf16[20]{0:T(256)(128)(2,1)}, u32[]{:S(2)}) copy-start(bf16[20]{0:T(256)(128)(2,1)} %param.28) | copy-start | bytes 124
  0.7 5.7 %copy-start.8 = (bf16[20,1280]{1,0:T(8,128)(2,1)S(1)}, bf16[20,1280]{1,0:T(8,128)(2,1)}, u32[]{:S(2)}) copy-start(bf16[20,1280]{1,0:T(8,128)(2,1)} %param.24) | copy-start | bytes 153604
  0.7 5.7 %copy-start.9 = (bf16[20,1280]{1,0:T(8,128)(2,1)S(1)}, bf16[20,1280]{1,0:T(8,128)(2,1)}, u32[]{:S(2)}) copy-start(bf16[20,1280]{1,0:T(8,128)(2,1)} %param.25) | copy-start | bytes 153604
  0.7 5.7 %copy-start.10 = (bf16[20,1280]{1,0:T(8,128)(2,1)S(1)}, bf16[20,1280]{1,0:T(8,128)(2,1)}, u32[]{:S(2)}) copy-start(bf16[20,1280]{1,0:T(8,128)(2,1)} %param.26) | copy-start | bytes 153604
  2.3 5.5 %copy-start.13 = (s32[1,256]{1,0:T(1,128)S(1)}, s32[1,256]{1,0:T(1,128)}, u32[]{:S(2)}) copy-start(s32[1,256]{1,0:T(1,128)} %seg_row.3) | copy-start | bytes 3076
  2.3 6.3 %copy-start.12 = (bf16[14,1280]{1,0:T(8,128)(2,1)S(1)}, bf16[14,1280]{1,0:T(8,128)(2,1)}, u32[]{:S(2)}) copy-start(bf16[14,1280]{1,0:T(8,128)(2,1)} %param.32) | copy-start | bytes 107524
  6.1 3.0 copy-start.4
  7.7 1.5 copy-start.3
  9.2 84.9 %copy-start.15 = (s32[1,128,7]{1,0,2:T(1,128)S(1)}, s32[1,128,7]{1,0,2:T(1,128)}, u32[]{:S(2)}) copy-start(s32[1,128,7]{1,0,2:T(1,128)} %param.22) | copy-start | bytes 10756
  280.6 136.2 %copy-start.2 = (bf16[448,1280]{1,0:T(8,128)(2,1)S(1)}, bf16[448,1280]{1,0:T(8,128)(2,1)}, u32[]{:S(2)}) copy-start(bf16[448,1280]{1,0:T(8,128)(2,1)} %get-tuple-element.85.p2) | copy-start | bytes 3440644
  416.7 4.4 %copy-start = (bf16[640,896]{1,0:T(8,128)(2,1)S(1)}, bf16[640,896]{1,0:T(8,128)(2,1)}, u32[]{:S(2)}) copy-start(bf16[640,896]{1,0:T(8,128)(2,1)} %get-tuple-element.83.p0) | copy-start | bytes 3440644
  416.7 4.4 %copy-start.1 = (bf16[640,896]{1,0:T(8,128)(2,1)S(1)}, bf16[640,896]{1,0:T(8,128)(2,1)}, u32[]{:S(2)}) copy-start(bf16[640,896]{1,0:T(8,128)(2,1)} %get-tuple-element.84.p1) | copy-start | bytes 3440644
  421.1 6.9 %copy-start.6 = (f32[32,4096]{1,0:T(8,128)S(1)}, f32[32,4096]{1,0:T(8,128)}, u32[]{:S(2)}) copy-start(f32[32,4096]{1,0:T(8,128)} %get-tuple-element.87) | copy-start | bytes 1572868
  428.0 8.3 %copy-start.5 = (f32[128,1280]{1,0:T(8,128)S(1)}, f32[128,1280]{1,0:T(8,128)}, u32[]{:S(2)}) copy-start(f32[128,1280]{1,0:T(8,128)} %get-tuple-element.86) | copy-start | bytes 1966084
  430.9 6.2 %copy-start.7 = (f32[16,1280]{1,0:T(8,128)S(1)}, f32[16,1280]{1,0:T(8,128)}, u32[]{:S(2)}) copy-start(f32[16,1280]{1,0:T(8,128)} %get-tuple-element.89) | copy-start | bytes 245764

commit v6 on v5

--- a/solution.py
+++ b/solution.py
@@ -194,13 +194,14 @@
     return pl.ds(mul(lax.axis_index("seq") * 128), 128)
 
 
-def allowed_keys(seg_row, seg_col):
+def allowed_keys(seg_row):
     hi = lax.axis_index("seq")
-    here = seq_rows()
-    mine = seg_col[here, :]
-    rows = mine.shape[0]
-    own = (seg_row[:, here] == mine) & (iota((rows, rows), 1) <= iota((rows, rows), 0))
-    prior = (seg_row[:, 0:rows] == mine) & (hi == 1)
+    rows = seg_row.shape[1] // 2
+    across = lambda at: jnp.broadcast_to(seg_row[:, at].astype(F32), (rows, rows))
+    here = across(seq_rows())
+    mine = here.T
+    own = (here == mine) & (iota((rows, rows), 1) <= iota((rows, rows), 0))
+    prior = (across(slice(0, rows)) == mine) & (hi == 1)
     return own, prior
 
 
@@ -319,19 +320,47 @@
     return first[0:shift], first[shift:n] + second[0 : n - shift], second[n - shift : n]
 
 
+def make_windows(j, shards, win_q, win_r, win_d):
+    query_w, key_w, value_w, out_w, gate_w, up_w, router_w, gain_a, gain_f, down_w = shards
+    own_rows, width = query_w.shape
+    place_rows = (iota((32, own_rows), 0) == iota((32, own_rows), 1) + 4 * j).astype(BF16)
+    put = lambda w: dot(place_rows, w).astype(BF16)
+    for k, w in enumerate((query_w, key_w, value_w)):
+        win_q[:, k * width : (k + 1) * width] = put(w[...])
+    row = iota((8, own_rows), 0)
+    gains = jnp.where(row == 0, gain_a[...].astype(F32), jnp.where(row == 1, gain_f[...].astype(F32), 0.0)).astype(BF16)
+    column = (iota((8, 128), 1) == iota((8, 128), 0)).astype(BF16)
+    win_q[:, GAINS * 128 : (GAINS + 1) * 128] = put(t_dot(gains, column).astype(BF16))
+    win_q[:, (GAINS + 1) * 128 :] = jnp.zeros((32, 128), BF16)
+    win_r[:, 0:width] = put(out_w[...])
+    narrow, wide = gate_w.shape[1], 1024
+    row, col = iota((narrow, wide), 0), iota((narrow, wide), 1)
+    spread = ((row == col - 2 * (col // 16)) & (lax.rem(col, 16) < 14)).astype(BF16)
+    for k, w in enumerate((gate_w, up_w)):
+        win_r[:, width + k * wide : width + (k + 1) * wide] = dot(put(w[...]), spread).astype(BF16)
+    start, n = ROUTER * 128, router_w.shape[1]
+    win_r[:, start:] = jnp.concatenate([put(router_w[...]), jnp.zeros((32, 256 - n), BF16)], axis=1)
+    n = down_w.shape[0]
+    place_rows = (iota((16, n), 0) == iota((16, n), 1)).astype(BF16)
+    win_d[...] = dot(place_rows, down_w[...]).astype(BF16)
+
+
 def forward_kernel(
-    win_q, win_r, win_d, e0, e1, e2, tok, cos, sin, seg_row, seg_col,
+    query_w, key_w, value_w, out_w, gate_w, up_w, router_w, gain_a, gain_f, down_w, e0, e1, e2, tok, cos, sin, seg_row,
     out_q, out_r, out_d, o0, o1, o2, act, q, kv, prior, mixed,
-    sib_q, sib_r, pair_q, pair_r, side_q, side_r, blk_q, blk_r, blk_d, w_buf, ssem, rsem, lsem, esem, wsem,
+    win_q, win_r, win_d, sib_q, sib_r, pair_q, pair_r, side_q, side_r, blk_q, blk_r, blk_d, w_buf, ssem, rsem, lsem, esem, wsem,
 ):
     spot = place()
     hi, y, z, lo, c = spot
     sib = device(hi, y, z, lo, 1 - c)
     xn = device(hi, y, z, 1 - lo, c)
     hn = device(1 - hi, y, z, lo, c)
+    width = tok.shape[1]
+    make_windows(
+        lo * 2 + c, (query_w, key_w, value_w, out_w, gate_w, up_w, router_w, gain_a, gain_f, down_w), win_q, win_r, win_d
+    )
     greet([sib, xn, hn] + list(ring_neighbours(*spot).values()))
     wires = Sender(ssem, rsem, lsem)
-    width = tok.shape[1]
     owner = c == hi
 
     @pl.when(hi == 0)
@@ -446,7 +475,7 @@
         def _():
             later.wait_recv()
 
-        own_ok, prior_ok = allowed_keys(seg_row, seg_col)
+        own_ok, prior_ok = allowed_keys(seg_row)
         for h in range(HEADS):
             _query, _keys, values, probs = head_probs(h, q, kv, prior, own_ok, prior_ok, width)
             mixed[:, h * 128 : (h + 1) * 128] = dot(probs.astype(BF16), values).astype(BF16)
@@ -471,11 +500,8 @@
     wires.finish()
 
 
-def forward(shard_q, shard_r, down, experts, tokens, cos, sin, seg_row, seg_col):
+def forward(shards, experts, tokens, cos, sin, seg_row):
     rows, width = tokens.shape
-    offset = 4 * lax.rem(lax.axis_index("exp"), 4)
-    window = lambda s: lax.dynamic_update_slice(jnp.zeros((32, s.shape[1]), BF16), s, (offset, 0))
-    down = jnp.pad(down, ((0, 2), (0, 0)))
     sems = 2 + 1 + 3 + 36 * 2 * 3 + 8
     vmem, anywhere = pl.BlockSpec(memory_space=pltpu.VMEM), pl.BlockSpec(memory_space=pl.ANY)
     half = {name: PIECES[name][1] * 128 for name in PIECES}
@@ -492,9 +518,10 @@
             shape(BF16, rows, 2 * width),
             shape(BF16, rows, width),
         ),
-        in_specs=[vmem] * 3 + [anywhere] * 3 + [vmem] * 5,
+        in_specs=[vmem] * len(shards) + [anywhere] * 3 + [vmem] * 4,
         out_specs=(anywhere,) * 6 + (vmem,) * 5,
-        scratch_shapes=[pltpu.VMEM((n, half[name]), BF16) for n in (32, 48, 48, 80) for name in "qr"]
+        scratch_shapes=[pltpu.VMEM(dims, BF16) for dims in ((32, Q_WIDE), (32, R_WIDE), (16, D_WIDE))]
+        + [pltpu.VMEM((n, half[name]), BF16) for n in (32, 48, 48, 80) for name in "qr"]
         + [
             pltpu.VMEM((64, half["d"]), BF16),
             pltpu.VMEM((2, 4, 4, 80, 512), BF16),
@@ -506,9 +533,15 @@
         ],
         compiler_params=pltpu.CompilerParams(collective_id=1, has_side_effects=True, vmem_limit_bytes=56 << 20),
         name="gather_attend",
-    )(window(shard_q), window(shard_r), down, *experts, tokens, cos, sin, seg_row, seg_col)
+    )(*shards, *experts, tokens, cos, sin, seg_row)
     w_q, w_r, w_d = (out[k].reshape(16 * out[k].shape[2], out[k].shape[3]) for k in range(3))
     return (w_q, w_r, w_d, out[3:6]) + tuple(out[6:])
+
+
+START = (3, 1, 1)
+R_PIECES = range(11, 24)
+Q_PIECES = range(0, 18, 2)
+KV_GAP = 4
 
 
 class RingSum:
@@ -637,7 +670,7 @@
 
 
 def backward_kernel(
-    left_r, right_r, sdown, act, q, kv, prior, seg_row, seg_col, grad_mixed, cos, sin, tok, grad_hidden, gain_f, w_q,
+    left_r, right_r, sdown, act, q, kv, prior, seg_row, grad_mixed, cos, sin, tok, grad_hidden, gain_f, w_q,
     p0, p1, p2,
     fin_q, fin_r, fin_d, t0, t1, t2, grad_tokens,
     *scratch,
@@ -721,6 +754,10 @@
 
             yield
 
+    experts = expert_steps()
+    for _ in range(START[0]):
+        next(experts, None)
+
     own_d = []
     for u in UNITS:
         s, w = unit_tiles("d", u, None)
@@ -742,15 +779,20 @@
     to_sib_d = [sdown.at[:, :, :, lanes("d", u, None, 1 - c)] for u in UNITS]
     group_r = RingSum(wires, "rd", hold, from_sib, bufs, {"r": to_sib_r, "d": to_sib_d}, spot)
     group_r.start()
+    for _ in range(START[1]):
+        next(experts, None)
     products(left_r, right_r, "r", c, hold["r"])
     for copy in own_d:
         copy.wait()
+    for _ in range(START[2]):
+        next(experts, None)
 
     def load(i):
         return pltpu.make_async_copy(w_q.at[:, pl.ds(i * 512, 512)], w_buf.at[i % 2], wsem.at[i % 2])
 
     load_gains = pltpu.make_async_copy(w_q.at[:, pl.ds(GAINS * 128, 128)], gain_tile, wsem.at[2])
-    exchange_kv = wires.describe(grad_prior, later, hn)
+    halves = [pl.ds(start, 640) for start in (0, width, 640, width + 640)]
+    exchange_kv = [wires.describe(grad_prior.at[:, cut], later.at[:, cut], hn) for cut in halves]
     to_sib_q = views("q", sent)
     group_q = RingSum(wires, "q", hold, from_sib, bufs, {"q": to_sib_q}, spot)
 
@@ -759,7 +801,7 @@
         load_gains.start()
         here = seq_rows()
         cosine, sine = cos[here, :], sin[here, :]
-        own_ok, prior_ok = allowed_keys(seg_row, seg_col)
+        own_ok, prior_ok = allowed_keys(seg_row)
         inv_root = 128.0**-0.5
 
         @pl.when(hi == 1)
@@ -782,11 +824,14 @@
             grad_own[:, behind] = grad_values[rows:]
             grad_prior[:, mine] = grad_keys[:rows].astype(BF16)
             grad_prior[:, behind] = grad_values[:rows].astype(BF16)
+            if h % 5 == 4:
+
+                @pl.when(hi == 1)
+                def _():
+                    for copy in exchange_kv[:2] if h == 4 else exchange_kv[2:]:
+                        copy.start()
+
             yield
-
-        @pl.when(hi == 1)
-        def _():
-            exchange_kv.start()
 
         right_q[0:rows, 3 * width :] = jnp.zeros((rows, Q_WIDE - 3 * width), BF16)
         right_q[rows:, :] = (iota((16, Q_WIDE), 1) == iota((16, Q_WIDE), 0) + GAINS * 128).astype(BF16)
@@ -803,9 +848,13 @@
             add_chunk(i)
             yield
 
+        for _ in range(KV_GAP):
+            yield
+
         @pl.when(hi == 0)
         def _():
-            exchange_kv.wait_recv()
+            for copy in exchange_kv:
+                copy.wait_recv()
 
         for h in range(HEADS):
             mine = slice(h * 128, (h + 1) * 128)
@@ -867,18 +916,19 @@
         for name in group:
             copies[name].wait_recv()
 
-    experts = expert_steps()
     busy = work()
-    for step in group_r.steps[:24]:
+    for n, step in enumerate(group_r.steps[:24]):
         step()
         next(busy, None)
-        next(experts, None)
+        if n in R_PIECES:
+            next(experts, None)
     for _ in busy:
-        next(experts, None)
+        pass
     rest = list(group_r.steps[24:])
-    for step in group_q.steps[:24]:
+    for n, step in enumerate(group_q.steps[:24]):
         step()
-        next(experts, None)
+        if n in Q_PIECES:
+            next(experts, None)
         if rest:
             rest.pop(0)()
     for _ in experts:
@@ -904,13 +954,14 @@
 
     @pl.when(hi == 1)
     def _():
-        exchange_kv.wait_send()
+        for copy in exchange_kv:
+            copy.wait_send()
 
     wires.finish()
 
 
 def backward(operands, parts):
-    rows, width = operands[12].shape
+    rows, width = operands[11].shape
     vmem, anywhere = pl.BlockSpec(memory_space=pltpu.VMEM), pl.BlockSpec(memory_space=pl.ANY)
     half = {name: PIECES[name][1] * 128 for name in PIECES}
     window = {"q": 48, "r": 48, "d": 32}
@@ -930,11 +981,11 @@
         pltpu.VMEM((2, width, 512), BF16),
         pltpu.VMEM((width, 128), BF16),
     ]
-    sems = 1 + 3 * (32 + 2 * 4 * 5 + 3)
+    sems = 4 + 3 * (32 + 2 * 4 * 5 + 3)
     scratch += [pltpu.SemaphoreType.DMA((n,)) for n in (sems, sems, 2, 3, 3, 3)]
     scratch += [pltpu.SemaphoreType.DMA((2, 3, 20))]
     spec = [vmem] * len(operands)
-    spec[2] = spec[15] = anywhere
+    spec[2] = spec[14] = anywhere
     return pl.pallas_call(
         backward_kernel,
         out_shape=tuple(shape(F32, *fin[name]) for name in PIECES)
@@ -1507,6 +1558,85 @@
     )(*operands, w_r, w_r, w_q)
 
 
+def finish_kernel(
+    p0, p1, p2, t0, t1, t2, fin_q, fin_r, fin_d,
+    g0, g1, g2, query, key, value, out, router, gate, up_, down, gains,
+):
+    i = pl.program_id(0)
+    hi, _y, _z, lo, c = place()
+    half = i // (pl.num_programs(0) // 2)
+    here = jnp.logical_and(c == hi, half == c)
+    for part, total, whole in ((p0, t0, g0), (p1, t1, g1), (p2, t2, g2)):
+
+        @pl.when(here)
+        def _(part=part, whole=whole):
+            whole[...] = part[...].astype(F32)
+
+        @pl.when(jnp.logical_not(here))
+        def _(total=total, whole=whole):
+            whole[...] = total[...].astype(F32)
+
+    own_rows, width = query.shape
+    tile = ROUTER * 128
+    for place_ in range(4):
+
+        @pl.when((i == 0) & (lo * 2 + c == place_))
+        def _(rows=slice(4 * place_, 4 * place_ + own_rows)):
+            query[...] = fin_q[rows, 0:width]
+            key[...] = fin_q[rows, width : 2 * width]
+            value[...] = fin_q[rows, 2 * width : 3 * width]
+            out[...] = fin_r[rows, 0:width]
+            router[...] = fin_r[rows, tile : tile + router.shape[1]]
+            wide, narrow = 1024, gate.shape[1]
+            row, col = iota((wide, narrow), 0), iota((wide, narrow), 1)
+            pick = ((col == row - 2 * (row // 16)) & (lax.rem(row, 16) < 14)).astype(BF16)
+            for dst, start in ((gate, width), (up_, width + wide)):
+                dst[...] = sum(dot(t, pick) for t in split_terms(fin_r[rows, start : start + wide]))
+            column = (iota((8, 128), 1) == iota((8, 128), 0)).astype(BF16)
+            both = sum(dot_t(column, t) for t in split_terms(fin_q[:, GAINS * 128 : (GAINS + 1) * 128]))
+            gains[...] = both[:, rows]
+
+    @pl.when(i == 0)
+    def _():
+        down[...] = fin_d[0 : down.shape[0], :]
+
+
+def finish(parts, sums, fin_q, fin_r, fin_d, own_rows, experts, inner):
+    steps = 4
+    width = fin_d.shape[1]
+    whole = lambda a: pl.BlockSpec(a.shape, lambda i: (0, 0))
+    block = lambda a: pl.BlockSpec((a.shape[0] // steps, a.shape[1]), lambda i: (i, 0))
+    first = steps // 2
+
+    def own_step(i):
+        hi, core = lax.axis_index("seq"), lax.rem(lax.axis_index("exp"), 2)
+        j = jnp.clip(i - core * first, 0, first - 1)
+        return jnp.where(hi == core, j, 0)
+
+    def total_step(i):
+        hi, core = lax.axis_index("seq"), lax.rem(lax.axis_index("exp"), 2)
+        inside = jnp.logical_and(hi == core, i // first == core)
+        return jnp.where(inside, jnp.where(core == 0, first, first - 1), i)
+
+    half_block = lambda a: pl.BlockSpec((2 * a.shape[0] // steps, a.shape[1]), lambda i: (own_step(i), 0))
+    total_block = lambda a: pl.BlockSpec((a.shape[0] // steps, a.shape[1]), lambda i: (total_step(i), 0))
+    small = (
+        [shape(F32, own_rows, width)] * 4
+        + [shape(F32, own_rows, experts)]
+        + [shape(F32, own_rows, inner)] * 2
+        + [shape(F32, inner // experts, width), shape(F32, 8, own_rows)]
+    )
+    return pl.pallas_call(
+        finish_kernel,
+        grid=(steps,),
+        out_shape=[shape(F32, *t.shape) for t in sums] + small,
+        in_specs=[half_block(p) for p in parts] + [total_block(t) for t in sums] + [whole(a) for a in (fin_q, fin_r, fin_d)],
+        out_specs=[block(t) for t in sums] + [whole(a) for a in small],
+        compiler_params=pltpu.CompilerParams(vmem_limit_bytes=60 << 20),
+        name="finish",
+    )(*parts, *sums, fin_q, fin_r, fin_d)
+
+
 def per_device(
     tokens,
     cotangent,
@@ -1530,23 +1660,14 @@
     width = tokens.shape[2]
     experts = w_router.shape[1]
     tokens, grad, routes = tokens[0], cotangent[0], routes[0]
-    seg_row = segments
-    seg_col = segments.reshape(-1, 1)
     own_experts = (expert_gate[0], expert_up[0], expert_down[0])
 
-    def spread(w):
-        w = w.reshape(w.shape[0], experts, w.shape[1] // experts)
-        return jnp.pad(w, ((0, 0), (0, 0), (0, 2))).reshape(w.shape[0], experts * 16)
-
     own_rows = w_query.shape[0]
-    zeros = lambda n: jnp.zeros((own_rows, n), BF16)
-    shard_q = jnp.concatenate(
-        [w_query, w_key, w_value, norm_gain_attn[:, None], norm_gain_ffn[:, None], zeros(254)], axis=1
-    )
-    shard_r = jnp.concatenate([w_out, spread(shared_gate), spread(shared_up), w_router, zeros(256 - experts)], axis=1)
+    shards = (w_query, w_key, w_value, w_out, shared_gate, shared_up, w_router)
+    shards += (norm_gain_attn.reshape(1, -1), norm_gain_ffn.reshape(1, -1), shared_down)
     cos, sin = rotary_tables(2 * rows)
     w_q, w_r, w_d, expert_w, act_attn, q, kv, prior, mixed = forward(
-        shard_q, shard_r, shared_down, own_experts, tokens, cos, sin, seg_row, seg_col
+        shards, own_experts, tokens, cos, sin, segments
     )
     rows_r, rows_l, hidden_one, act_ffn, gates_t, slot_t, out_s, grad_in_s, grad_gu, grad_sdown = route(
         tokens, mixed, routes, grad, w_q, w_r, w_d
@@ -1557,38 +1678,27 @@
         (back_r, back_l, slot_t, gates_t, grad, hidden_one, out_s, grad_in_s, mixed, act_ffn, grad_gu), w_r, w_q
     )
     fin_q, fin_r, fin_d, *sums, grad_tokens = backward(
-        (left_r, right_r, grad_sdown.reshape(4, 4, 64, width), act_attn, q, kv, prior, seg_row, seg_col)
+        (left_r, right_r, grad_sdown.reshape(4, 4, 64, width), act_attn, q, kv, prior, segments)
         + (grad_mixed, cos, sin, tokens, grad_hidden, gain_ffn, w_q),
         parts,
     )
-    offset = 4 * lax.rem(lax.axis_index("exp"), 4)
-    own_q = lax.dynamic_slice(fin_q, (offset, 0), (own_rows, Q_WIDE))
-    own_r = lax.dynamic_slice(fin_r, (offset, 0), (own_rows, R_WIDE))
-
-    def gathered_hidden(w):
-        return w.reshape(w.shape[0], experts, 16)[:, :, :14].reshape(w.shape[0], experts * 14)
-
-    core = lax.rem(lax.axis_index("exp"), 2)
-    kept_here = (core == lax.axis_index("seq")) & (jnp.arange(2) == core)
-    expert_grads = [
-        jnp.where(kept_here[:, None, None], own[None], total.reshape((2,) + own.shape)).astype(F32).reshape(1, *total.shape)
-        for own, total in zip(parts, sums)
-    ]
-    router = ROUTER * 128
+    *expert_grads, query, key, value, out, router, gate, up_grad, down, gains = finish(
+        parts, sums, fin_q, fin_r, fin_d, own_rows, experts, shared_gate.shape[1]
+    )
     return (
         layer_out[None],
         grad_tokens[None],
-        own_q[:, GAINS * 128],
-        own_q[:, :1280],
-        own_q[:, 1280:2560],
-        own_q[:, 2560:3840],
-        own_r[:, :1280],
-        own_q[:, GAINS * 128 + 1],
-        own_r[:, router : router + experts],
-        gathered_hidden(own_r[:, 1280:2304]),
-        gathered_hidden(own_r[:, 2304:3328]),
-        fin_d[:14],
-        *expert_grads,
+        gains[0],
+        query,
+        key,
+        value,
+        out,
+        gains[1],
+        router,
+        gate,
+        up_grad,
+        down,
+        *(g[None] for g in expert_grads),
     )
 
 

time: 446 us -> 433 us (0.971)
  local copies, waits for them, and re-layouts: 19.1 us -> 3.54 us
  Pallas kernels: 407 us -> 421 us
  other arithmetic: 11.2 us -> 0 us
    pallas_call x0 -> x1, Pallas kernels: none -> 11.6 us  [finish(): pl.pallas_call(finish_kernel, grid=(steps,), out_shape=[shape(F32, *t.sha...]
    convert_element_type x2 -> x0, other arithmetic: 11.2 us -> none  [per_device(): jnp.where(kept_here[:, None, None], own[None], total.reshape((2,) + own.s...]
    pallas_call x1, Pallas kernels: 84.4 us -> 93.7 us  [expert(): pl.pallas_call(expert_kernel, out_shape=(shape(BF16, *r), shape(F32, *las...]
    pallas_call x1, Pallas kernels: 136 us -> 128 us  [backward(): pl.pallas_call(backward_kernel, out_shape=tuple((shape(F32, *fin[name]) f...]
    reshape x9 -> x0, local copies, waits for them, and re-layouts: 7.06 us -> none  [the longest x2 2.95 us: spread(): w = w.reshape(w.shape[0], experts, w.shape[1] // experts)]
    slice x4 -> x0, local copies, waits for them, and re-layouts: 5.83 us -> none  [the longest x1 1.83 us: per_device(): own_q[:, 2560:3840]]
where the time goes in v6:
time: 433 us; the launch traced here: 426 us
  Pallas kernels  421 us (97%)
    pallas_call x1, Pallas kernels, backward(): pl.pallas_call(backward_kernel, out_shape=tuple((shape(F32, *fin[name]) f...  128 us
    pallas_call x1, Pallas kernels, expert(): pl.pallas_call(expert_kernel, out_shape=(shape(BF16, *r), shape(F32, *las...  93.7 us
    pallas_call x1, Pallas kernels, route(): pl.pallas_call(route_kernel, out_shape=(shape(BF16, *r), shape(F32, *last...  89.8 us
    pallas_call x1, Pallas kernels, forward(): pl.pallas_call(forward_kernel, out_shape=(shape(BF16, 4, 4, 80, Q_WIDE),...  86.8 us
    pallas_call x1, Pallas kernels, finish(): pl.pallas_call(finish_kernel, grid=(steps,), out_shape=[shape(F32, *t.sha...  11.6 us
    pallas_call x1, Pallas kernels, combine(): pl.pallas_call(combine_kernel, grid=(1,), out_shape=outs, in_specs=[whole...  11.2 us

profile of v6, /device:TPU:1, one launch (start us, length us, event | category | flops | bytes accessed | tf_op | source)
XLA Modules:
  0.0 425.7 jit_solution(17984703603595337131)
XLA Ops:
  0.6 1.4 copy.34
  2.1 86.8 %gather_attend.1 = (bf16[4,4,80,4096]{3,2,1,0:T(8,128)(2,1)}, bf16[4,4,80,3584]{3,2,1,0:T(8,128)(2,1)}, bf16[4,4,64,1280]{3,2,1,0:T(8,128)(2,1)}, bf16[1280,896]...) custom-call(bf16[20,1280]{1,0:T(8,128)(2,1)} %query_w.1, ...), custom_call_target="tpu_custom_call" | custom-call | tf_op jit(solution)/shard_map/gather_attend/pallas_call | solution.py:508
  88.9 89.8 %route_shared.1 = (bf16[4,4,4,16,2560]{4,3,2,1,0:T(8,128)(2,1)}, f32[4,4,4,1,2688]{4,3,2,1,0:T(1,128)}, f32[128,1280]{1,0:T(8,128)}, bf16[128,1280]{1,0:T(8,128)...) custom-call(bf16[128,1280]{1,0:T(8,128)(2,1)} %bitcast.37, ...), custom_call_target="tpu_custom_call" | custom-call | tf_op jit(solution)/shard_map/route_shared/pallas_call | solution.py:1291
  178.7 93.7 %expert_back.1 = (bf16[4,4,4,16,2560]{4,3,2,1,0:T(8,128)(2,1)}, f32[4,4,4,1,2560]{4,3,2,1,0:T(1,128)}, bf16[640,896]{1,0:T(8,128)(2,1)}, bf16[640,896]{1,0:T(8,128)(2,1)}, bf16[448,1280]{1,0:T(8,128)(2,1)}) custom-call(bf16[4,4,4,16,2560]{4,3,2,1,0:T(8,128)(2,1)} %get-tuple-element.70.rows_r, f32[4,4,4,1,2688]{4,3,2,1,0:T(1,128)} %get-tuple-element.71.rows_l, ...), custom_call_target="tpu_custom_call" | custom-call | tf_op jit(solution)/shard_map/expert_back/pallas_call | solution.py:1462
  272.4 11.2 %combine.1 = (bf16[128,1280]{1,0:T(8,128)(2,1)}, f32[128,1280]{1,0:T(8,128)}, bf16[128,1280]{1,0:T(8,128)(2,1)}, bf16[256,1280]{1,0:T(8,128)(2,1)}, bf16[256,3584]{1,0:T(8,128)(2,1)}, /*index=5*/f32[1,1280]{1,0:T(1,128)}) custom-call(bf16[64,16,2560]{2,1,0:T(8,128)(2,1)} %bitcast.35, f32[64,1,2560]{2,1,0:T(1,128)} %bitcast.44, ...), custom_call_target="tpu_custom_call" | custom-call | tf_op jit(solution)/shard_map/combine/pallas_call | solution.py:1545
  283.6 128.2 %attend_back_sums.1 = (f32[32,4096]{1,0:T(8,128)}, f32[32,3584]{1,0:T(8,128)}, f32[16,1280]{1,0:T(8,128)}, bf16[1280,896]{1,0:T(8,128)(2,1)}, bf16[1280,896]{1,0...) custom-call(bf16[256,1280]{1,0:T(8,128)(2,1)} %get-tuple-element.85.left_r, ...), custom_call_target="tpu_custom_call" | custom-call | tf_op jit(solution)/shard_map/attend_back_sums/pallas_call | solution.py:989
  411.8 0.0 copy-start
  411.8 11.6 %finish.1 = (f32[1280,896]{1,0:T(8,128)}, f32[1280,896]{1,0:T(8,128)}, f32[896,1280]{1,0:T(8,128)}, f32[20,1280]{1,0:T(8,128)}, f32[20,1280]{1,0:T(8,128)}, /*in...) custom-call(bf16[640,896]{1,0:T(8,128)(2,1)} %get-tuple-element.95.p, ...), custom_call_target="tpu_custom_call" | custom-call | tf_op jit(solution)/shard_map/finish/pallas_call | solution.py:1629
  423.4 1.3 slice_bitcast_fusion
  424.7 0.0 copy-done
  424.7 0.8 copy.36
Async XLA Ops:
  411.8 12.9 %copy-start = (f32[128,1280]{1,0:T(8,128)S(1)}, f32[128,1280]{1,0:T(8,128)}, u32[]{:S(2)}) copy-start(f32[128,1280]{1,0:T(8,128)} %get-tuple-element.98) | copy-start | bytes 1966084

commit v7 on v6

--- a/solution.py
+++ b/solution.py
@@ -933,8 +933,14 @@
             rest.pop(0)()
     for _ in experts:
         pass
-    interleave(group_q.steps[24:], window_sums("rd"))
-    for _ in window_sums("q"):
+    first, second = window_sums("rd"), window_sums("q")
+    next(first)
+    for step in group_q.steps[24:]:
+        step()
+    next(second)
+    for _ in first:
+        next(second, None)
+    for _ in second:
         pass
     for k, i in pieces:
         across_piece(k, i).wait_send()
@@ -1020,7 +1026,7 @@
         hi, y, z, lo, c = spot
         self.stays = c == hi
         self.moves = jnp.logical_not(self.stays)
-        self.pending, self.sent, self.used = {}, [], [0, 0]
+        self.pending, self.sent, self.used, self.made = {}, [], [0, 0], []
 
     def along(self, axis, k):
         hi, y, z, lo, c = self.spot
@@ -1157,8 +1163,14 @@
         self.sent.append(wait_sent)
 
     def first(self, turn, at):
-        for part in range(PARTS):
+        now = PARTS // 2 if self.outward else PARTS
+        for part in range(now):
             self.go(part, 0, turn, at)
+        self.made.append((turn, at))
+        if len(self.made) == 4:
+            for part in range(now, PARTS):
+                for turn, at in self.made:
+                    self.go(part, 0, turn, at)
 
     def next(self, phase):
         for part in range(PARTS):

time: 433 us -> 423 us (0.977)
  Pallas kernels: 421 us -> 414 us
    pallas_call x1, Pallas kernels: 128 us -> 122 us  [backward(): pl.pallas_call(backward_kernel, out_shape=tuple((shape(F32, *fin[name]) f...]
where the time goes in v7:
time: 423 us; the launch traced here: 418 us
  Pallas kernels  414 us (98%)
    pallas_call x1, Pallas kernels, backward(): pl.pallas_call(backward_kernel, out_shape=tuple((shape(F32, *fin[name]) f...  122 us
    pallas_call x1, Pallas kernels, expert(): pl.pallas_call(expert_kernel, out_shape=(shape(BF16, *r), shape(F32, *las...  95.3 us
    pallas_call x1, Pallas kernels, route(): pl.pallas_call(route_kernel, out_shape=(shape(BF16, *r), shape(F32, *last...  87.2 us
    pallas_call x1, Pallas kernels, forward(): pl.pallas_call(forward_kernel, out_shape=(shape(BF16, 4, 4, 80, Q_WIDE),...  86.8 us
    pallas_call x1, Pallas kernels, finish(): pl.pallas_call(finish_kernel, grid=(steps,), out_shape=[shape(F32, *t.sha...  11.6 us
    pallas_call x1, Pallas kernels, combine(): pl.pallas_call(combine_kernel, grid=(1,), out_shape=outs, in_specs=[whole...  11.2 us

profile of v7, /device:TPU:1, one launch (start us, length us, event | category | flops | bytes accessed | tf_op | source)
XLA Modules:
  0.0 418.3 jit_solution(5071291220980568083)
XLA Ops:
  0.6 1.4 copy.34
  2.1 86.8 %gather_attend.1 = (bf16[4,4,80,4096]{3,2,1,0:T(8,128)(2,1)}, bf16[4,4,80,3584]{3,2,1,0:T(8,128)(2,1)}, bf16[4,4,64,1280]{3,2,1,0:T(8,128)(2,1)}, bf16[1280,896]...) custom-call(bf16[20,1280]{1,0:T(8,128)(2,1)} %query_w.1, ...), custom_call_target="tpu_custom_call" | custom-call | tf_op jit(solution)/shard_map/gather_attend/pallas_call | solution.py:508
  88.9 87.2 %route_shared.1 = (bf16[4,4,4,16,2560]{4,3,2,1,0:T(8,128)(2,1)}, f32[4,4,4,1,2688]{4,3,2,1,0:T(1,128)}, f32[128,1280]{1,0:T(8,128)}, bf16[128,1280]{1,0:T(8,128)...) custom-call(bf16[128,1280]{1,0:T(8,128)(2,1)} %bitcast.37, ...), custom_call_target="tpu_custom_call" | custom-call | tf_op jit(solution)/shard_map/route_shared/pallas_call | solution.py:1303
  176.0 95.3 %expert_back.1 = (bf16[4,4,4,16,2560]{4,3,2,1,0:T(8,128)(2,1)}, f32[4,4,4,1,2560]{4,3,2,1,0:T(1,128)}, bf16[640,896]{1,0:T(8,128)(2,1)}, bf16[640,896]{1,0:T(8,128)(2,1)}, bf16[448,1280]{1,0:T(8,128)(2,1)}) custom-call(bf16[4,4,4,16,2560]{4,3,2,1,0:T(8,128)(2,1)} %get-tuple-element.70.rows_r, f32[4,4,4,1,2688]{4,3,2,1,0:T(1,128)} %get-tuple-element.71.rows_l, ...), custom_call_target="tpu_custom_call" | custom-call | tf_op jit(solution)/shard_map/expert_back/pallas_call | solution.py:1474
  271.4 11.2 %combine.1 = (bf16[128,1280]{1,0:T(8,128)(2,1)}, f32[128,1280]{1,0:T(8,128)}, bf16[128,1280]{1,0:T(8,128)(2,1)}, bf16[256,1280]{1,0:T(8,128)(2,1)}, bf16[256,3584]{1,0:T(8,128)(2,1)}, /*index=5*/f32[1,1280]{1,0:T(1,128)}) custom-call(bf16[64,16,2560]{2,1,0:T(8,128)(2,1)} %bitcast.35, f32[64,1,2560]{2,1,0:T(1,128)} %bitcast.44, ...), custom_call_target="tpu_custom_call" | custom-call | tf_op jit(solution)/shard_map/combine/pallas_call | solution.py:1557
  282.6 121.7 %attend_back_sums.1 = (f32[32,4096]{1,0:T(8,128)}, f32[32,3584]{1,0:T(8,128)}, f32[16,1280]{1,0:T(8,128)}, bf16[1280,896]{1,0:T(8,128)(2,1)}, bf16[1280,896]{1,0...) custom-call(bf16[256,1280]{1,0:T(8,128)(2,1)} %get-tuple-element.85.left_r, ...), custom_call_target="tpu_custom_call" | custom-call | tf_op jit(solution)/shard_map/attend_back_sums/pallas_call | solution.py:995
  404.3 0.0 copy-start
  404.3 11.6 %finish.1 = (f32[1280,896]{1,0:T(8,128)}, f32[1280,896]{1,0:T(8,128)}, f32[896,1280]{1,0:T(8,128)}, f32[20,1280]{1,0:T(8,128)}, f32[20,1280]{1,0:T(8,128)}, /*in...) custom-call(bf16[640,896]{1,0:T(8,128)(2,1)} %get-tuple-element.95.p, ...), custom_call_target="tpu_custom_call" | custom-call | tf_op jit(solution)/shard_map/finish/pallas_call | solution.py:1641
  415.9 1.3 slice_bitcast_fusion
  417.2 0.0 copy-done
  417.2 0.8 copy.36
Async XLA Ops:
  404.3 12.9 %copy-start = (f32[128,1280]{1,0:T(8,128)S(1)}, f32[128,1280]{1,0:T(8,128)}, u32[]{:S(2)}) copy-start(f32[128,1280]{1,0:T(8,128)} %get-tuple-element.98) | copy-start | bytes 1966084
